TPU v7x, 256 devices: a whole 4x4x8 slice. The times are simulated.
256 devices in a mesh: member: 8 (over y, z_hi), space: 32 (over x, z_lo, core).
Axes of the slice: x: 4, y: 4, z: 8 (z_hi: 2, z_lo: 4; z = z_hi * 4 + z_lo), core: 2. Of those that a mesh axis runs over, the one named last changes fastest.
Arguments:
- latent: bfloat16 [8, 32768, 1024], P('member', 'space'), may hold values from -6 to 6
- neighbours: int32 [4, 32768], P(None, 'space'), may hold values from 0 to 32767, as said below
- norm_gain: float32 [1024], replicated, may hold values from 0.1 to 1.9
- w_mix: bfloat16 [1024, 1024], replicated, may hold values from -0.1875 to 0.1875
- w_out: bfloat16 [1024, 100], replicated, may hold values from -0.1875 to 0.1875
- observed: float32 [100, 32768], P(None, 'space'), may hold values from -6 to 6
- cell_area: float32 [32768], P('space'), may hold values from 0.3 to 3
- var_weight: float32 [100], replicated, may hold values from 1 to 16
Outputs:
- crps_field: float32 [32768], P('space')
- grad_latent: bfloat16 [8, 32768, 1024], P('member', 'space')
- grad_mix: float32 [1024, 1024], P('space')
- grad_out: float32 [1024, 100], P('space')
Inputs may be any that keep to these rules, and one draw needn't show every extreme that they name: neighbours[k, c] lies within 128 cells of c; neighbours[0, c] lies exactly 128 cells from c.
All inputs are finite; a program needn't handle non-finite values.
Results may differ from a plain program's by a relative error of at most 0.02.
Values may be sent and summed in bfloat16 or wider, within the bound.
No kernel may reach another device: no remote copies, remote signals or barrier semaphores. Data moves between devices by JAX's collectives and lax.ppermute only.
A program may use at most 128 MiB of HBM per device.

v0:
```python
import math

import jax
import jax.numpy as jnp
from jax import lax
from jax.sharding import PartitionSpec as P

D = 1024
NBRS = 4
HALO = 128


smoothing = 0.1
root_two_pi = math.sqrt(2.0 / math.pi)
cubic = 0.044715
epsilon = 1e-06
fair_shift = 0.05


def extended_2(cells, sides, width):
    for axis, dim in sides:
        count = lax.axis_size(axis)
        ends = count - 1
        head = lax.slice_in_dim(cells, 0, width, axis=dim)
        tail = lax.slice_in_dim(cells, cells.shape[dim] - width, cells.shape[dim], axis=dim)
        cells = jnp.concatenate(
            [
                lax.ppermute(tail, axis, [(i, (i + 1) % count) for i in range(ends)]),
                cells,
                lax.ppermute(head, axis, [((i + 1) % count, i) for i in range(ends)]),
            ],
            axis=dim,
        )
    return cells


def passed_along(value, axis, steps):
    count = lax.axis_size(axis)
    initial, last = (max(0, -steps), min(count, count - steps))
    return lax.ppermute(value, axis, [(source, source + steps) for source in range(initial, last)])


def gelu_parts(preact):
    tanh_input = root_two_pi * (preact + cubic * preact * preact * preact)
    tanh_value = jnp.tanh(tanh_input)
    activation = 0.5 * preact * (1.0 + tanh_value)
    derivative = 0.5 * (1.0 + tanh_value) + 0.5 * preact * (
        1.0 - tanh_value * tanh_value
    ) * root_two_pi * (1.0 + 3.0 * cubic * preact * preact)
    return (activation, derivative)


def decoder_forward(center, aggregate, norm_gain, w_mix):
    combined = center.astype(jnp.float32) + aggregate
    inverse = lax.rsqrt(jnp.mean(combined * combined, axis=1, keepdims=True) + epsilon)
    normed = (combined * inverse * norm_gain).astype(jnp.bfloat16)
    preact = jnp.dot(normed, w_mix, preferred_element_type=jnp.float32)
    activation, derivative = gelu_parts(preact)
    hidden = (combined + activation).astype(jnp.bfloat16)
    return (combined, inverse, normed, derivative, hidden)


def decoder_backward(g_member, combined, inverse, derivative, norm_gain, w_mix, w_out):
    d_hidden = lax.dot_general(
        g_member, w_out, (((0,), (1,)), ((), ())), preferred_element_type=jnp.float32
    )
    d_pre = (d_hidden * derivative).astype(jnp.bfloat16)
    d_normed = lax.dot_general(
        d_pre, w_mix, (((1,), (1,)), ((), ())), preferred_element_type=jnp.float32
    )
    scaled = d_normed * norm_gain
    d_combined = (
        d_hidden
        + inverse * scaled
        - combined
        * (inverse * inverse * inverse)
        * jnp.mean(combined * scaled, axis=1, keepdims=True)
    )
    return (d_pre, d_combined)


def shards(latent, neighbours, norm_gain, w_mix, w_out, observed, cell_area, var_weight):
    member_count = lax.axis_size("member")
    space_count = lax.axis_size("space")
    member_pos = lax.axis_index("member")
    space_pos = lax.axis_index("space")
    cell_count = latent.shape[1]
    center = latent[0]
    extended = extended_2(center, (("space", 0),), HALO)
    local_edges = (neighbours - (space_pos * cell_count - HALO)).reshape(-1)
    gathered = jnp.take(extended, local_edges, axis=0).astype(jnp.float32)
    aggregate = jnp.sum(gathered.reshape(NBRS, cell_count, D), axis=0) / NBRS
    combined, inverse, normed, derivative, hidden = decoder_forward(
        center, aggregate, norm_gain, w_mix
    )
    prediction = lax.dot_general(
        w_out, hidden, (((0,), (1,)), ((), ())), preferred_element_type=jnp.float32
    )
    fair_weight = 1.0 - fair_shift / member_count
    pair_coef = fair_weight / (2.0 * member_count * (member_count - 1))
    own_field = prediction[None]
    shard_piece = lax.all_gather(own_field, "member", axis=0, tiled=True)
    piece_ids = jnp.arange(shard_piece.shape[0], dtype=jnp.int32)
    distinct = (piece_ids != member_pos)[:, None, None]
    pair_gap = own_field - shard_piece
    smooth = jnp.sqrt(pair_gap * pair_gap + smoothing * smoothing)
    pair_s = jnp.sum(jnp.where(distinct, smooth, 0.0), axis=0)
    pair_ds = jnp.sum(jnp.where(distinct, pair_gap / smooth, 0.0), axis=0)
    cell_weight = var_weight[:, None] * cell_area[None, :]
    obs_gap = prediction - observed
    smooth_obs = jnp.sqrt(obs_gap * obs_gap + smoothing * smoothing)
    member_term = smooth_obs / member_count - pair_coef * pair_s
    local_losses = jnp.sum(cell_weight * member_term, axis=0)
    crps_field = lax.psum(local_losses, "member")
    g_pred = (
        cell_weight * (obs_gap / smooth_obs / member_count - 2.0 * pair_coef * pair_ds)
    ).astype(jnp.bfloat16)
    d_pre, d_combined = decoder_backward(
        g_pred, combined, inverse, derivative, norm_gain, w_mix, w_out
    )
    spread = (
        jnp.zeros(extended.shape, jnp.float32)
        .at[local_edges]
        .add(jnp.tile(d_combined / NBRS, (NBRS, 1)))
    )
    upper_rim = spread[HALO + cell_count :]
    lower_rim = spread[:HALO]
    from_below = passed_along(upper_rim.astype(jnp.bfloat16), "space", 1).astype(upper_rim.dtype)
    from_above = passed_along(lower_rim.astype(jnp.bfloat16), "space", -1).astype(lower_rim.dtype)
    grad_rows = d_combined + spread[HALO : HALO + cell_count]
    grad_rows = grad_rows.at[:HALO].add(from_below)
    grad_rows = grad_rows.at[cell_count - HALO :].add(from_above)
    part_mix = lax.dot_general(
        normed, d_pre, (((0,), (0,)), ((), ())), preferred_element_type=jnp.float32
    )
    part_out = lax.dot_general(
        hidden, g_pred, (((0,), (1,)), ((), ())), preferred_element_type=jnp.float32
    )
    shares = lax.psum_scatter(
        jnp.concatenate([part_mix, part_out], axis=1).astype(jnp.bfloat16),
        "space",
        scatter_dimension=0,
        tiled=True,
    )
    totals = lax.psum(shares, "member").astype(jnp.float32)
    grad_scale = 1.0 / math.sqrt(member_count * cell_count * space_count)
    return (
        crps_field,
        grad_rows.astype(jnp.bfloat16)[None],
        totals[:, :D] * grad_scale,
        totals[:, D:] * grad_scale,
    )


def solution(mesh):
    return jax.shard_map(
        shards,
        mesh=mesh,
        in_specs=(
            P("member", "space", None),
            P(None, "space"),
            P(),
            P(),
            P(),
            P(None, "space"),
            P("space"),
            P(),
        ),
        out_specs=(P("space"), P("member", "space", None), P("space", None), P("space", None)),
        check_vma=False,
    )
```

profile of v0, /device:TPU:2, one launch (start us, length us, event | category | flops | bytes accessed | tf_op | source)
XLA Modules:
  0.0 440.0 jit_solution(13847396152284449713)
XLA Ops:
  8.4 1.9 collective-permute-start
  10.4 6.3 %collective-permute-start.1 = (bf16[128,1024]{1,0:T(8,128)(2,1)S(1)}, bf16[128,1024]{1,0:T(8,128)(2,1)S(1)}, u32[]{:S(2)}, u32[]{:S(2)}) collective-permute-start(bf16[128,1024]{1,0:T(8,128)(2,1)S(1)} %get-tuple-element.45), channel_id=1, source_target_pairs={{1,0},{2,1},{3,2},{4,3},{5,4},{6,5},{7,6},{8,7},{9,8},{10,9},{11,1... | collective-permute-start | bytes 786440 | tf_op jit(solution)/shard_map/ppermute | solution.py:30
  20.6 3.4 pad_maximum_fusion
  24.0 23.0 %gather_fusion = bf16[4096,1024]{1,0:T(8,128)(2,1)} fusion(bf16[1280,1024]{1,0:T(8,128)(2,1)} %pad_maximum_fusion, s32[4096]{0:T(1024)S(1)} %broadcast_clamp_fusion), kind=kCustom, calls=%fused_computation | custom fusion | bytes 16793600 | tf_op jit(solution)/shard_map/jit(_take)/gather | solution.py:91
  46.9 5.4 %convert_reduce_fusion = f32[1024,1024]{1,0:T(8,128)S(1)} fusion(bf16[4,1024,1024]{2,1,0:T(8,128)(2,1)} %bitcast.33, pred[4,1024]{1,0:T(4,128)(4,1)S(1)} %compare_and_fusion), kind=kLoop, calls=%fused_computation.2 | loop fusion | flops 11534336 | bytes 12587008 | tf_op jit(solution)/shard_map/reduce_sum | solution.py:92
  53.2 5.1 %add_convert_fusion = (bf16[1024,1024]{1,0:T(8,128)(2,1)S(1)}, f32[1024,1024]{1,0:T(8,128)}) fusion(f32[1024,1024]{1,0:T(8,128)S(1)} %get-tuple-element.41, bf16[1024,1024]{1,0:T(8,128)(2,1)S(1)} %copy-done, f32[1024]{0:T(1024)S(1)} %copy-done.13, f32[1024]{0:T(1024)S(1)} %get-tuple-element.49), kind=kOutput, calls=%fused_computation.15 | convolution fusion | flops 2161115136 | bytes 12591104 | tf_op jit(solution)/shard_map/dot_general | solution.py:57
  61.4 98.6 %all-gather.4.cloned.1.call-done = f32[8,100,1024]{2,1,0:T(8,128)} async-done(((f32[1,100,1024]{2,1,0:T(8,128)}), f32[8,100,1024]{2,1,0:T(8,128)}) %all-gather.4.cloned.1.call-update) | async-done | bytes 3276816 | tf_op jit(solution)/shard_map/all_gather | solution.py:102
  160.0 4.4 select_reduce_fusion
  166.6 4.2 fusion.6
  170.8 2.7 convolution_convert_fusion
  175.1 4.3 copy.19
  179.8 5.4 %multiply_reduce_fusion = (f32[1024]{0:T(1024)S(1)}, f32[1024,1024]{1,0:T(8,128)S(1)}) fusion(f32[1024,1024]{1,0:T(8,128)} %copy-done.2, f32[1024]{0:T(1024)S(1)} %copy-done.13, bf16[1024,1024]{1,0:T(8,128)(2,1)} %copy-done.15, bf16[1024,1024]{1,0:T(8,128)(2,1)S(1)} %copy-done), kind=kOutput, calls=%fused_computation.14 | convolution fusion | flops 2150628352 | bytes 12591104 | tf_op jit(solution)/shard_map/dot_general | solution.py:68
  185.2 2.8 broadcast_multiply_fusion
  188.0 8.1 %tile.4 = f32[4,1024,1024]{2,1,0:T(8,128)} broadcast(f32[1024,1024]{1,0:T(8,128)S(1)} %get-tuple-element.38), dimensions={1,2} | broadcast | bytes 20971520 | tf_op jit(solution)/shard_map/tile | solution.py:124
  196.1 38.9 %scatter_custom_fusion = f32[1280,1024]{1,0:T(8,128)} fusion(s32[4096]{0:T(1024)S(1)} %bitcast.39, f32[4096,1024]{1,0:T(8,128)} %bitcast.34, f32[]{:T(128)} %constant.107.clone.1), kind=kCustom, calls=%fused_computation.23 | custom fusion | flops 4194304 | bytes 5243392 | tf_op jit(solution)/shard_map/scatter-add | solution.py:124
  235.0 3.1 convert.10
  238.1 2.1 collective-permute-start.3
  240.2 2.4 collective-permute-start.2
  242.6 5.1 %slice_add_fusion = f32[1024,1024]{1,0:T(8,128)} fusion(f32[1024,1024]{1,0:T(8,128)} %get-tuple-element.39, f32[1280,1024]{1,0:T(8,128)S(1)} %copy-done.1), kind=kLoop, calls=%fused_computation.12 | loop fusion | flops 1048576 | bytes 12582912 | tf_op jit(solution)/shard_map/add | solution.py:130
  247.7 24.5 %psum.14 = f32[1024]{0:T(1024)} all-reduce(f32[1024]{0:T(1024)S(1)} %get-tuple-element.47), channel_id=1, replica_groups=mesh['member'=8,'space'=32] {'member'}, use_global_device_ids=true, to_apply=%region_4.5 | all-reduce | flops 1024 | bytes 8192 | tf_op jit(solution)/shard_map/psum | solution.py:114
  272.2 1.9 fusion.10
  276.0 28.4 %reduce-scatter.4.cloned.1.call-done = bf16[32,1124]{1,0:T(8,128)(2,1)} async-done(((bf16[1024,1124]{1,0:T(8,128)(2,1)}), bf16[32,1124]{1,0:T(8,128)(2,1)}) %reduce-scatter.4.cloned.1.call-update) | async-done | bytes 71952
  306.2 3.8 convert_bitcast_fusion
  310.0 120.9 %all-reduce.2.cloned.1.call-done = bf16[32,1124]{0,1:T(8,128)(2,1)} async-done(((bf16[32,1124]{0,1:T(8,128)(2,1)}), bf16[32,1124]{0,1:T(8,128)(2,1)}) %all-reduce.2.cloned.1.call-update) | async-done | bytes 71952 | tf_op jit(solution)/shard_map/psum | solution.py:145
  (66 shorter events, 19.3 us)
Async XLA Ops:
  7.2 46.0 %copy-start = (bf16[1024,1024]{1,0:T(8,128)(2,1)S(1)}, bf16[1024,1024]{1,0:T(8,128)(2,1)}, u32[]{:S(2)}) copy-start(bf16[1024,1024]{1,0:T(8,128)(2,1)} %param.15) | copy-start | bytes 6291460
  7.2 152.8 %all-gather.4.cloned.1.call-start = ((), (), s32[]{:S(2)}) async-start(), calls=%async_computation.2 | async-start | bytes 3833856 | tf_op jit(solution)/shard_map/all_gather | solution.py:102
  8.4 10.5 %collective-permute-start = (bf16[128,1024]{1,0:T(8,128)(2,1)S(1)}, bf16[128,1024]{1,0:T(8,128)(2,1)S(1)}, u32[]{:S(2)}, u32[]{:S(2)}) collective-permute-start(bf16[128,1024]{1,0:T(8,128)(2,1)S(1)} %get-tuple-element.44), channel_id=1, source_target_pairs={{0,1},{1,2},{2,3},{3,4},{4,5},{5,6},{6,7},{7,8},{8,9},{9,10},{10,1... | collective-permute-start | bytes 786440 | tf_op jit(solution)/shard_map/ppermute | solution.py:28
  10.4 10.2 %collective-permute-start.1 = (bf16[128,1024]{1,0:T(8,128)(2,1)S(1)}, bf16[128,1024]{1,0:T(8,128)(2,1)S(1)}, u32[]{:S(2)}, u32[]{:S(2)}) collective-permute-start(bf16[128,1024]{1,0:T(8,128)(2,1)S(1)} %get-tuple-element.45), channel_id=1, source_target_pairs={{1,0},{2,1},{3,2},{4,3},{5,4},{6,5},{7,6},{8,7},{9,8},{10,9},{11,1... | collective-permute-start | bytes 786440 | tf_op jit(solution)/shard_map/ppermute | solution.py:30
  46.9 5.4 %copy-start.7 = (bf16[1,1024,1024]{2,1,0:T(8,128)(2,1)S(1)}, bf16[1,1024,1024]{2,1,0:T(8,128)(2,1)}, u32[]{:S(2)}) copy-start(bf16[1,1024,1024]{2,1,0:T(8,128)(2,1)} %param.12) | copy-start | bytes 6291460
  52.4 0.8 copy-start.13
  53.1 5.1 %copy-start.2 = (f32[1024,1024]{1,0:T(8,128)}, f32[1024,1024]{1,0:T(8,128)S(1)}, u32[]{:S(2)}) copy-start(f32[1024,1024]{1,0:T(8,128)S(1)} %get-tuple-element.41) | copy-start | bytes 12582916
  53.2 6.4 %copy-start.11 = (bf16[1024,100]{0,1:T(8,128)(2,1)S(1)}, bf16[1024,100]{0,1:T(8,128)(2,1)}, u32[]{:S(2)}) copy-start(bf16[1024,100]{0,1:T(8,128)(2,1)} %param.16) | copy-start | bytes 614404
  58.3 1.3 copy-start.5
  58.3 106.1 %copy-start.10 = (f32[100,1024]{1,0:T(8,128)S(1)}, f32[100,1024]{1,0:T(8,128)}, u32[]{:S(2)}) copy-start(f32[100,1024]{1,0:T(8,128)} %param.17) | copy-start | bytes 1228804
  58.3 106.1 %copy-start.12 = (f32[1024]{0:T(1024)S(1)}, f32[1024]{0:T(1024)}, u32[]{:S(2)}) copy-start(f32[1024]{0:T(1024)} %param.18) | copy-start | bytes 12292
  58.3 106.1 %copy-start.14 = (f32[100]{0:T(128)S(1)}, f32[100]{0:T(128)}, u32[]{:S(2)}) copy-start(f32[100]{0:T(128)} %param.19) | copy-start | bytes 1204
  61.1 103.3 %copy-start.8 = (f32[1024,100]{0,1:T(8,128)S(1)}, f32[1024,100]{0,1:T(8,128)}, u32[]{:S(2)}) copy-start(f32[1024,100]{0,1:T(8,128)} %fusion.15) | copy-start | bytes 1228804
  61.1 243.2 %reduce-scatter.4.cloned.1.call-start = ((), (), s32[]{:S(2)}) async-start(), calls=%async_computation.3 | async-start | bytes 2433024
  160.0 4.8 %copy-start.6 = (bf16[1024,1024]{1,0:T(8,128)(2,1)S(1)}, bf16[1024,1024]{1,0:T(8,128)(2,1)}, u32[]{:S(2)}) copy-start(bf16[1024,1024]{1,0:T(8,128)(2,1)} %copy-done.5) | copy-start | bytes 6291460
  164.4 2.2 copy-start.16
  166.6 4.2 copy-start.3
  170.8 2.7 copy-start.15
  179.5 251.4 %all-reduce.2.cloned.1.call-start = ((), (), s32[]{:S(2)}) async-start(), calls=%async_computation.1 | async-start | bytes 577536 | tf_op jit(solution)/shard_map/psum | solution.py:145
  179.7 5.5 %copy-start.4 = (f32[1024,1024]{1,0:T(8,128)S(1)}, f32[1024,1024]{1,0:T(8,128)}, u32[]{:S(2)}) copy-start(f32[1024,1024]{1,0:T(8,128)} %copy-done.2) | copy-start | bytes 12582916
  179.8 5.5 %copy-start.9 = (f32[1024,1024]{1,0:T(8,128)S(1)}, f32[1024,1024]{1,0:T(8,128)}, u32[]{:S(2)}) copy-start(f32[1024,1024]{1,0:T(8,128)} %get-tuple-element.53) | copy-start | bytes 12582916
  235.0 7.6 %copy-start.1 = (f32[1280,1024]{1,0:T(8,128)S(1)}, f32[1280,1024]{1,0:T(8,128)}, u32[]{:S(2)}) copy-start(f32[1280,1024]{1,0:T(8,128)} %scatter_custom_fusion) | copy-start | bytes 15728644
  238.1 36.0 %collective-permute-start.3 = (bf16[128,1024]{1,0:T(8,128)(2,1)S(1)}, bf16[128,1024]{1,0:T(8,128)(2,1)S(1)}, u32[]{:S(2)}, u32[]{:S(2)}) collective-permute-start(bf16[128,1024]{1,0:T(8,128)(2,1)S(1)} %get-tuple-element.42), channel_id=1, source_target_pairs={{1,0},{2,1},{3,2},{4,3},{5,4},{6,5},{7,6},{8,7},{9,8},{10,9},{11,1... | collective-permute-start | bytes 786440 | tf_op jit(solution)/shard_map/ppermute | solution.py:40
  240.2 32.0 %collective-permute-start.2 = (bf16[128,1024]{1,0:T(8,128)(2,1)S(1)}, bf16[128,1024]{1,0:T(8,128)(2,1)S(1)}, u32[]{:S(2)}, u32[]{:S(2)}) collective-permute-start(bf16[128,1024]{1,0:T(8,128)(2,1)S(1)} %get-tuple-element.43), channel_id=1, source_target_pairs={{0,1},{1,2},{2,3},{3,4},{4,5},{5,6},{6,7},{7,8},{8,9},{9,10},{10,1... | collective-permute-start | bytes 786440 | tf_op jit(solution)/shard_map/ppermute | solution.py:40
Sparse Core Ops, SparseCore 0:
  61.3 98.6 all-gather.3
  179.6 124.7 reduce-scatter.3
  307.0 123.7 all-reduce.1
where the time goes:
time: 441 us; the launch traced here: 440 us
  waiting for transfers between devices  250 us (57%)
  other arithmetic  76 us (17%)
  local copies, waits for them, and re-layouts  42.6 us (10%)
  blocking collectives  24.5 us (6%)
  matrix products  19.4 us (4%)
  between operations  14.1 us (3%)
  starting transfers between devices  13.2 us (3%)
    psum x1, waiting for transfers between devices, shards(): totals = lax.psum(shares, 'member').astype(jnp.float32)  121 us
    all_gather x1, waiting for transfers between devices, shards(): shard_piece = lax.all_gather(own_field, 'member', axis=0, tiled=True)  98.6 us
    scatter-add x1, other arithmetic, shards(): spread = jnp.zeros(extended.shape, jnp.float32).at[local_edges].add(jnp.t...  38.9 us
    unnamed x4, waiting for transfers between devices  28.5 us
    psum x1, blocking collectives, shards(): crps_field = lax.psum(local_losses, 'member')  24.5 us
    gather x1, local copies, waits for them, and re-layouts, shards(): gathered = jnp.take(extended, local_edges, axis=0).astype(jnp.float32)  23 us
    unnamed x39, local copies, waits for them, and re-layouts  10.3 us
  transfers between devices with their start and end apart: 7, of which 5 were waited for; matrix products, arithmetic and copies ran while one was open for 16% of the time, Pallas kernels for 0%

commit v1 on v0

v1 whole, which is shorter than its diff:
```python
import math

import jax
import jax.numpy as jnp
from jax import lax
from jax.experimental import pallas as pl
from jax.experimental.pallas import tpu as pltpu
from jax.sharding import PartitionSpec as P

D = 1024
VARS = 100
NBRS = 4
HALO = 128
ROWS = 112
MEMBERS = 8
CELLS = 1024
BLK = 256
STEPS = CELLS // BLK
PIECE = CELLS // MEMBERS
WIDE = D + 128

smoothing = 0.1
root_two_pi = math.sqrt(2.0 / math.pi)
cubic = 0.044715
epsilon = 1e-06
fair_shift = 0.05
fair_weight = 1.0 - fair_shift / MEMBERS
pair_coef = fair_weight / (2.0 * MEMBERS * (MEMBERS - 1))

bf16 = jnp.bfloat16
f32 = jnp.float32
VMEM_LIMIT = 56 * 1024 * 1024


def whole(shape):
    return pl.BlockSpec(shape, lambda *_: (0,) * len(shape), pipeline_mode=pl.Buffered(1))


def edge_matrix(nb_ref, base, scale):
    local = (nb_ref[...] - base).T
    column = lax.broadcasted_iota(jnp.int32, (BLK, BLK + 2 * HALO), 1)
    count = jnp.zeros((BLK, BLK + 2 * HALO), f32)
    for k in range(NBRS):
        count = count + jnp.where(column == local[:, k : k + 1], scale, 0.0)
    return count


def forward_kernel(
    nb_ref, lat_ref, low_ref, high_ref, gain_ref, mix_ref, out_ref,
    normed_ref, hidden_ref, deriv_ref, inv_ref, pred_ref, send_ref, ext,
):
    step = pl.program_id(0)

    @pl.when(step == 0)
    def _():
        ext[0:HALO] = low_ref[...]
        ext[HALO : HALO + CELLS] = lat_ref[...]
        ext[HALO + CELLS :] = high_ref[...]

    first = pl.multiple_of(step * BLK, BLK)
    base = lax.axis_index("space") * CELLS - HALO + first
    edges = edge_matrix(nb_ref, base, 1.0).astype(bf16)
    window = ext[pl.ds(first, BLK + 2 * HALO)]
    total = jnp.dot(edges, window, preferred_element_type=f32)
    combined = window[HALO : HALO + BLK].astype(f32) + total * (1.0 / NBRS)
    inverse = lax.rsqrt(jnp.mean(combined * combined, axis=1, keepdims=True) + epsilon)
    normed = (combined * inverse * gain_ref[...]).astype(bf16)
    normed_ref[...] = normed
    inv_ref[...] = inverse
    x = jnp.dot(normed, mix_ref[...], preferred_element_type=f32)
    square = x * x
    tanh = jnp.tanh(x * (root_two_pi + (root_two_pi * cubic) * square))
    half = 0.5 + 0.5 * tanh
    activation = x * half
    deriv_ref[...] = (
        half + activation * (1.0 - tanh) * (root_two_pi + (3.0 * root_two_pi * cubic) * square)
    ).astype(bf16)
    hidden = (combined + activation).astype(bf16)
    hidden_ref[...] = hidden
    pred = lax.dot_general(
        out_ref[...], hidden, (((1,), (1,)), ((), ())), preferred_element_type=f32
    )
    pred_ref[...] = pred
    rounded = pred.astype(bf16)
    for j in range(BLK // PIECE):
        send_ref[j] = rounded[:, j * PIECE : (j + 1) * PIECE]


def forward(neighbours, center, low, high, gain, w_mix, w_out):
    rows = pl.BlockSpec((BLK, D), lambda i: (i, 0))
    return pl.pallas_call(
        forward_kernel,
        grid=(STEPS,),
        in_specs=[
            pl.BlockSpec((NBRS, BLK), lambda i: (0, i)),
            whole((CELLS, D)),
            whole((HALO, D)),
            whole((HALO, D)),
            whole((1, D)),
            whole((D, D)),
            whole((ROWS, D)),
        ],
        out_specs=[
            rows,
            rows,
            rows,
            pl.BlockSpec((BLK, 1), lambda i: (i, 0)),
            pl.BlockSpec((ROWS, BLK), lambda i: (0, i)),
            pl.BlockSpec((BLK // PIECE, ROWS, PIECE), lambda i: (i, 0, 0)),
        ],
        out_shape=[
            jax.ShapeDtypeStruct((CELLS, D), bf16),
            jax.ShapeDtypeStruct((CELLS, D), bf16),
            jax.ShapeDtypeStruct((CELLS, D), bf16),
            jax.ShapeDtypeStruct((CELLS, 1), f32),
            jax.ShapeDtypeStruct((ROWS, CELLS), f32),
            jax.ShapeDtypeStruct((MEMBERS, ROWS, PIECE), bf16),
        ],
        scratch_shapes=[pltpu.VMEM((CELLS + 2 * HALO, D), bf16)],
        compiler_params=pltpu.CompilerParams(vmem_limit_bytes=VMEM_LIMIT),
        cost_estimate=pl.CostEstimate(
            flops=4 * CELLS * D * D, bytes_accessed=14 << 20, transcendentals=CELLS * D
        ),
        name="forward",
    )(neighbours, center, low, high, gain, w_mix, w_out)


def pair_kernel(pred_ref, obs_ref, area_ref, weight_ref, back_ref):
    first = pl.multiple_of(lax.axis_index("member") * PIECE, PIECE)
    area = area_ref[:, pl.ds(first, PIECE)]
    loss = jnp.zeros((16, PIECE), f32)
    for tile in range(ROWS // 16):
        rows = slice(16 * tile, 16 * tile + 16)
        preds = [pred_ref[m, rows].astype(f32) for m in range(MEMBERS)]
        observed = obs_ref[rows, pl.ds(first, PIECE)]
        slopes = [jnp.zeros((16, PIECE), f32)] * MEMBERS
        near = jnp.zeros((16, PIECE), f32)
        apart = jnp.zeros((16, PIECE), f32)
        for m in range(MEMBERS):
            gap = preds[m] - observed
            value = gap * gap + smoothing * smoothing
            near = near + value * lax.rsqrt(value)
            for k in range(m + 1, MEMBERS):
                gap = preds[m] - preds[k]
                value = gap * gap + smoothing * smoothing
                root = lax.rsqrt(value)
                apart = apart + value * root
                slope = gap * root
                slopes[m] = slopes[m] + slope
                slopes[k] = slopes[k] - slope
        loss = loss + weight_ref[rows] * (
            near * (1.0 / MEMBERS) - (2.0 * pair_coef) * apart
        )
        if tile < ROWS // 16 - 1:
            for m in range(MEMBERS):
                back_ref[m, rows] = slopes[m].astype(bf16)
    loss = jnp.sum(loss, axis=0, keepdims=True) * area
    high = loss.astype(bf16).astype(f32)
    middle = (loss - high).astype(bf16).astype(f32)
    low = loss - high - middle
    row = lax.broadcasted_iota(jnp.int32, (16, PIECE), 0) - (VARS - (ROWS - 16))
    for m in range(MEMBERS):
        tail = jnp.where(row < 0, slopes[m], 0.0)
        for at, part in enumerate((high, middle, low)):
            tail = jnp.where(row == at, part, tail)
        back_ref[m, ROWS - 16 : ROWS] = tail.astype(bf16)


def pair_terms(preds, observed, area, weight):
    return pl.pallas_call(
        pair_kernel,
        out_shape=jax.ShapeDtypeStruct((MEMBERS, ROWS, PIECE), bf16),
        cost_estimate=pl.CostEstimate(
            flops=1 << 24, bytes_accessed=1 << 20, transcendentals=1 << 20
        ),
        compiler_params=pltpu.CompilerParams(vmem_limit_bytes=VMEM_LIMIT),
        name="pairs",
    )(preds, observed, area, weight)


def weights_kernel(
    pos_ref, pair_ref, pred_ref, obs_ref, area_ref, weight_ref, out_ref, deriv_ref, hidden_ref, normed_ref,
    g_ref, pre_ref, loss_ref, keep_ref, send_ref, pre_all, out_sum,
):
    step = pl.program_id(0)

    @pl.when(step < STEPS)
    def _():
        pair = jnp.concatenate([pair_ref[j] for j in range(BLK // PIECE)], axis=1).astype(f32)
        loss_ref[...] = jnp.sum(pair[VARS : VARS + 3], axis=0, keepdims=True)
        gap = pred_ref[...] - obs_ref[...]
        slope = gap * lax.rsqrt(gap * gap + smoothing * smoothing)
        g = (
            weight_ref[...]
            * area_ref[...]
            * (slope * (1.0 / MEMBERS) - (2.0 * pair_coef) * pair)
        ).astype(bf16)
        g_ref[...] = g
        d_hidden = lax.dot_general(
            g, out_ref[...], (((0,), (0,)), ((), ())), preferred_element_type=f32
        )
        d_pre = (d_hidden * deriv_ref[...].astype(f32)).astype(bf16)
        pre_ref[...] = d_pre
        pre_all[pl.ds(pl.multiple_of(step * BLK, BLK), BLK)] = d_pre
        part = jnp.dot(g, hidden_ref[...], preferred_element_type=f32)

        @pl.when(step == 0)
        def _():
            out_sum[0:ROWS] = part
            out_sum[ROWS:] = jnp.zeros((128 - ROWS, D), f32)

        @pl.when(step > 0)
        def _():
            out_sum[0:ROWS] += part

    @pl.when(step >= STEPS)
    def _():
        x_at = lax.rem(pos_ref[0] + step - STEPS, 4)
        mix = lax.dot_general(
            normed_ref[...], pre_all[...], (((0,), (0,)), ((), ())), preferred_element_type=f32
        ).astype(bf16)
        out = out_sum[:, pl.ds(pl.multiple_of(x_at * BLK, BLK), BLK)].T.astype(bf16)
        mine = pos_ref[2] == 0
        for z in range(4):
            at = lax.rem(z + 4 - pos_ref[1], 4)
            for source, lanes in ((mix, slice(0, D)), (out, slice(D, WIDE))):
                even = source[64 * z : 64 * z + 32]
                odd = source[64 * z + 32 : 64 * z + 64]
                keep_ref[0, at, :, lanes] = jnp.where(mine, even, odd)
                send_ref[0, at, :, lanes] = jnp.where(mine, odd, even)


def weight_parts(pos, pair, pred, observed, area, weight, w_out, deriv, hidden, normed):
    first = lambda i: jnp.minimum(i, STEPS - 1)
    later = lambda i: jnp.maximum(i - STEPS, 0)
    rows = pl.BlockSpec((BLK, D), lambda i, pos: (first(i), 0))
    columns = pl.BlockSpec((ROWS, BLK), lambda i, pos: (0, first(i)))
    line = pl.BlockSpec((1, BLK), lambda i, pos: (0, first(i)))
    share = pl.BlockSpec((1, 4, 32, WIDE), lambda i, pos: (later(i), 0, 0, 0))
    return pl.pallas_call(
        weights_kernel,
        grid_spec=pltpu.PrefetchScalarGridSpec(
            num_scalar_prefetch=1,
            grid=(2 * STEPS,),
            in_specs=[
                pl.BlockSpec((BLK // PIECE, ROWS, PIECE), lambda i, pos: (first(i), 0, 0)),
                columns,
                columns,
                line,
                whole((ROWS, 1)),
                whole((ROWS, D)),
                rows,
                rows,
                pl.BlockSpec((CELLS, BLK), lambda i, pos: (0, lax.rem(pos[0] + later(i), 4))),
            ],
            out_specs=[columns, rows, line, share, share],
            scratch_shapes=[pltpu.VMEM((CELLS, D), bf16), pltpu.VMEM((128, D), f32)],
        ),
        out_shape=[
            jax.ShapeDtypeStruct((ROWS, CELLS), bf16),
            jax.ShapeDtypeStruct((CELLS, D), bf16),
            jax.ShapeDtypeStruct((1, CELLS), f32),
            jax.ShapeDtypeStruct((4, 4, 32, WIDE), bf16),
            jax.ShapeDtypeStruct((4, 4, 32, WIDE), bf16),
        ],
        compiler_params=pltpu.CompilerParams(vmem_limit_bytes=VMEM_LIMIT),
        cost_estimate=pl.CostEstimate(
            flops=3 * CELLS * D * D, bytes_accessed=14 << 20, transcendentals=0
        ),
        name="weights",
    )(pos, pair, pred, observed, area, weight, w_out, deriv, hidden, normed)


def latent_kernel(
    nb_ref, g_ref, out_ref, pre_ref, mix_ref, gain_ref, normed_ref, inv_ref,
    grad_ref, low_ref, high_ref, carry,
):
    step = pl.program_id(0)
    d_hidden = lax.dot_general(
        g_ref[...], out_ref[...], (((0,), (0,)), ((), ())), preferred_element_type=f32
    )
    d_normed = lax.dot_general(
        pre_ref[...], mix_ref[...], (((1,), (1,)), ((), ())), preferred_element_type=f32
    )
    gain = gain_ref[...]
    normed = normed_ref[...].astype(f32)
    mean = jnp.mean(normed * d_normed, axis=1, keepdims=True)
    d_combined = d_hidden + inv_ref[...] * (d_normed * gain - normed * (1.0 / gain) * mean)
    first = pl.multiple_of(step * BLK, BLK)
    base = lax.axis_index("space") * CELLS - HALO + first
    edges = edge_matrix(nb_ref, base, 1.0 / NBRS)
    row = lax.broadcasted_iota(jnp.int32, edges.shape, 0)
    column = lax.broadcasted_iota(jnp.int32, edges.shape, 1)
    edges = (edges + jnp.where(column == row + HALO, 1.0, 0.0)).astype(bf16)
    spread = lax.dot_general(
        edges, d_combined.astype(bf16), (((0,), (0,)), ((), ())), preferred_element_type=f32
    )

    @pl.when(step == 0)
    def _():
        low_ref[...] = spread[0:HALO].astype(bf16)
        grad_ref[0:HALO] = spread[HALO:BLK].astype(bf16)

    @pl.when(step > 0)
    def _():
        grad_ref[pl.ds(pl.multiple_of(first - HALO, HALO), BLK)] = (
            spread[0:BLK] + carry[...]
        ).astype(bf16)

    carry[...] = spread[BLK:]

    @pl.when(step == STEPS - 1)
    def _():
        grad_ref[CELLS - HALO :] = spread[BLK : BLK + HALO].astype(bf16)
        high_ref[...] = spread[BLK + HALO :].astype(bf16)


def latent_parts(neighbours, g, w_out, d_pre, w_mix, gain, normed, inverse):
    rows = pl.BlockSpec((BLK, D), lambda i: (i, 0))
    rim = jax.ShapeDtypeStruct((HALO, D), bf16)
    return pl.pallas_call(
        latent_kernel,
        grid=(STEPS,),
        in_specs=[
            pl.BlockSpec((NBRS, BLK), lambda i: (0, i)),
            pl.BlockSpec((ROWS, BLK), lambda i: (0, i)),
            whole((ROWS, D)),
            rows,
            whole((D, D)),
            whole((1, D)),
            rows,
            pl.BlockSpec((BLK, 1), lambda i: (i, 0)),
        ],
        out_specs=[whole((CELLS, D)), whole((HALO, D)), whole((HALO, D))],
        out_shape=[jax.ShapeDtypeStruct((CELLS, D), bf16), rim, rim],
        scratch_shapes=[pltpu.VMEM((BLK, D), f32)],
        compiler_params=pltpu.CompilerParams(vmem_limit_bytes=VMEM_LIMIT),
        cost_estimate=pl.CostEstimate(
            flops=4 * CELLS * D * D, bytes_accessed=10 << 20, transcendentals=0
        ),
        name="latent",
    )(neighbours, g, w_out, d_pre, w_mix, gain, normed, inverse)


def rim_kernel(grad_ref, low_ref, high_ref, out_ref):
    step = pl.program_id(0)
    other = jnp.where(step == 0, low_ref[...], high_ref[...])
    out_ref[...] = (grad_ref[...].astype(f32) + other.astype(f32)).astype(bf16)


def add_rims(grad, low, high):
    rim = pl.BlockSpec((HALO, D), lambda i: (i * (CELLS // HALO - 1), 0))
    return pl.pallas_call(
        rim_kernel,
        grid=(2,),
        in_specs=[rim, whole((HALO, D)), whole((HALO, D))],
        out_specs=rim,
        out_shape=jax.ShapeDtypeStruct((CELLS, D), bf16),
        input_output_aliases={0: 0},
        cost_estimate=pl.CostEstimate(flops=1 << 18, bytes_accessed=3 << 19, transcendentals=0),
        name="rims",
    )(grad, low, high)


def along(value, axis, move):
    pairs = [(i, move(i)) for i in range(lax.axis_size(axis))]
    return lax.ppermute(value, axis, [pair for pair in pairs if pair[1] is not None])


def next_band(i):
    return i + 1 if i < 31 else None


def last_band(i):
    return i - 1 if i > 0 else None


def summed(parts):
    total = parts[0].astype(f32)
    for part in parts[1:]:
        total = total + part.astype(f32)
    return total


def shards(latent, neighbours, norm_gain, w_mix, w_out, observed, cell_area, var_weight):
    space = lax.axis_index("space")
    pos = jnp.stack([space // 8, space // 2 % 4, space % 2]).astype(jnp.int32)
    center = latent[0]
    low = along(center[CELLS - HALO :], "space", next_band)
    high = along(center[:HALO], "space", last_band)
    gain = norm_gain.reshape(1, D)
    area = cell_area.reshape(1, CELLS)
    out_t = jnp.pad(w_out.T, ((0, ROWS - VARS), (0, 0)))
    observed = jnp.pad(observed, ((0, ROWS - VARS), (0, 0)))
    weight = jnp.pad(var_weight, (0, ROWS - VARS)).reshape(ROWS, 1)

    normed, hidden, deriv, inverse, pred, pieces = forward(
        neighbours, center, low, high, gain, w_mix, out_t
    )
    pieces = lax.all_to_all(pieces, "member", 0, 0, tiled=True)
    pairs = pair_terms(pieces, observed, area, weight)
    pairs = lax.all_to_all(pairs, "member", 0, 0, tiled=True)
    g, d_pre, losses, keep, send = weight_parts(
        pos, pairs, pred, observed, area, weight, out_t, deriv, hidden, normed
    )
    got = along(send, "space", lambda i: i ^ 1)
    grad, low_rim, high_rim = latent_parts(
        neighbours, g, out_t, d_pre, w_mix, gain, normed, inverse
    )
    from_above = along(low_rim, "space", last_band)
    from_below = along(high_rim, "space", next_band)
    grad = add_rims(grad, from_below, from_above)

    def over_x(k):
        return along(summed([keep[k], got[k]]).astype(bf16), "space", lambda i: (i + 8 * k) % 32)

    share = summed([keep[0], got[0]] + [over_x(k) for k in (1, 2, 3)]).astype(bf16)

    def over_z(k):
        return along(share[k], "space", lambda i: i // 8 * 8 + (i + 2 * k) % 8)

    share = summed([share[0]] + [over_z(k) for k in (1, 2, 3)]).astype(bf16)
    share = summed(
        [share] + [along(share, "member", lambda i: (i + 2 * k) % 8) for k in (1, 2, 3)]
    ).astype(bf16)
    totals = summed([share, along(share, "member", lambda i: i ^ 1)])
    grad_scale = 1.0 / math.sqrt(MEMBERS * CELLS * 32)
    return (
        losses.reshape(CELLS),
        grad[None],
        totals[:, :D] * grad_scale,
        totals[:, D : D + VARS] * grad_scale,
    )


def solution(mesh):
    return jax.shard_map(
        shards,
        mesh=mesh,
        in_specs=(
            P("member", "space", None),
            P(None, "space"),
            P(),
            P(),
            P(),
            P(None, "space"),
            P("space"),
            P(),
        ),
        out_specs=(P("space"), P("member", "space", None), P("space", None), P("space", None)),
        check_vma=False,
    )
```

time: 441 us -> 146 us (0.33)
  waiting for transfers between devices: 250 us -> 52.1 us
  other arithmetic: 76 us -> 4.46 us
  Pallas kernels: 0 us -> 38.5 us
  local copies, waits for them, and re-layouts: 42.6 us -> 7.09 us
  starting transfers between devices: 13.2 us -> 41 us
  blocking collectives: 24.5 us -> 0 us
  matrix products: 19.4 us -> 0 us
  between operations: 14.1 us -> 0.8 us
    psum x1 -> x0, waiting for transfers between devices: 121 us -> none  [shards(): totals = lax.psum(shares, 'member').astype(jnp.float32)]
    all_gather x1 -> x0, waiting for transfers between devices: 98.6 us -> none  [shards(): shard_piece = lax.all_gather(own_field, 'member', axis=0, tiled=True)]
    scatter-add x3 -> x0, other arithmetic: 42.7 us -> none  [the longest x1 38.9 us: shards(): spread = jnp.zeros(extended.shape, jnp.float32).at[local_edges].add(jnp.t...]
    pallas_call x0 -> x5, Pallas kernels: none -> 38.5 us  [the longest x1 12.9 us: forward(): pl.pallas_call(forward_kernel, grid=(STEPS,), in_specs=[pl.BlockSpec((NBR...]
    ppermute x4 -> x15, waiting for transfers between devices: 2.34 us -> 32.3 us  [along(): lax.ppermute(value, axis, [pair for pair in pairs if pair[1] is not None])]
    unnamed x4 -> x0, waiting for transfers between devices: 28.5 us -> none
    psum x1 -> x0, blocking collectives: 24.5 us -> none  [shards(): crps_field = lax.psum(local_losses, 'member')]
    gather x1 -> x0, local copies, waits for them, and re-layouts: 23 us -> none  [shards(): gathered = jnp.take(extended, local_edges, axis=0).astype(jnp.float32)]
  transfers between devices with their start and end apart: 7 -> 17, of which waited for: 5 -> 13; matrix products, arithmetic and copies ran while one was open for 16% -> 3% of each run, Pallas kernels for 0% -> 9%
where the time goes in v1:
time: 146 us; the launch traced here: 144 us
  waiting for transfers between devices  52.1 us (36%)
  starting transfers between devices  41 us (28%)
  Pallas kernels  38.5 us (26%)
  local copies, waits for them, and re-layouts  7.09 us (5%)
  other arithmetic  4.46 us (3%)
    ppermute x15, waiting for transfers between devices, along(): lax.ppermute(value, axis, [pair for pair in pairs if pair[1] is not None])  32.3 us
    ppermute x15, starting transfers between devices, along(): lax.ppermute(value, axis, [pair for pair in pairs if pair[1] is not None])  29.2 us
    pallas_call x1, Pallas kernels, forward(): pl.pallas_call(forward_kernel, grid=(STEPS,), in_specs=[pl.BlockSpec((NBR...  12.9 us
    pallas_call x1, Pallas kernels, weight_parts(): pl.pallas_call(weights_kernel, grid_spec=pltpu.PrefetchScalarGridSpec(num...  10.8 us
    pallas_call x1, Pallas kernels, latent_parts(): pl.pallas_call(latent_kernel, grid=(STEPS,), in_specs=[pl.BlockSpec((NBRS...  10.5 us
    all_to_all x1, waiting for transfers between devices, shards(): pairs = lax.all_to_all(pairs, 'member', 0, 0, tiled=True)  10.3 us
    all_to_all x1, waiting for transfers between devices, shards(): pieces = lax.all_to_all(pieces, 'member', 0, 0, tiled=True)  9.45 us
    all_to_all x1, starting transfers between devices, shards(): pieces = lax.all_to_all(pieces, 'member', 0, 0, tiled=True)  8.4 us
  transfers between devices with their start and end apart: 17, of which 13 were waited for; matrix products, arithmetic and copies ran while one was open for 3% of the time, Pallas kernels for 9%

profile of v1, /device:TPU:2, one launch (start us, length us, event | category | flops | bytes accessed | tf_op | source)
XLA Modules:
  0.0 143.9 jit_solution(8339909477136315076)
XLA Ops:
  1.7 5.9 %collective-permute-start.1 = (bf16[128,1024]{1,0:T(8,128)(2,1)S(1)}, bf16[128,1024]{1,0:T(8,128)(2,1)S(1)}, u32[]{:S(2)}, u32[]{:S(2)}) collective-permute-start(bf16[128,1024]{1,0:T(8,128)(2,1)S(1)} %get-tuple-element.35), channel_id=1, source_target_pairs={{1,0},{2,1},{3,2},{4,3},{5,4},{6,5},{7,6},{8,7},{9,8},{10,9},{11,1... | collective-permute-start | bytes 786440 | tf_op jit(solution)/shard_map/ppermute | solution.py:367
  7.7 1.9 %collective-permute-start = (bf16[128,1024]{1,0:T(8,128)(2,1)S(1)}, bf16[128,1024]{1,0:T(8,128)(2,1)S(1)}, u32[]{:S(2)}, u32[]{:S(2)}) collective-permute-start(bf16[128,1024]{1,0:T(8,128)(2,1)S(1)} %get-tuple-element.36), channel_id=1, source_target_pairs={{0,1},{1,2},{2,3},{3,4},{4,5},{5,6},{6,7},{7,8},{8,9},{9,10},{10,1... | collective-permute-start | bytes 786440 | tf_op jit(solution)/shard_map/ppermute | solution.py:367
  11.2 2.3 %collective-permute-done.1.high_ref = bf16[128,1024]{1,0:T(8,128)(2,1)S(1)} collective-permute-done((bf16[128,1024]{1,0:T(8,128)(2,1)S(1)}, bf16[128,1024]{1,0:T(8,128)(2,1)S(1)}, u32[]{:S(2)}, u32[]{:S(2)}) %collective-permute-start.1) | collective-permute-done | bytes 262176 | tf_op jit(solution)/shard_map/ppermute | solution.py:367
  13.6 4.5 %collective-permute-done.low_ref = bf16[128,1024]{1,0:T(8,128)(2,1)S(1)} collective-permute-done((bf16[128,1024]{1,0:T(8,128)(2,1)S(1)}, bf16[128,1024]{1,0:T(8,128)(2,1)S(1)}, u32[]{:S(2)}, u32[]{:S(2)}) %collective-permute-start) | collective-permute-done | bytes 262176 | tf_op jit(solution)/shard_map/ppermute | solution.py:367
  18.8 12.9 %forward.1 = (bf16[1024,1024]{1,0:T(8,128)(2,1)}, bf16[1024,1024]{1,0:T(8,128)(2,1)}, bf16[1024,1024]{1,0:T(8,128)(2,1)}, f32[1024,1]{1,0:T(8,128)}, f32[112,1024]{1,0:T(8,128)}, /*index=5*/bf16[8,112,128]{2,1,0:T(8,128)(2,1)}) custom-call(s32[4,1024]{1,0:T(4,128)} %nb_ref.3, bf16[1024,1024]{1,0:T(8,128)(2,1)} %bitcast.42, bf16[128,1024]{1,0:T(8,128)(2,1)} %copy-done.6, ...), custom_call_target="tpu_custom_call" | custom-call | flops 4294967296 | bytes 14680064 | tf_op jit(solution)/shard_map/forward/pallas_call | solution.py:91
  31.6 8.4 %all-to-all-start = ((bf16[8,112,128]{2,1,0:T(8,128)(2,1)}), bf16[8,112,128]{2,1,0:T(8,128)(2,1)S(1)}, u32[]{:S(2)}, u32[]{:S(2)}) async-start(bf16[8,112,128]{2,1,0:T(8,128)(2,1)} %get-tuple-element.18), calls=%async_computation | async-start | bytes 458752 | tf_op jit(solution)/shard_map/all_to_all | solution.py:400
  41.6 9.5 %all-to-all-done.pred_ref = bf16[8,112,128]{2,1,0:T(8,128)(2,1)S(1)} async-done(((bf16[8,112,128]{2,1,0:T(8,128)(2,1)}), bf16[8,112,128]{2,1,0:T(8,128)(2,1)S(1)}, u32[]{:S(2)}, u32[]{:S(2)}) %all-to-all-start) | async-done | bytes 229408 | tf_op jit(solution)/shard_map/all_to_all | solution.py:400
  51.7 2.4 %pairs.1 = bf16[8,112,128]{2,1,0:T(8,128)(2,1)} custom-call(bf16[8,112,128]{2,1,0:T(8,128)(2,1)} %copy-done.4, f32[112,1024]{1,0:T(8,128)} %pad.13.obs_ref, f32[1,1024]{1,0:T(1,128)} %bitcast.43, f32[112,1]{1,0:T(8,128)} %copy.13.weight_ref), custom_call_target="tpu_custom_call" | custom-call | flops 16777216 | bytes 1048576 | tf_op jit(solution)/shard_map/pairs/pallas_call | solution.py:170
  54.2 3.4 %all-to-all-start.1 = ((bf16[8,112,128]{2,1,0:T(8,128)(2,1)}), bf16[8,112,128]{2,1,0:T(8,128)(2,1)S(1)}, u32[]{:S(2)}, u32[]{:S(2)}) async-start(bf16[8,112,128]{2,1,0:T(8,128)(2,1)} %pairs.1), calls=%async_computation.1 | async-start | bytes 458752 | tf_op jit(solution)/shard_map/all_to_all | solution.py:402
  58.2 10.3 %all-to-all-done.1.pair_ref = bf16[8,112,128]{2,1,0:T(8,128)(2,1)S(1)} async-done(((bf16[8,112,128]{2,1,0:T(8,128)(2,1)}), bf16[8,112,128]{2,1,0:T(8,128)(2,1)S(1)}, u32[]{:S(2)}, u32[]{:S(2)}) %all-to-all-start.1) | async-done | bytes 229408 | tf_op jit(solution)/shard_map/all_to_all | solution.py:402
  69.2 10.8 %weights.1 = (bf16[112,1024]{1,0:T(8,128)(2,1)}, bf16[1024,1024]{1,0:T(8,128)(2,1)}, f32[1,1024]{1,0:T(1,128)}, bf16[4,4,32,1152]{3,2,1,0:T(8,128)(2,1)}, bf16[4,4,32,1152]{3,2,1,0:T(8,128)(2,1)}) custom-call(s32[3]{0:T(128)} %pad_add_fusion.pos_ref, bf16[8,112,128]{2,1,0:T(8,128)(2,1)} %copy-done.3, f32[112,1024]{1,0:T(8,128)} %get-tuple-element.19.pred_ref, ...), custom_call_target="tpu_custom_call" | custom-call | flops 3221225472 | bytes 14680064 | tf_op jit(solution)/shard_map/weights/pallas_call | solution.py:240
  80.1 3.0 %collective-permute-done.4 = bf16[4,4,32,1152]{3,2,1,0:T(8,128)(2,1)S(1)} collective-permute-done((bf16[4,4,32,1152]{3,2,1,0:T(8,128)(2,1)}, bf16[4,4,32,1152]{3,2,1,0:T(8,128)(2,1)S(1)}, u32[]{:S(2)}, u32[]{:S(2)}) %collective-permute-start.4) | collective-permute-done | bytes 1179680 | tf_op jit(solution)/shard_map/ppermute | solution.py:367
  86.6 2.4 %collective-permute-start.6 = (bf16[4,32,1152]{2,1,0:T(8,128)(2,1)S(1)}, bf16[4,32,1152]{2,1,0:T(8,128)(2,1)S(1)}, u32[]{:S(2)}, u32[]{:S(2)}) collective-permute-start(bf16[4,32,1152]{2,1,0:T(8,128)(2,1)S(1)} %get-tuple-element.34), channel_id=1, source_target_pairs={{0,16},{1,17},{2,18},{3,19},{4,20},{5,21},{6,22},{7,23},{8,24},{9,... | collective-permute-start | bytes 884744 | tf_op jit(solution)/shard_map/ppermute | solution.py:367
  89.0 5.4 %collective-permute-done.5 = bf16[4,32,1152]{2,1,0:T(8,128)(2,1)S(1)} collective-permute-done((bf16[4,32,1152]{2,1,0:T(8,128)(2,1)S(1)}, bf16[4,32,1152]{2,1,0:T(8,128)(2,1)S(1)}, u32[]{:S(2)}, u32[]{:S(2)}) %collective-permute-start.5) | collective-permute-done | bytes 294944 | tf_op jit(solution)/shard_map/ppermute | solution.py:367
  95.0 7.0 %collective-permute-done.6 = bf16[4,32,1152]{2,1,0:T(8,128)(2,1)S(1)} collective-permute-done((bf16[4,32,1152]{2,1,0:T(8,128)(2,1)S(1)}, bf16[4,32,1152]{2,1,0:T(8,128)(2,1)S(1)}, u32[]{:S(2)}, u32[]{:S(2)}) %collective-permute-start.6) | collective-permute-done | bytes 294944 | tf_op jit(solution)/shard_map/ppermute | solution.py:367
  104.6 2.5 %collective-permute-start.10 = (bf16[32,1152]{1,0:T(8,128)(2,1)S(1)}, bf16[32,1152]{1,0:T(8,128)(2,1)S(1)}, u32[]{:S(2)}, u32[]{:S(2)}) collective-permute-start(bf16[32,1152]{1,0:T(8,128)(2,1)S(1)} %get-tuple-element.38), channel_id=1, source_target_pairs={{0,6},{1,7},{2,0},{3,1},{4,2},{5,3},{6,4},{7,5},{8,14},{9,15},{10,... | collective-permute-start | bytes 221192 | tf_op jit(solution)/shard_map/ppermute | solution.py:367
  107.2 2.8 %collective-permute-done.8 = bf16[32,1152]{1,0:T(8,128)(2,1)S(1)} collective-permute-done((bf16[32,1152]{1,0:T(8,128)(2,1)S(1)}, bf16[32,1152]{1,0:T(8,128)(2,1)S(1)}, u32[]{:S(2)}, u32[]{:S(2)}) %collective-permute-start.8) | collective-permute-done | bytes 73760 | tf_op jit(solution)/shard_map/ppermute | solution.py:367
  110.0 2.5 %collective-permute-done.9 = bf16[32,1152]{1,0:T(8,128)(2,1)S(1)} collective-permute-done((bf16[32,1152]{1,0:T(8,128)(2,1)S(1)}, bf16[32,1152]{1,0:T(8,128)(2,1)S(1)}, u32[]{:S(2)}, u32[]{:S(2)}) %collective-permute-start.9) | collective-permute-done | bytes 73760 | tf_op jit(solution)/shard_map/ppermute | solution.py:367
  115.1 10.5 %latent.1 = (bf16[1024,1024]{1,0:T(8,128)(2,1)}, bf16[128,1024]{1,0:T(8,128)(2,1)}, bf16[128,1024]{1,0:T(8,128)(2,1)}) custom-call(s32[4,1024]{1,0:T(4,128)} %nb_ref.3, bf16[112,1024]{1,0:T(8,128)(2,1)} %get-tuple-element.24.g_ref, bf16[112,1024]{1,0:T(8,128)(2,1)} %pad.12.out_ref, bf16[1024,1024]{1,0:T(8,128)(2,1)} %get-tuple-element.25.pre_ref, ...), custom_call_target="tpu_custom_call" | custom-call | flops 4294967296 | bytes 10485760 | tf_op jit(solution)/shard_map/latent/pallas_call | solution.py:321
  125.6 1.9 %collective-permute-start.2 = (bf16[128,1024]{1,0:T(8,128)(2,1)}, bf16[128,1024]{1,0:T(8,128)(2,1)S(1)}, u32[]{:S(2)}, u32[]{:S(2)}) collective-permute-start(bf16[128,1024]{1,0:T(8,128)(2,1)} %get-tuple-element.28), channel_id=1, source_target_pairs={{0,1},{1,2},{2,3},{3,4},{4,5},{5,6},{6,7},{7,8},{8,9},{9,10},{10,1... | collective-permute-start | bytes 786440 | tf_op jit(solution)/shard_map/ppermute | solution.py:367
  127.5 6.3 %collective-permute-start.3 = (bf16[128,1024]{1,0:T(8,128)(2,1)}, bf16[128,1024]{1,0:T(8,128)(2,1)S(1)}, u32[]{:S(2)}, u32[]{:S(2)}) collective-permute-start(bf16[128,1024]{1,0:T(8,128)(2,1)} %get-tuple-element.29), channel_id=1, source_target_pairs={{1,0},{2,1},{3,2},{4,3},{5,4},{6,5},{7,6},{8,7},{9,8},{10,9},{11,1... | collective-permute-start | bytes 786440 | tf_op jit(solution)/shard_map/ppermute | solution.py:367
  133.9 1.9 %collective-permute-start.14 = (bf16[32,1152]{1,0:T(8,128)(2,1)S(1)}, bf16[32,1152]{1,0:T(8,128)(2,1)S(1)}, u32[]{:S(2)}, u32[]{:S(2)}) collective-permute-start(bf16[32,1152]{1,0:T(8,128)(2,1)S(1)} %add_convert_fusion.3), channel_id=1, source_target_pairs={{0,32},{32,0},{64,96},{96,64},{128,160},{160,128},{192,224},{224,1... | collective-permute-start | bytes 221192 | tf_op jit(solution)/shard_map/ppermute | solution.py:367
  137.0 2.7 %collective-permute-done.3.high_ref = bf16[128,1024]{1,0:T(8,128)(2,1)S(1)} collective-permute-done((bf16[128,1024]{1,0:T(8,128)(2,1)}, bf16[128,1024]{1,0:T(8,128)(2,1)S(1)}, u32[]{:S(2)}, u32[]{:S(2)}) %collective-permute-start.3) | collective-permute-done | bytes 262176 | tf_op jit(solution)/shard_map/ppermute | solution.py:367
  140.4 2.0 %rims.1 = bf16[1024,1024]{1,0:T(8,128)(2,1)} custom-call(bf16[1024,1024]{1,0:T(8,128)(2,1)} %get-tuple-element.27.grad_ref, bf16[128,1024]{1,0:T(8,128)(2,1)} %copy-done.1, bf16[128,1024]{1,0:T(8,128)(2,1)} %copy-done.2), custom_call_target="tpu_custom_call", output_to_operand_aliasing={{}: (0, {})} | custom-call | flops 262144 | bytes 1572864 | tf_op jit(solution)/shard_map/rims/pallas_call | solution.py:353
  (45 shorter events, 19.8 us)
Async XLA Ops:
  1.7 11.9 %collective-permute-start.1 = (bf16[128,1024]{1,0:T(8,128)(2,1)S(1)}, bf16[128,1024]{1,0:T(8,128)(2,1)S(1)}, u32[]{:S(2)}, u32[]{:S(2)}) collective-permute-start(bf16[128,1024]{1,0:T(8,128)(2,1)S(1)} %get-tuple-element.35), channel_id=1, source_target_pairs={{1,0},{2,1},{3,2},{4,3},{5,4},{6,5},{7,6},{8,7},{9,8},{10,9},{11,1... | collective-permute-start | bytes 786440 | tf_op jit(solution)/shard_map/ppermute | solution.py:367
  7.7 10.4 %collective-permute-start = (bf16[128,1024]{1,0:T(8,128)(2,1)S(1)}, bf16[128,1024]{1,0:T(8,128)(2,1)S(1)}, u32[]{:S(2)}, u32[]{:S(2)}) collective-permute-start(bf16[128,1024]{1,0:T(8,128)(2,1)S(1)} %get-tuple-element.36), channel_id=1, source_target_pairs={{0,1},{1,2},{2,3},{3,4},{4,5},{5,6},{6,7},{7,8},{8,9},{9,10},{10,1... | collective-permute-start | bytes 786440 | tf_op jit(solution)/shard_map/ppermute | solution.py:367
  13.6 4.5 %copy-start.5 = (bf16[128,1024]{1,0:T(8,128)(2,1)}, bf16[128,1024]{1,0:T(8,128)(2,1)S(1)}, u32[]{:S(2)}) copy-start(bf16[128,1024]{1,0:T(8,128)(2,1)S(1)} %collective-permute-done.1.high_ref) | copy-start | bytes 786436
  18.0 0.7 copy-start.6
  18.7 21.3 %copy-start.7 = (f32[100]{0:T(128)S(1)}, f32[100]{0:T(128)}, u32[]{:S(2)}) copy-start(f32[100]{0:T(128)} %param.15) | copy-start | bytes 1204
  18.7 22.0 %copy-start = (f32[100,1024]{1,0:T(8,128)S(1)}, f32[100,1024]{1,0:T(8,128)}, u32[]{:S(2)}) copy-start(f32[100,1024]{1,0:T(8,128)} %param.13) | copy-start | bytes 1228804
  31.6 19.4 %all-to-all-start = ((bf16[8,112,128]{2,1,0:T(8,128)(2,1)}), bf16[8,112,128]{2,1,0:T(8,128)(2,1)S(1)}, u32[]{:S(2)}, u32[]{:S(2)}) async-start(bf16[8,112,128]{2,1,0:T(8,128)(2,1)} %get-tuple-element.18), calls=%async_computation | async-start | bytes 458752 | tf_op jit(solution)/shard_map/all_to_all | solution.py:400
  51.0 0.7 copy-start.4
  54.2 14.4 %all-to-all-start.1 = ((bf16[8,112,128]{2,1,0:T(8,128)(2,1)}), bf16[8,112,128]{2,1,0:T(8,128)(2,1)S(1)}, u32[]{:S(2)}, u32[]{:S(2)}) async-start(bf16[8,112,128]{2,1,0:T(8,128)(2,1)} %pairs.1), calls=%async_computation.1 | async-start | bytes 458752 | tf_op jit(solution)/shard_map/all_to_all | solution.py:402
  80.0 3.1 %collective-permute-start.4 = (bf16[4,4,32,1152]{3,2,1,0:T(8,128)(2,1)}, bf16[4,4,32,1152]{3,2,1,0:T(8,128)(2,1)S(1)}, u32[]{:S(2)}, u32[]{:S(2)}) collective-permute-start(bf16[4,4,32,1152]{3,2,1,0:T(8,128)(2,1)} %get-tuple-element.31), channel_id=1, source_target_pairs={{0,1},{1,0},{2,3},{3,2},{4,5},{5,4},{6,7},{7,6},{8,9},{9,8},{10,11... | collective-permute-start | bytes 3538952 | tf_op jit(solution)/shard_map/ppermute | solution.py:367
  84.5 9.9 %collective-permute-start.5 = (bf16[4,32,1152]{2,1,0:T(8,128)(2,1)S(1)}, bf16[4,32,1152]{2,1,0:T(8,128)(2,1)S(1)}, u32[]{:S(2)}, u32[]{:S(2)}) collective-permute-start(bf16[4,32,1152]{2,1,0:T(8,128)(2,1)S(1)} %get-tuple-element.32), channel_id=1, source_target_pairs={{0,8},{1,9},{2,10},{3,11},{4,12},{5,13},{6,14},{7,15},{8,16},{9,17... | collective-permute-start | bytes 884744 | tf_op jit(solution)/shard_map/ppermute | solution.py:367
  86.1 9.0 %collective-permute-start.7 = (bf16[4,32,1152]{2,1,0:T(8,128)(2,1)S(1)}, bf16[4,32,1152]{2,1,0:T(8,128)(2,1)S(1)}, u32[]{:S(2)}, u32[]{:S(2)}) collective-permute-start(bf16[4,32,1152]{2,1,0:T(8,128)(2,1)S(1)} %get-tuple-element.33), channel_id=1, source_target_pairs={{0,24},{1,25},{2,26},{3,27},{4,28},{5,29},{6,30},{7,31},{8,0},{9,1... | collective-permute-start | bytes 884744 | tf_op jit(solution)/shard_map/ppermute | solution.py:367
  86.6 15.5 %collective-permute-start.6 = (bf16[4,32,1152]{2,1,0:T(8,128)(2,1)S(1)}, bf16[4,32,1152]{2,1,0:T(8,128)(2,1)S(1)}, u32[]{:S(2)}, u32[]{:S(2)}) collective-permute-start(bf16[4,32,1152]{2,1,0:T(8,128)(2,1)S(1)} %get-tuple-element.34), channel_id=1, source_target_pairs={{0,16},{1,17},{2,18},{3,19},{4,20},{5,21},{6,22},{7,23},{8,24},{9,... | collective-permute-start | bytes 884744 | tf_op jit(solution)/shard_map/ppermute | solution.py:367
  103.3 6.7 %collective-permute-start.8 = (bf16[32,1152]{1,0:T(8,128)(2,1)S(1)}, bf16[32,1152]{1,0:T(8,128)(2,1)S(1)}, u32[]{:S(2)}, u32[]{:S(2)}) collective-permute-start(bf16[32,1152]{1,0:T(8,128)(2,1)S(1)} %get-tuple-element.37), channel_id=1, source_target_pairs={{0,2},{1,3},{2,4},{3,5},{4,6},{5,7},{6,0},{7,1},{8,10},{9,11},{10,... | collective-permute-start | bytes 221192 | tf_op jit(solution)/shard_map/ppermute | solution.py:367
  104.6 5.3 %collective-permute-start.10 = (bf16[32,1152]{1,0:T(8,128)(2,1)S(1)}, bf16[32,1152]{1,0:T(8,128)(2,1)S(1)}, u32[]{:S(2)}, u32[]{:S(2)}) collective-permute-start(bf16[32,1152]{1,0:T(8,128)(2,1)S(1)} %get-tuple-element.38), channel_id=1, source_target_pairs={{0,6},{1,7},{2,0},{3,1},{4,2},{5,3},{6,4},{7,5},{8,14},{9,15},{10,... | collective-permute-start | bytes 221192 | tf_op jit(solution)/shard_map/ppermute | solution.py:367
  107.2 5.3 %collective-permute-start.9 = (bf16[32,1152]{1,0:T(8,128)(2,1)S(1)}, bf16[32,1152]{1,0:T(8,128)(2,1)S(1)}, u32[]{:S(2)}, u32[]{:S(2)}) collective-permute-start(bf16[32,1152]{1,0:T(8,128)(2,1)S(1)} %get-tuple-element.39), channel_id=1, source_target_pairs={{0,4},{1,5},{2,6},{3,7},{4,0},{5,1},{6,2},{7,3},{8,12},{9,13},{10,... | collective-permute-start | bytes 221192 | tf_op jit(solution)/shard_map/ppermute | solution.py:367
  112.5 21.4 %collective-permute-start.13 = (bf16[32,1152]{1,0:T(8,128)(2,1)S(1)}, bf16[32,1152]{1,0:T(8,128)(2,1)S(1)}, u32[]{:S(2)}, u32[]{:S(2)}) collective-permute-start(bf16[32,1152]{1,0:T(8,128)(2,1)S(1)} %fusion.8), channel_id=1, source_target_pairs={{0,192},{32,224},{64,0},{96,32},{128,64},{160,96},{192,128},{224,1... | collective-permute-start | bytes 221192 | tf_op jit(solution)/shard_map/ppermute | solution.py:367
  113.4 20.5 %collective-permute-start.12 = (bf16[32,1152]{1,0:T(8,128)(2,1)S(1)}, bf16[32,1152]{1,0:T(8,128)(2,1)S(1)}, u32[]{:S(2)}, u32[]{:S(2)}) collective-permute-start(bf16[32,1152]{1,0:T(8,128)(2,1)S(1)} %fusion.8), channel_id=1, source_target_pairs={{0,128},{32,160},{64,192},{96,224},{128,0},{160,32},{192,64},{224,... | collective-permute-start | bytes 221192 | tf_op jit(solution)/shard_map/ppermute | solution.py:367
  114.8 19.0 %collective-permute-start.11 = (bf16[32,1152]{1,0:T(8,128)(2,1)S(1)}, bf16[32,1152]{1,0:T(8,128)(2,1)S(1)}, u32[]{:S(2)}, u32[]{:S(2)}) collective-permute-start(bf16[32,1152]{1,0:T(8,128)(2,1)S(1)} %fusion.8), channel_id=1, source_target_pairs={{0,64},{32,96},{64,128},{96,160},{128,192},{160,224},{192,0},{224,... | collective-permute-start | bytes 221192 | tf_op jit(solution)/shard_map/ppermute | solution.py:367
  125.6 11.4 %collective-permute-start.2 = (bf16[128,1024]{1,0:T(8,128)(2,1)}, bf16[128,1024]{1,0:T(8,128)(2,1)S(1)}, u32[]{:S(2)}, u32[]{:S(2)}) collective-permute-start(bf16[128,1024]{1,0:T(8,128)(2,1)} %get-tuple-element.28), channel_id=1, source_target_pairs={{0,1},{1,2},{2,3},{3,4},{4,5},{5,6},{6,7},{7,8},{8,9},{9,10},{10,1... | collective-permute-start | bytes 786440 | tf_op jit(solution)/shard_map/ppermute | solution.py:367
  127.5 12.1 %collective-permute-start.3 = (bf16[128,1024]{1,0:T(8,128)(2,1)}, bf16[128,1024]{1,0:T(8,128)(2,1)S(1)}, u32[]{:S(2)}, u32[]{:S(2)}) collective-permute-start(bf16[128,1024]{1,0:T(8,128)(2,1)} %get-tuple-element.29), channel_id=1, source_target_pairs={{1,0},{2,1},{3,2},{4,3},{5,4},{6,5},{7,6},{8,7},{9,8},{10,9},{11,1... | collective-permute-start | bytes 786440 | tf_op jit(solution)/shard_map/ppermute | solution.py:367
  133.9 8.6 %collective-permute-start.14 = (bf16[32,1152]{1,0:T(8,128)(2,1)S(1)}, bf16[32,1152]{1,0:T(8,128)(2,1)S(1)}, u32[]{:S(2)}, u32[]{:S(2)}) collective-permute-start(bf16[32,1152]{1,0:T(8,128)(2,1)S(1)} %add_convert_fusion.3), channel_id=1, source_target_pairs={{0,32},{32,0},{64,96},{96,64},{128,160},{160,128},{192,224},{224,1... | collective-permute-start | bytes 221192 | tf_op jit(solution)/shard_map/ppermute | solution.py:367
  137.0 2.7 %copy-start.1 = (bf16[128,1024]{1,0:T(8,128)(2,1)}, bf16[128,1024]{1,0:T(8,128)(2,1)S(1)}, u32[]{:S(2)}) copy-start(bf16[128,1024]{1,0:T(8,128)(2,1)S(1)} %collective-permute-done.2.low_ref) | copy-start | bytes 786436
  139.7 0.7 copy-start.2
  (1 other events, 0.7 us)

commit v2 on v1

--- a/solution.py
+++ b/solution.py
@@ -36,38 +36,28 @@
     return pl.BlockSpec(shape, lambda *_: (0,) * len(shape), pipeline_mode=pl.Buffered(1))
 
 
-def edge_matrix(nb_ref, base, scale):
-    local = (nb_ref[...] - base).T
-    column = lax.broadcasted_iota(jnp.int32, (BLK, BLK + 2 * HALO), 1)
-    count = jnp.zeros((BLK, BLK + 2 * HALO), f32)
+def edge_matrix(neighbours, base, width, scale):
+    local = (neighbours - base).T
+    column = lax.broadcasted_iota(jnp.int32, (local.shape[0], width), 1)
+    count = jnp.zeros(column.shape, f32)
     for k in range(NBRS):
         count = count + jnp.where(column == local[:, k : k + 1], scale, 0.0)
     return count
 
 
-def forward_kernel(
-    nb_ref, lat_ref, low_ref, high_ref, gain_ref, mix_ref, out_ref,
-    normed_ref, hidden_ref, deriv_ref, inv_ref, pred_ref, send_ref, ext,
-):
-    step = pl.program_id(0)
-
-    @pl.when(step == 0)
-    def _():
-        ext[0:HALO] = low_ref[...]
-        ext[HALO : HALO + CELLS] = lat_ref[...]
-        ext[HALO + CELLS :] = high_ref[...]
-
-    first = pl.multiple_of(step * BLK, BLK)
-    base = lax.axis_index("space") * CELLS - HALO + first
-    edges = edge_matrix(nb_ref, base, 1.0).astype(bf16)
-    window = ext[pl.ds(first, BLK + 2 * HALO)]
+def gathered(neighbours, base, window):
+    edges = edge_matrix(neighbours, base, window.shape[0], 1.0).astype(bf16)
     total = jnp.dot(edges, window, preferred_element_type=f32)
-    combined = window[HALO : HALO + BLK].astype(f32) + total * (1.0 / NBRS)
+    own = window[HALO : HALO + edges.shape[0]].astype(f32)
+    return own + total * (1.0 / NBRS)
+
+
+def decode(combined, gain, mix, out_t, normed_ref, hidden_ref, deriv_ref, inv_ref, pred_ref, send_ref):
     inverse = lax.rsqrt(jnp.mean(combined * combined, axis=1, keepdims=True) + epsilon)
-    normed = (combined * inverse * gain_ref[...]).astype(bf16)
+    normed = (combined * inverse * gain).astype(bf16)
     normed_ref[...] = normed
     inv_ref[...] = inverse
-    x = jnp.dot(normed, mix_ref[...], preferred_element_type=f32)
+    x = jnp.dot(normed, mix, preferred_element_type=f32)
     square = x * x
     tanh = jnp.tanh(x * (root_two_pi + (root_two_pi * cubic) * square))
     half = 0.5 + 0.5 * tanh
@@ -77,56 +67,125 @@
     ).astype(bf16)
     hidden = (combined + activation).astype(bf16)
     hidden_ref[...] = hidden
-    pred = lax.dot_general(
-        out_ref[...], hidden, (((1,), (1,)), ((), ())), preferred_element_type=f32
-    )
+    pred = lax.dot_general(out_t, hidden, (((1,), (1,)), ((), ())), preferred_element_type=f32)
     pred_ref[...] = pred
     rounded = pred.astype(bf16)
     for j in range(BLK // PIECE):
         send_ref[j] = rounded[:, j * PIECE : (j + 1) * PIECE]
 
 
+def interior_kernel(
+    nb0_ref, nb1_ref, lat_ref, gain_ref, mix_ref, out_ref,
+    out_t_ref, normed_ref, hidden_ref, deriv_ref, inv_ref, pred_ref, send_ref,
+):
+    step = pl.program_id(0)
+
+    @pl.when(step == 0)
+    def _():
+        row = lax.broadcasted_iota(jnp.int32, (ROWS, VARS), 0)
+        column = lax.broadcasted_iota(jnp.int32, (ROWS, VARS), 1)
+        pick = jnp.where(row == column, 1.0, 0.0).astype(bf16)
+        out_t_ref[...] = lax.dot_general(
+            pick, out_ref[...], (((1,), (1,)), ((), ())), preferred_element_type=f32
+        ).astype(bf16)
+
+    first = pl.multiple_of(step * BLK, BLK)
+    neighbours = jnp.concatenate([nb0_ref[...], nb1_ref[...]], axis=1)
+    base = lax.axis_index("space") * CELLS + first
+    combined = gathered(neighbours, base, lat_ref[pl.ds(first, BLK + 2 * HALO)])
+    decode(
+        combined, gain_ref[...], mix_ref[...], out_t_ref[...],
+        normed_ref, hidden_ref, deriv_ref, inv_ref, pred_ref, send_ref,
+    )
+
+
+def rim_cells_kernel(
+    nb0_ref, nb1_ref, last_ref, head_ref, low_ref, high_ref, gain_ref, mix_ref, out_t_ref,
+    *refs,
+):
+    start = lax.axis_index("space") * CELLS
+    window = jnp.concatenate([last_ref[...], high_ref[...]], axis=0)
+    last = gathered(nb0_ref[...], start + CELLS - BLK, window)
+    window = jnp.concatenate([low_ref[...], head_ref[...]], axis=0)
+    head = gathered(nb1_ref[...], start - HALO, window)
+    combined = jnp.concatenate([last, head], axis=0)
+    decode(combined, gain_ref[...], mix_ref[...], out_t_ref[...], *refs[6:])
+
+
 def forward(neighbours, center, low, high, gain, w_mix, w_out):
-    rows = pl.BlockSpec((BLK, D), lambda i: (i, 0))
-    return pl.pallas_call(
-        forward_kernel,
-        grid=(STEPS,),
+    shapes = [
+        jax.ShapeDtypeStruct((CELLS, D), bf16),
+        jax.ShapeDtypeStruct((CELLS, D), bf16),
+        jax.ShapeDtypeStruct((CELLS, D), bf16),
+        jax.ShapeDtypeStruct((CELLS, 1), f32),
+        jax.ShapeDtypeStruct((ROWS, CELLS), f32),
+        jax.ShapeDtypeStruct((MEMBERS, ROWS, PIECE), bf16),
+    ]
+
+    def blocks(at):
+        rows = pl.BlockSpec((BLK, D), lambda i: (at(i), 0))
+        return [
+            rows,
+            rows,
+            rows,
+            pl.BlockSpec((BLK, 1), lambda i: (at(i), 0)),
+            pl.BlockSpec((ROWS, BLK), lambda i: (0, at(i))),
+            pl.BlockSpec((BLK // PIECE, ROWS, PIECE), lambda i: (at(i), 0, 0)),
+        ]
+
+    def edges_at(column):
+        return pl.BlockSpec((NBRS, PIECE), lambda i: (0, column(i)))
+
+    def cost(steps):
+        return pl.CostEstimate(
+            flops=steps * 4 * BLK * D * D, bytes_accessed=steps * 3 << 20, transcendentals=steps * BLK * D
+        )
+
+    out_t, *arrays = pl.pallas_call(
+        interior_kernel,
+        grid=(STEPS - 1,),
         in_specs=[
-            pl.BlockSpec((NBRS, BLK), lambda i: (0, i)),
+            edges_at(lambda i: 2 * i + 1),
+            edges_at(lambda i: 2 * i + 2),
             whole((CELLS, D)),
+            whole((1, D)),
+            whole((D, D)),
+            whole((D, VARS)),
+        ],
+        out_specs=[whole((ROWS, D))] + blocks(lambda i: i),
+        out_shape=[jax.ShapeDtypeStruct((ROWS, D), bf16)] + shapes,
+        compiler_params=pltpu.CompilerParams(vmem_limit_bytes=VMEM_LIMIT),
+        cost_estimate=cost(STEPS - 1),
+        name="interior",
+    )(neighbours, neighbours, center, gain, w_mix, w_out)
+    arrays = pl.pallas_call(
+        rim_cells_kernel,
+        grid=(1,),
+        in_specs=[
+            edges_at(lambda i: MEMBERS - 1),
+            edges_at(lambda i: 0),
+            pl.BlockSpec((BLK, D), lambda i: (STEPS - 1, 0)),
+            pl.BlockSpec((BLK, D), lambda i: (0, 0)),
             whole((HALO, D)),
             whole((HALO, D)),
             whole((1, D)),
             whole((D, D)),
             whole((ROWS, D)),
-        ],
-        out_specs=[
-            rows,
-            rows,
-            rows,
-            pl.BlockSpec((BLK, 1), lambda i: (i, 0)),
-            pl.BlockSpec((ROWS, BLK), lambda i: (0, i)),
-            pl.BlockSpec((BLK // PIECE, ROWS, PIECE), lambda i: (i, 0, 0)),
-        ],
-        out_shape=[
-            jax.ShapeDtypeStruct((CELLS, D), bf16),
-            jax.ShapeDtypeStruct((CELLS, D), bf16),
-            jax.ShapeDtypeStruct((CELLS, D), bf16),
-            jax.ShapeDtypeStruct((CELLS, 1), f32),
-            jax.ShapeDtypeStruct((ROWS, CELLS), f32),
-            jax.ShapeDtypeStruct((MEMBERS, ROWS, PIECE), bf16),
-        ],
-        scratch_shapes=[pltpu.VMEM((CELLS + 2 * HALO, D), bf16)],
+        ]
+        + [pl.BlockSpec(memory_space=pl.ANY)] * len(shapes),
+        out_specs=blocks(lambda i: STEPS - 1),
+        out_shape=shapes,
+        input_output_aliases={9 + i: i for i in range(len(shapes))},
         compiler_params=pltpu.CompilerParams(vmem_limit_bytes=VMEM_LIMIT),
-        cost_estimate=pl.CostEstimate(
-            flops=4 * CELLS * D * D, bytes_accessed=14 << 20, transcendentals=CELLS * D
-        ),
-        name="forward",
-    )(neighbours, center, low, high, gain, w_mix, w_out)
+        cost_estimate=cost(1),
+        name="rim_cells",
+    )(neighbours, neighbours, center, center, low, high, gain, w_mix, out_t, *arrays)
+    return out_t, arrays
 
 
 def pair_kernel(pred_ref, obs_ref, area_ref, weight_ref, back_ref):
-    first = pl.multiple_of(lax.axis_index("member") * PIECE, PIECE)
+    piece = lax.rem(lax.axis_index("member") + 1, MEMBERS)
+    first = pl.multiple_of(piece * PIECE, PIECE)
     area = area_ref[:, pl.ds(first, PIECE)]
     loss = jnp.zeros((16, PIECE), f32)
     for tile in range(ROWS // 16):
@@ -179,7 +238,7 @@
 
 
 def weights_kernel(
-    pos_ref, pair_ref, pred_ref, obs_ref, area_ref, weight_ref, out_ref, deriv_ref, hidden_ref, normed_ref,
+    pos_ref, pair_ref, pred_ref, obs0_ref, obs1_ref, area0_ref, area1_ref, weight_ref, out_ref, deriv_ref, hidden_ref, normed_ref,
     g_ref, pre_ref, loss_ref, keep_ref, send_ref, pre_all, out_sum,
 ):
     step = pl.program_id(0)
@@ -187,12 +246,16 @@
     @pl.when(step < STEPS)
     def _():
         pair = jnp.concatenate([pair_ref[j] for j in range(BLK // PIECE)], axis=1).astype(f32)
-        loss_ref[...] = jnp.sum(pair[VARS : VARS + 3], axis=0, keepdims=True)
-        gap = pred_ref[...] - obs_ref[...]
+        loss = jnp.sum(pair[VARS : VARS + 3], axis=0, keepdims=True)
+        for j in range(BLK // PIECE):
+            at = lax.rem(2 * step + 1 + j, MEMBERS) * PIECE
+            loss_ref[:, pl.ds(pl.multiple_of(at, PIECE), PIECE)] = loss[:, j * PIECE : (j + 1) * PIECE]
+        area = jnp.concatenate([area0_ref[...], area1_ref[...]], axis=1)
+        gap = pred_ref[...] - jnp.concatenate([obs0_ref[...], obs1_ref[...]], axis=1)
         slope = gap * lax.rsqrt(gap * gap + smoothing * smoothing)
         g = (
             weight_ref[...]
-            * area_ref[...]
+            * area
             * (slope * (1.0 / MEMBERS) - (2.0 * pair_coef) * pair)
         ).astype(bf16)
         g_ref[...] = g
@@ -235,7 +298,8 @@
     later = lambda i: jnp.maximum(i - STEPS, 0)
     rows = pl.BlockSpec((BLK, D), lambda i, pos: (first(i), 0))
     columns = pl.BlockSpec((ROWS, BLK), lambda i, pos: (0, first(i)))
-    line = pl.BlockSpec((1, BLK), lambda i, pos: (0, first(i)))
+    left = lambda i, pos: (0, 2 * first(i) + 1)
+    right = lambda i, pos: (0, lax.rem(2 * first(i) + 2, MEMBERS))
     share = pl.BlockSpec((1, 4, 32, WIDE), lambda i, pos: (later(i), 0, 0, 0))
     return pl.pallas_call(
         weights_kernel,
@@ -245,15 +309,17 @@
             in_specs=[
                 pl.BlockSpec((BLK // PIECE, ROWS, PIECE), lambda i, pos: (first(i), 0, 0)),
                 columns,
-                columns,
-                line,
+                pl.BlockSpec((ROWS, PIECE), left),
+                pl.BlockSpec((ROWS, PIECE), right),
+                pl.BlockSpec((1, PIECE), left),
+                pl.BlockSpec((1, PIECE), right),
                 whole((ROWS, 1)),
                 whole((ROWS, D)),
                 rows,
                 rows,
                 pl.BlockSpec((CELLS, BLK), lambda i, pos: (0, lax.rem(pos[0] + later(i), 4))),
             ],
-            out_specs=[columns, rows, line, share, share],
+            out_specs=[columns, rows, whole((1, CELLS)), share, share],
             scratch_shapes=[pltpu.VMEM((CELLS, D), bf16), pltpu.VMEM((128, D), f32)],
         ),
         out_shape=[
@@ -268,12 +334,12 @@
             flops=3 * CELLS * D * D, bytes_accessed=14 << 20, transcendentals=0
         ),
         name="weights",
-    )(pos, pair, pred, observed, area, weight, w_out, deriv, hidden, normed)
+    )(pos, pair, pred, observed, observed, area, area, weight, w_out, deriv, hidden, normed)
 
 
 def latent_kernel(
-    nb_ref, g_ref, out_ref, pre_ref, mix_ref, gain_ref, normed_ref, inv_ref,
-    grad_ref, low_ref, high_ref, carry,
+    nb0_ref, nb1_ref, g_ref, out_ref, pre_ref, mix_ref, gain_ref, normed_ref, inv_ref,
+    grad_ref, low_ref, high_ref, carry, tail,
 ):
     step = pl.program_id(0)
     d_hidden = lax.dot_general(
@@ -286,60 +352,67 @@
     normed = normed_ref[...].astype(f32)
     mean = jnp.mean(normed * d_normed, axis=1, keepdims=True)
     d_combined = d_hidden + inv_ref[...] * (d_normed * gain - normed * (1.0 / gain) * mean)
-    first = pl.multiple_of(step * BLK, BLK)
-    base = lax.axis_index("space") * CELLS - HALO + first
-    edges = edge_matrix(nb_ref, base, 1.0 / NBRS)
-    row = lax.broadcasted_iota(jnp.int32, edges.shape, 0)
-    column = lax.broadcasted_iota(jnp.int32, edges.shape, 1)
-    edges = (edges + jnp.where(column == row + HALO, 1.0, 0.0)).astype(bf16)
-    spread = lax.dot_general(
-        edges, d_combined.astype(bf16), (((0,), (0,)), ((), ())), preferred_element_type=f32
-    )
+    d_combined = d_combined.astype(bf16)
+    start = lax.axis_index("space") * CELLS
+
+    def spread(neighbours, base, cells, width):
+        edges = edge_matrix(neighbours, base, width, 1.0 / NBRS)
+        row = lax.broadcasted_iota(jnp.int32, edges.shape, 0)
+        column = lax.broadcasted_iota(jnp.int32, edges.shape, 1)
+        edges = (edges + jnp.where(column == row + HALO, 1.0, 0.0)).astype(bf16)
+        return lax.dot_general(
+            edges, cells, (((0,), (0,)), ((), ())), preferred_element_type=f32
+        )
 
     @pl.when(step == 0)
     def _():
-        low_ref[...] = spread[0:HALO].astype(bf16)
-        grad_ref[0:HALO] = spread[HALO:BLK].astype(bf16)
+        last = spread(nb0_ref[...], start + CELLS - BLK, d_combined[0:HALO], BLK + HALO)
+        tail[...] = last[0:BLK]
+        high_ref[...] = last[BLK:].astype(bf16)
+        head = spread(nb1_ref[...], start - HALO, d_combined[HALO:], BLK + HALO)
+        low_ref[...] = head[0:HALO].astype(bf16)
+        carry[...] = head[HALO:]
 
     @pl.when(step > 0)
     def _():
-        grad_ref[pl.ds(pl.multiple_of(first - HALO, HALO), BLK)] = (
-            spread[0:BLK] + carry[...]
-        ).astype(bf16)
-
-    carry[...] = spread[BLK:]
+        first = pl.multiple_of((step - 1) * BLK, BLK)
+        neighbours = jnp.concatenate([nb0_ref[...], nb1_ref[...]], axis=1)
+        part = spread(neighbours, start + first, d_combined, BLK + 2 * HALO)
+        grad_ref[pl.ds(first, BLK)] = (part[0:BLK] + carry[...]).astype(bf16)
+        carry[...] = part[BLK:]
 
     @pl.when(step == STEPS - 1)
     def _():
-        grad_ref[CELLS - HALO :] = spread[BLK : BLK + HALO].astype(bf16)
-        high_ref[...] = spread[BLK + HALO :].astype(bf16)
+        grad_ref[CELLS - BLK :] = (carry[...] + tail[...]).astype(bf16)
 
 
 def latent_parts(neighbours, g, w_out, d_pre, w_mix, gain, normed, inverse):
-    rows = pl.BlockSpec((BLK, D), lambda i: (i, 0))
+    at = lambda i: lax.rem(i + STEPS - 1, STEPS)
+    rows = pl.BlockSpec((BLK, D), lambda i: (at(i), 0))
     rim = jax.ShapeDtypeStruct((HALO, D), bf16)
     return pl.pallas_call(
         latent_kernel,
         grid=(STEPS,),
         in_specs=[
-            pl.BlockSpec((NBRS, BLK), lambda i: (0, i)),
-            pl.BlockSpec((ROWS, BLK), lambda i: (0, i)),
+            pl.BlockSpec((NBRS, PIECE), lambda i: (0, 2 * at(i) + 1)),
+            pl.BlockSpec((NBRS, PIECE), lambda i: (0, lax.rem(2 * at(i) + 2, MEMBERS))),
+            pl.BlockSpec((ROWS, BLK), lambda i: (0, at(i))),
             whole((ROWS, D)),
             rows,
             whole((D, D)),
             whole((1, D)),
             rows,
-            pl.BlockSpec((BLK, 1), lambda i: (i, 0)),
+            pl.BlockSpec((BLK, 1), lambda i: (at(i), 0)),
         ],
         out_specs=[whole((CELLS, D)), whole((HALO, D)), whole((HALO, D))],
         out_shape=[jax.ShapeDtypeStruct((CELLS, D), bf16), rim, rim],
-        scratch_shapes=[pltpu.VMEM((BLK, D), f32)],
+        scratch_shapes=[pltpu.VMEM((BLK, D), f32), pltpu.VMEM((BLK, D), f32)],
         compiler_params=pltpu.CompilerParams(vmem_limit_bytes=VMEM_LIMIT),
         cost_estimate=pl.CostEstimate(
             flops=4 * CELLS * D * D, bytes_accessed=10 << 20, transcendentals=0
         ),
         name="latent",
-    )(neighbours, g, w_out, d_pre, w_mix, gain, normed, inverse)
+    )(neighbours, neighbours, g, w_out, d_pre, w_mix, gain, normed, inverse)
 
 
 def rim_kernel(grad_ref, low_ref, high_ref, out_ref):
@@ -390,13 +463,11 @@
     high = along(center[:HALO], "space", last_band)
     gain = norm_gain.reshape(1, D)
     area = cell_area.reshape(1, CELLS)
-    out_t = jnp.pad(w_out.T, ((0, ROWS - VARS), (0, 0)))
     observed = jnp.pad(observed, ((0, ROWS - VARS), (0, 0)))
     weight = jnp.pad(var_weight, (0, ROWS - VARS)).reshape(ROWS, 1)
 
-    normed, hidden, deriv, inverse, pred, pieces = forward(
-        neighbours, center, low, high, gain, w_mix, out_t
-    )
+    out_t, arrays = forward(neighbours, center, low, high, gain, w_mix, w_out)
+    normed, hidden, deriv, inverse, pred, pieces = arrays
     pieces = lax.all_to_all(pieces, "member", 0, 0, tiled=True)
     pairs = pair_terms(pieces, observed, area, weight)
     pairs = lax.all_to_all(pairs, "member", 0, 0, tiled=True)
@@ -404,25 +475,29 @@
         pos, pairs, pred, observed, area, weight, out_t, deriv, hidden, normed
     )
     got = along(send, "space", lambda i: i ^ 1)
+
+    def over_x(k):
+        return along(summed([keep[k], got[k]]).astype(bf16), "space", lambda i: (i + 8 * k) % 32)
+
+    arrived = [over_x(k) for k in (1, 2, 3)]
     grad, low_rim, high_rim = latent_parts(
         neighbours, g, out_t, d_pre, w_mix, gain, normed, inverse
     )
+    arrived, grad = lax.optimization_barrier((arrived, grad))
     from_above = along(low_rim, "space", last_band)
     from_below = along(high_rim, "space", next_band)
-    grad = add_rims(grad, from_below, from_above)
-
-    def over_x(k):
-        return along(summed([keep[k], got[k]]).astype(bf16), "space", lambda i: (i + 8 * k) % 32)
-
-    share = summed([keep[0], got[0]] + [over_x(k) for k in (1, 2, 3)]).astype(bf16)
+    share = summed([keep[0], got[0]] + arrived).astype(bf16)
 
     def over_z(k):
         return along(share[k], "space", lambda i: i // 8 * 8 + (i + 2 * k) % 8)
 
-    share = summed([share[0]] + [over_z(k) for k in (1, 2, 3)]).astype(bf16)
-    share = summed(
-        [share] + [along(share, "member", lambda i: (i + 2 * k) % 8) for k in (1, 2, 3)]
-    ).astype(bf16)
+    arrived = [over_z(k) for k in (1, 2, 3)]
+    arrived, from_above, from_below = lax.optimization_barrier((arrived, from_above, from_below))
+    share = summed([share[0]] + arrived).astype(bf16)
+    arrived = [along(share, "member", lambda i: (i + 2 * k) % 8) for k in (1, 2, 3)]
+    grad = add_rims(grad, from_below, from_above)
+    arrived, grad = lax.optimization_barrier((arrived, grad))
+    share = summed([share] + arrived).astype(bf16)
     totals = summed([share, along(share, "member", lambda i: i ^ 1)])
     grad_scale = 1.0 / math.sqrt(MEMBERS * CELLS * 32)
     return (

time: 146 us -> 137 us (0.938)
  the two profiles are of different devices: /device:TPU:2 before, /device:TPU:8 now
where the time goes in v2:
time: 137 us
  starting transfers between devices  43.6 us (32%)
  Pallas kernels  42.5 us (31%)
  waiting for transfers between devices  38.6 us (28%)
  local copies, waits for them, and re-layouts  6.61 us (5%)
  other arithmetic  4.51 us (3%)
    ppermute x15, starting transfers between devices, along(): lax.ppermute(value, axis, [pair for pair in pairs if pair[1] is not None])  26.5 us
    ppermute x15, waiting for transfers between devices, along(): lax.ppermute(value, axis, [pair for pair in pairs if pair[1] is not None])  19.6 us
    pallas_call x1, Pallas kernels, latent_parts(): pl.pallas_call(latent_kernel, grid=(STEPS,), in_specs=[pl.BlockSpec((NBRS...  11.9 us
    all_to_all x1, starting transfers between devices, shards(): pieces = lax.all_to_all(pieces, 'member', 0, 0, tiled=True)  11.5 us
    all_to_all x1, waiting for transfers between devices, shards(): pairs = lax.all_to_all(pairs, 'member', 0, 0, tiled=True)  11 us
    pallas_call x1, Pallas kernels, weight_parts(): pl.pallas_call(weights_kernel, grid_spec=pltpu.PrefetchScalarGridSpec(num...  10.9 us
    pallas_call x1, Pallas kernels, forward(): pl.pallas_call(interior_kernel, grid=(STEPS - 1,), in_specs=[edges_at(lam...  10.5 us
    all_to_all x1, waiting for transfers between devices, shards(): pieces = lax.all_to_all(pieces, 'member', 0, 0, tiled=True)  7.97 us
  transfers between devices with their start and end apart: 17, of which 8 were waited for; matrix products, arithmetic and copies ran while one was open for 4% of the time, Pallas kernels for 18%

profile of v2, /device:TPU:8, one launch (start us, length us, event | category | flops | bytes accessed | tf_op | source)
XLA Modules:
  0.0 136.6 jit_solution(459835317923734983)
XLA Ops:
  1.7 1.8 %collective-permute-start = (bf16[128,1024]{1,0:T(8,128)(2,1)S(1)}, bf16[128,1024]{1,0:T(8,128)(2,1)S(1)}, u32[]{:S(2)}, u32[]{:S(2)}) collective-permute-start(bf16[128,1024]{1,0:T(8,128)(2,1)S(1)} %get-tuple-element.76), channel_id=1, source_target_pairs={{0,1},{1,2},{2,3},{3,4},{4,5},{5,6},{6,7},{7,8},{8,9},{9,10},{10,1... | collective-permute-start | bytes 786440 | tf_op jit(solution)/shard_map/ppermute | solution.py:440
  4.8 1.8 %copy.19.out_ref = bf16[1024,100]{1,0:T(8,128)(2,1)} copy(bf16[1024,100]{0,1:T(8,128)(2,1)} %param.12) | data formatting | bytes 409600 | tf_op args[4]
  6.6 10.5 %interior.1 = (bf16[112,1024]{1,0:T(8,128)(2,1)}, bf16[1024,1024]{1,0:T(8,128)(2,1)}, bf16[1024,1024]{1,0:T(8,128)(2,1)}, bf16[1024,1024]{1,0:T(8,128)(2,1)}, f3...) custom-call(s32[4,1024]{1,0:T(4,128)} %nb1_ref.5, s32[4,1024]{1,0:T(4,128)} %nb1_ref.5, ...), custom_call_target="tpu_custom_call" | custom-call | flops 3221225472 | bytes 9437184 | tf_op jit(solution)/shard_map/interior/pallas_call | solution.py:144
  17.9 4.9 %rim_cells.1 = (bf16[1024,1024]{1,0:T(8,128)(2,1)}, bf16[1024,1024]{1,0:T(8,128)(2,1)}, bf16[1024,1024]{1,0:T(8,128)(2,1)}, f32[1024,1]{1,0:T(8,128)}, f32[112,1...) custom-call(s32[4,1024]{1,0:T(4,128)} %nb1_ref.5, ...), custom_call_target="tpu_custom_call", output_to_operand_aliasing={{0}: (9, {}), {1}: (10, {}), {2}: (11, {}), {3}: (12, {}), ... | custom-call | flops 1073741824 | bytes 3145728 | tf_op jit(solution)/shard_map/rim_cells/pallas_call | solution.py:161
  22.7 11.5 %all-to-all-start = ((bf16[8,112,128]{2,1,0:T(8,128)(2,1)}), bf16[8,112,128]{2,1,0:T(8,128)(2,1)S(1)}, u32[]{:S(2)}, u32[]{:S(2)}) async-start(bf16[8,112,128]{2,1,0:T(8,128)(2,1)} %get-tuple-element.45), calls=%async_computation | async-start | bytes 458752 | tf_op jit(solution)/shard_map/all_to_all | solution.py:471
  35.8 8.0 %all-to-all-done.pred_ref = bf16[8,112,128]{2,1,0:T(8,128)(2,1)S(1)} async-done(((bf16[8,112,128]{2,1,0:T(8,128)(2,1)}), bf16[8,112,128]{2,1,0:T(8,128)(2,1)S(1)}, u32[]{:S(2)}, u32[]{:S(2)}) %all-to-all-start) | async-done | bytes 229408 | tf_op jit(solution)/shard_map/all_to_all | solution.py:471
  44.5 2.4 %pairs.1 = bf16[8,112,128]{2,1,0:T(8,128)(2,1)} custom-call(bf16[8,112,128]{2,1,0:T(8,128)(2,1)} %copy-done.6, f32[112,1024]{1,0:T(8,128)} %pad.8.obs_ref.obs0_ref.obs1_ref, f32[1,1024]{1,0:T(1,128)} %bitcast.46, f32[112,1]{1,0:T(8,128)} %copy.20.weight_ref), custom_call_target="tpu_custom_call" | custom-call | flops 16777216 | bytes 1048576 | tf_op jit(solution)/shard_map/pairs/pallas_call | solution.py:229
  46.9 5.6 %all-to-all-start.1 = ((bf16[8,112,128]{2,1,0:T(8,128)(2,1)}), bf16[8,112,128]{2,1,0:T(8,128)(2,1)S(1)}, u32[]{:S(2)}, u32[]{:S(2)}) async-start(bf16[8,112,128]{2,1,0:T(8,128)(2,1)} %pairs.1), calls=%async_computation.1 | async-start | bytes 458752 | tf_op jit(solution)/shard_map/all_to_all | solution.py:473
  53.1 11.0 %all-to-all-done.1.pair_ref = bf16[8,112,128]{2,1,0:T(8,128)(2,1)S(1)} async-done(((bf16[8,112,128]{2,1,0:T(8,128)(2,1)}), bf16[8,112,128]{2,1,0:T(8,128)(2,1)S(1)}, u32[]{:S(2)}, u32[]{:S(2)}) %all-to-all-start.1) | async-done | bytes 229408 | tf_op jit(solution)/shard_map/all_to_all | solution.py:473
  64.9 10.9 %weights.1 = (bf16[112,1024]{1,0:T(8,128)(2,1)}, bf16[1024,1024]{1,0:T(8,128)(2,1)}, f32[1,1024]{1,0:T(1,128)}, bf16[4,4,32,1152]{3,2,1,0:T(8,128)(2,1)}, bf16[4,4,32,1152]{3,2,1,0:T(8,128)(2,1)}) custom-call(s32[3]{0:T(128)} %pad_add_fusion.pos_ref, bf16[8,112,128]{2,1,0:T(8,128)(2,1)} %copy-done.5, f32[112,1024]{1,0:T(8,128)} %get-tuple-element.46.pred_ref, ...), custom_call_target="tpu_custom_call" | custom-call | flops 3221225472 | bytes 14680064 | tf_op jit(solution)/shard_map/weights/pallas_call | solution.py:304
  75.9 3.0 %collective-permute-done.2 = bf16[4,4,32,1152]{3,2,1,0:T(8,128)(2,1)S(1)} collective-permute-done((bf16[4,4,32,1152]{3,2,1,0:T(8,128)(2,1)}, bf16[4,4,32,1152]{3,2,1,0:T(8,128)(2,1)S(1)}, u32[]{:S(2)}, u32[]{:S(2)}) %collective-permute-start.2) | collective-permute-done | bytes 1179680 | tf_op jit(solution)/shard_map/ppermute | solution.py:440
  80.3 3.6 %collective-permute-start.3 = (bf16[4,32,1152]{2,1,0:T(8,128)(2,1)S(1)}, bf16[4,32,1152]{2,1,0:T(8,128)(2,1)S(1)}, u32[]{:S(2)}, u32[]{:S(2)}) collective-permute-start(bf16[4,32,1152]{2,1,0:T(8,128)(2,1)S(1)} %get-tuple-element.74), channel_id=1, source_target_pairs={{0,8},{1,9},{2,10},{3,11},{4,12},{5,13},{6,14},{7,15},{8,16},{9,17... | collective-permute-start | bytes 884744 | tf_op jit(solution)/shard_map/ppermute | solution.py:440
  83.8 2.7 %collective-permute-start.4 = (bf16[4,32,1152]{2,1,0:T(8,128)(2,1)S(1)}, bf16[4,32,1152]{2,1,0:T(8,128)(2,1)S(1)}, u32[]{:S(2)}, u32[]{:S(2)}) collective-permute-start(bf16[4,32,1152]{2,1,0:T(8,128)(2,1)S(1)} %get-tuple-element.73), channel_id=1, source_target_pairs={{0,16},{1,17},{2,18},{3,19},{4,20},{5,21},{6,22},{7,23},{8,24},{9,... | collective-permute-start | bytes 884744 | tf_op jit(solution)/shard_map/ppermute | solution.py:440
  88.0 11.9 %latent.1 = (bf16[1024,1024]{1,0:T(8,128)(2,1)}, bf16[128,1024]{1,0:T(8,128)(2,1)}, bf16[128,1024]{1,0:T(8,128)(2,1)}) custom-call(s32[4,1024]{1,0:T(4,128)} %nb1_ref.5, s32[4,1024]{1,0:T(4,128)} %nb1_ref.5, bf16[112,1024]{1,0:T(8,128)(2,1)} %get-tuple-element.53.g_ref, bf16[112,1024]{1,0:T(8,128)(2,1)} %get-tuple-element.38.out_t_ref.out_ref, ...), custom_call_target="tpu_custom_call" | custom-call | flops 4294967296 | bytes 10485760 | tf_op jit(solution)/shard_map/latent/pallas_call | solution.py:393
  101.2 1.5 %collective-permute-start.9 = (bf16[128,1024]{1,0:T(8,128)(2,1)}, bf16[128,1024]{1,0:T(8,128)(2,1)S(1)}, u32[]{:S(2)}, u32[]{:S(2)}) collective-permute-start(bf16[128,1024]{1,0:T(8,128)(2,1)} %get-tuple-element.60), channel_id=1, source_target_pairs={{1,0},{2,1},{3,2},{4,3},{5,4},{6,5},{7,6},{8,7},{9,8},{10,9},{11,1... | collective-permute-start | bytes 786440 | tf_op jit(solution)/shard_map/ppermute | solution.py:440
  103.9 4.0 %collective-permute-start.6 = (bf16[32,1152]{1,0:T(8,128)(2,1)S(1)}, bf16[32,1152]{1,0:T(8,128)(2,1)S(1)}, u32[]{:S(2)}, u32[]{:S(2)}) collective-permute-start(bf16[32,1152]{1,0:T(8,128)(2,1)S(1)} %get-tuple-element.79), channel_id=1, source_target_pairs={{0,2},{1,3},{2,4},{3,5},{4,6},{5,7},{6,0},{7,1},{8,10},{9,11},{10,... | collective-permute-start | bytes 221192 | tf_op jit(solution)/shard_map/ppermute | solution.py:440
  108.8 1.5 %collective-permute-start.8 = (bf16[32,1152]{1,0:T(8,128)(2,1)S(1)}, bf16[32,1152]{1,0:T(8,128)(2,1)S(1)}, u32[]{:S(2)}, u32[]{:S(2)}) collective-permute-start(bf16[32,1152]{1,0:T(8,128)(2,1)S(1)} %get-tuple-element.77), channel_id=1, source_target_pairs={{0,6},{1,7},{2,0},{3,1},{4,2},{5,3},{6,4},{7,5},{8,14},{9,15},{10,... | collective-permute-start | bytes 221192 | tf_op jit(solution)/shard_map/ppermute | solution.py:440
  110.4 5.4 %collective-permute-done.6 = bf16[32,1152]{1,0:T(8,128)(2,1)S(1)} collective-permute-done((bf16[32,1152]{1,0:T(8,128)(2,1)S(1)}, bf16[32,1152]{1,0:T(8,128)(2,1)S(1)}, u32[]{:S(2)}, u32[]{:S(2)}) %collective-permute-start.6) | collective-permute-done | bytes 73760 | tf_op jit(solution)/shard_map/ppermute | solution.py:440
  115.7 2.2 %collective-permute-done.7 = bf16[32,1152]{1,0:T(8,128)(2,1)S(1)} collective-permute-done((bf16[32,1152]{1,0:T(8,128)(2,1)S(1)}, bf16[32,1152]{1,0:T(8,128)(2,1)S(1)}, u32[]{:S(2)}, u32[]{:S(2)}) %collective-permute-start.7) | collective-permute-done | bytes 73760 | tf_op jit(solution)/shard_map/ppermute | solution.py:440
  118.9 3.0 %collective-permute-start.12 = (bf16[32,1152]{1,0:T(8,128)(2,1)S(1)}, bf16[32,1152]{1,0:T(8,128)(2,1)S(1)}, u32[]{:S(2)}, u32[]{:S(2)}) collective-permute-start(bf16[32,1152]{1,0:T(8,128)(2,1)S(1)} %fusion.8), channel_id=1, source_target_pairs={{0,128},{32,160},{64,192},{96,224},{128,0},{160,32},{192,64},{224,... | collective-permute-start | bytes 221192 | tf_op jit(solution)/shard_map/ppermute | solution.py:440
  122.2 2.0 %rims.1 = bf16[1024,1024]{1,0:T(8,128)(2,1)} custom-call(bf16[1024,1024]{1,0:T(8,128)(2,1)} %get-tuple-element.65.grad_ref, bf16[128,1024]{1,0:T(8,128)(2,1)} %copy-done.3, bf16[128,1024]{1,0:T(8,128)(2,1)} %copy-done.4), custom_call_target="tpu_custom_call", output_to_operand_aliasing={{}: (0, {})} | custom-call | flops 262144 | bytes 1572864 | tf_op jit(solution)/shard_map/rims/pallas_call | solution.py:426
  124.8 1.5 %collective-permute-done.13 = bf16[32,1152]{1,0:T(8,128)(2,1)S(1)} collective-permute-done((bf16[32,1152]{1,0:T(8,128)(2,1)S(1)}, bf16[32,1152]{1,0:T(8,128)(2,1)S(1)}, u32[]{:S(2)}, u32[]{:S(2)}) %collective-permute-start.13) | collective-permute-done | bytes 73760 | tf_op jit(solution)/shard_map/ppermute | solution.py:440
  126.3 2.2 %collective-permute-start.14 = (bf16[32,1152]{1,0:T(8,128)(2,1)S(1)}, bf16[32,1152]{1,0:T(8,128)(2,1)S(1)}, u32[]{:S(2)}, u32[]{:S(2)}) collective-permute-start(bf16[32,1152]{1,0:T(8,128)(2,1)S(1)} %add_convert_fusion.3), channel_id=1, source_target_pairs={{0,32},{32,0},{64,96},{96,64},{128,160},{160,128},{192,224},{224,1... | collective-permute-start | bytes 221192 | tf_op jit(solution)/shard_map/ppermute | solution.py:440
  128.5 6.8 %collective-permute-done.14 = bf16[32,1152]{1,0:T(8,128)(2,1)S(1)} collective-permute-done((bf16[32,1152]{1,0:T(8,128)(2,1)S(1)}, bf16[32,1152]{1,0:T(8,128)(2,1)S(1)}, u32[]{:S(2)}, u32[]{:S(2)}) %collective-permute-start.14) | collective-permute-done | bytes 73760 | tf_op jit(solution)/shard_map/ppermute | solution.py:440
  (46 shorter events, 16.3 us)
Async XLA Ops:
  1.7 15.3 %collective-permute-start = (bf16[128,1024]{1,0:T(8,128)(2,1)S(1)}, bf16[128,1024]{1,0:T(8,128)(2,1)S(1)}, u32[]{:S(2)}, u32[]{:S(2)}) collective-permute-start(bf16[128,1024]{1,0:T(8,128)(2,1)S(1)} %get-tuple-element.76), channel_id=1, source_target_pairs={{0,1},{1,2},{2,3},{3,4},{4,5},{5,6},{6,7},{7,8},{8,9},{9,10},{10,1... | collective-permute-start | bytes 786440 | tf_op jit(solution)/shard_map/ppermute | solution.py:440
  3.5 13.6 %collective-permute-start.1 = (bf16[128,1024]{1,0:T(8,128)(2,1)S(1)}, bf16[128,1024]{1,0:T(8,128)(2,1)S(1)}, u32[]{:S(2)}, u32[]{:S(2)}) collective-permute-start(bf16[128,1024]{1,0:T(8,128)(2,1)S(1)} %get-tuple-element.75), channel_id=1, source_target_pairs={{1,0},{2,1},{3,2},{4,3},{5,4},{6,5},{7,6},{8,7},{9,8},{10,9},{11,1... | collective-permute-start | bytes 786440 | tf_op jit(solution)/shard_map/ppermute | solution.py:440
  17.1 0.7 copy-start.1
  17.1 0.8 copy-start.2
  17.8 16.4 %copy-start.7 = (f32[100]{0:T(128)S(1)}, f32[100]{0:T(128)}, u32[]{:S(2)}) copy-start(f32[100]{0:T(128)} %param.15) | copy-start | bytes 1204
  17.9 17.2 %copy-start = (f32[100,1024]{1,0:T(8,128)S(1)}, f32[100,1024]{1,0:T(8,128)}, u32[]{:S(2)}) copy-start(f32[100,1024]{1,0:T(8,128)} %param.13) | copy-start | bytes 1228804
  22.7 21.1 %all-to-all-start = ((bf16[8,112,128]{2,1,0:T(8,128)(2,1)}), bf16[8,112,128]{2,1,0:T(8,128)(2,1)S(1)}, u32[]{:S(2)}, u32[]{:S(2)}) async-start(bf16[8,112,128]{2,1,0:T(8,128)(2,1)} %get-tuple-element.45), calls=%async_computation | async-start | bytes 458752 | tf_op jit(solution)/shard_map/all_to_all | solution.py:471
  43.8 0.7 copy-start.6
  46.9 17.3 %all-to-all-start.1 = ((bf16[8,112,128]{2,1,0:T(8,128)(2,1)}), bf16[8,112,128]{2,1,0:T(8,128)(2,1)S(1)}, u32[]{:S(2)}, u32[]{:S(2)}) async-start(bf16[8,112,128]{2,1,0:T(8,128)(2,1)} %pairs.1), calls=%async_computation.1 | async-start | bytes 458752 | tf_op jit(solution)/shard_map/all_to_all | solution.py:473
  75.8 3.1 %collective-permute-start.2 = (bf16[4,4,32,1152]{3,2,1,0:T(8,128)(2,1)}, bf16[4,4,32,1152]{3,2,1,0:T(8,128)(2,1)S(1)}, u32[]{:S(2)}, u32[]{:S(2)}) collective-permute-start(bf16[4,4,32,1152]{3,2,1,0:T(8,128)(2,1)} %get-tuple-element.52), channel_id=1, source_target_pairs={{0,1},{1,0},{2,3},{3,2},{4,5},{5,4},{6,7},{7,6},{8,9},{9,8},{10,11... | collective-permute-start | bytes 3538952 | tf_op jit(solution)/shard_map/ppermute | solution.py:440
  80.3 22.4 %collective-permute-start.3 = (bf16[4,32,1152]{2,1,0:T(8,128)(2,1)S(1)}, bf16[4,32,1152]{2,1,0:T(8,128)(2,1)S(1)}, u32[]{:S(2)}, u32[]{:S(2)}) collective-permute-start(bf16[4,32,1152]{2,1,0:T(8,128)(2,1)S(1)} %get-tuple-element.74), channel_id=1, source_target_pairs={{0,8},{1,9},{2,10},{3,11},{4,12},{5,13},{6,14},{7,15},{8,16},{9,17... | collective-permute-start | bytes 884744 | tf_op jit(solution)/shard_map/ppermute | solution.py:440
  83.8 18.8 %collective-permute-start.4 = (bf16[4,32,1152]{2,1,0:T(8,128)(2,1)S(1)}, bf16[4,32,1152]{2,1,0:T(8,128)(2,1)S(1)}, u32[]{:S(2)}, u32[]{:S(2)}) collective-permute-start(bf16[4,32,1152]{2,1,0:T(8,128)(2,1)S(1)} %get-tuple-element.73), channel_id=1, source_target_pairs={{0,16},{1,17},{2,18},{3,19},{4,20},{5,21},{6,22},{7,23},{8,24},{9,... | collective-permute-start | bytes 884744 | tf_op jit(solution)/shard_map/ppermute | solution.py:440
  86.6 16.1 %collective-permute-start.5 = (bf16[4,32,1152]{2,1,0:T(8,128)(2,1)S(1)}, bf16[4,32,1152]{2,1,0:T(8,128)(2,1)S(1)}, u32[]{:S(2)}, u32[]{:S(2)}) collective-permute-start(bf16[4,32,1152]{2,1,0:T(8,128)(2,1)S(1)} %get-tuple-element.72), channel_id=1, source_target_pairs={{0,24},{1,25},{2,26},{3,27},{4,28},{5,29},{6,30},{7,31},{8,0},{9,1... | collective-permute-start | bytes 884744 | tf_op jit(solution)/shard_map/ppermute | solution.py:440
  99.9 10.5 %collective-permute-start.10 = (bf16[128,1024]{1,0:T(8,128)(2,1)}, bf16[128,1024]{1,0:T(8,128)(2,1)S(1)}, u32[]{:S(2)}, u32[]{:S(2)}) collective-permute-start(bf16[128,1024]{1,0:T(8,128)(2,1)} %get-tuple-element.61), channel_id=1, source_target_pairs={{0,1},{1,2},{2,3},{3,4},{4,5},{5,6},{6,7},{7,8},{8,9},{9,10},{10,1... | collective-permute-start | bytes 786440 | tf_op jit(solution)/shard_map/ppermute | solution.py:440
  101.2 9.2 %collective-permute-start.9 = (bf16[128,1024]{1,0:T(8,128)(2,1)}, bf16[128,1024]{1,0:T(8,128)(2,1)S(1)}, u32[]{:S(2)}, u32[]{:S(2)}) collective-permute-start(bf16[128,1024]{1,0:T(8,128)(2,1)} %get-tuple-element.60), channel_id=1, source_target_pairs={{1,0},{2,1},{3,2},{4,3},{5,4},{6,5},{7,6},{8,7},{9,8},{10,9},{11,1... | collective-permute-start | bytes 786440 | tf_op jit(solution)/shard_map/ppermute | solution.py:440
  103.9 11.8 %collective-permute-start.6 = (bf16[32,1152]{1,0:T(8,128)(2,1)S(1)}, bf16[32,1152]{1,0:T(8,128)(2,1)S(1)}, u32[]{:S(2)}, u32[]{:S(2)}) collective-permute-start(bf16[32,1152]{1,0:T(8,128)(2,1)S(1)} %get-tuple-element.79), channel_id=1, source_target_pairs={{0,2},{1,3},{2,4},{3,5},{4,6},{5,7},{6,0},{7,1},{8,10},{9,11},{10,... | collective-permute-start | bytes 221192 | tf_op jit(solution)/shard_map/ppermute | solution.py:440
  107.9 10.0 %collective-permute-start.7 = (bf16[32,1152]{1,0:T(8,128)(2,1)S(1)}, bf16[32,1152]{1,0:T(8,128)(2,1)S(1)}, u32[]{:S(2)}, u32[]{:S(2)}) collective-permute-start(bf16[32,1152]{1,0:T(8,128)(2,1)S(1)} %get-tuple-element.78), channel_id=1, source_target_pairs={{0,4},{1,5},{2,6},{3,7},{4,0},{5,1},{6,2},{7,3},{8,12},{9,13},{10,... | collective-permute-start | bytes 221192 | tf_op jit(solution)/shard_map/ppermute | solution.py:440
  108.8 9.1 %collective-permute-start.8 = (bf16[32,1152]{1,0:T(8,128)(2,1)S(1)}, bf16[32,1152]{1,0:T(8,128)(2,1)S(1)}, u32[]{:S(2)}, u32[]{:S(2)}) collective-permute-start(bf16[32,1152]{1,0:T(8,128)(2,1)S(1)} %get-tuple-element.77), channel_id=1, source_target_pairs={{0,6},{1,7},{2,0},{3,1},{4,2},{5,3},{6,4},{7,5},{8,14},{9,15},{10,... | collective-permute-start | bytes 221192 | tf_op jit(solution)/shard_map/ppermute | solution.py:440
  110.3 11.8 %copy-start.3 = (bf16[128,1024]{1,0:T(8,128)(2,1)}, bf16[128,1024]{1,0:T(8,128)(2,1)S(1)}, u32[]{:S(2)}) copy-start(bf16[128,1024]{1,0:T(8,128)(2,1)S(1)} %collective-permute-done.10.low_ref) | copy-start | bytes 786436
  110.3 11.8 %copy-start.4 = (bf16[128,1024]{1,0:T(8,128)(2,1)}, bf16[128,1024]{1,0:T(8,128)(2,1)S(1)}, u32[]{:S(2)}) copy-start(bf16[128,1024]{1,0:T(8,128)(2,1)S(1)} %collective-permute-done.9.high_ref) | copy-start | bytes 786436
  118.0 6.2 %collective-permute-start.11 = (bf16[32,1152]{1,0:T(8,128)(2,1)S(1)}, bf16[32,1152]{1,0:T(8,128)(2,1)S(1)}, u32[]{:S(2)}, u32[]{:S(2)}) collective-permute-start(bf16[32,1152]{1,0:T(8,128)(2,1)S(1)} %fusion.8), channel_id=1, source_target_pairs={{0,64},{32,96},{64,128},{96,160},{128,192},{160,224},{192,0},{224,... | collective-permute-start | bytes 221192 | tf_op jit(solution)/shard_map/ppermute | solution.py:440
  118.9 5.9 %collective-permute-start.12 = (bf16[32,1152]{1,0:T(8,128)(2,1)S(1)}, bf16[32,1152]{1,0:T(8,128)(2,1)S(1)}, u32[]{:S(2)}, u32[]{:S(2)}) collective-permute-start(bf16[32,1152]{1,0:T(8,128)(2,1)S(1)} %fusion.8), channel_id=1, source_target_pairs={{0,128},{32,160},{64,192},{96,224},{128,0},{160,32},{192,64},{224,... | collective-permute-start | bytes 221192 | tf_op jit(solution)/shard_map/ppermute | solution.py:440
  121.9 4.4 %collective-permute-start.13 = (bf16[32,1152]{1,0:T(8,128)(2,1)S(1)}, bf16[32,1152]{1,0:T(8,128)(2,1)S(1)}, u32[]{:S(2)}, u32[]{:S(2)}) collective-permute-start(bf16[32,1152]{1,0:T(8,128)(2,1)S(1)} %fusion.8), channel_id=1, source_target_pairs={{0,192},{32,224},{64,0},{96,32},{128,64},{160,96},{192,128},{224,1... | collective-permute-start | bytes 221192 | tf_op jit(solution)/shard_map/ppermute | solution.py:440
  126.3 9.0 %collective-permute-start.14 = (bf16[32,1152]{1,0:T(8,128)(2,1)S(1)}, bf16[32,1152]{1,0:T(8,128)(2,1)S(1)}, u32[]{:S(2)}, u32[]{:S(2)}) collective-permute-start(bf16[32,1152]{1,0:T(8,128)(2,1)S(1)} %add_convert_fusion.3), channel_id=1, source_target_pairs={{0,32},{32,0},{64,96},{96,64},{128,160},{160,128},{192,224},{224,1... | collective-permute-start | bytes 221192 | tf_op jit(solution)/shard_map/ppermute | solution.py:440
  (1 other events, 0.7 us)

commit v3 on v2

--- a/solution.py
+++ b/solution.py
@@ -29,27 +29,26 @@
 
 bf16 = jnp.bfloat16
 f32 = jnp.float32
-VMEM_LIMIT = 56 * 1024 * 1024
+VMEM_LIMIT = 24 * 1024 * 1024
 
 
 def whole(shape):
     return pl.BlockSpec(shape, lambda *_: (0,) * len(shape), pipeline_mode=pl.Buffered(1))
 
 
-def edge_matrix(neighbours, base, width, scale):
+def edge_matrix(neighbours, base, width):
     local = (neighbours - base).T
-    column = lax.broadcasted_iota(jnp.int32, (local.shape[0], width), 1)
-    count = jnp.zeros(column.shape, f32)
+    shape = (local.shape[0], width)
+    column = lax.broadcasted_iota(jnp.int32, shape, 1)
+    row = lax.broadcasted_iota(jnp.int32, shape, 0)
+    count = jnp.where(column == row + HALO, float(NBRS), 0.0)
     for k in range(NBRS):
-        count = count + jnp.where(column == local[:, k : k + 1], scale, 0.0)
-    return count
-
-
-def gathered(neighbours, base, window):
-    edges = edge_matrix(neighbours, base, window.shape[0], 1.0).astype(bf16)
-    total = jnp.dot(edges, window, preferred_element_type=f32)
-    own = window[HALO : HALO + edges.shape[0]].astype(f32)
-    return own + total * (1.0 / NBRS)
+        count = count + jnp.where(column == local[:, k : k + 1], 1.0, 0.0)
+    return count.astype(bf16)
+
+
+def gathered(edges, window):
+    return jnp.dot(edges, window, preferred_element_type=f32) * (1.0 / NBRS)
 
 
 def decode(combined, gain, mix, out_t, normed_ref, hidden_ref, deriv_ref, inv_ref, pred_ref, send_ref):
@@ -75,56 +74,106 @@
 
 
 def interior_kernel(
-    nb0_ref, nb1_ref, lat_ref, gain_ref, mix_ref, out_ref,
-    out_t_ref, normed_ref, hidden_ref, deriv_ref, inv_ref, pred_ref, send_ref,
+    nb0_ref, nb1_ref, gain_ref, out_ref, lat_hbm, mix_hbm,
+    out_t_ref, ends_ref, mix_out, edges_ref, normed_ref, hidden_ref, deriv_ref, inv_ref, pred_ref,
+    *refs,
 ):
+    send_ref, lat, mix, sems = refs
     step = pl.program_id(0)
+    copies = [
+        pltpu.make_async_copy(
+            lat_hbm.at[i * BLK : (i + 1) * BLK], lat.at[i * BLK : (i + 1) * BLK], sems.at[i]
+        )
+        for i in range(STEPS)
+    ] + [
+        pltpu.make_async_copy(
+            mix_hbm.at[i * BLK : (i + 1) * BLK], mix.at[i * BLK : (i + 1) * BLK], sems.at[STEPS + i]
+        )
+        for i in range(STEPS)
+    ]
+    first = pl.multiple_of(step * BLK, BLK)
 
     @pl.when(step == 0)
     def _():
+        for at in (0, 1, 4, 5, 6, 7, 2, 3):
+            copies[at].start()
         row = lax.broadcasted_iota(jnp.int32, (ROWS, VARS), 0)
         column = lax.broadcasted_iota(jnp.int32, (ROWS, VARS), 1)
         pick = jnp.where(row == column, 1.0, 0.0).astype(bf16)
         out_t_ref[...] = lax.dot_general(
-            pick, out_ref[...], (((1,), (1,)), ((), ())), preferred_element_type=f32
+            pick, out_ref[...], (((1,), (0,)), ((), ())), preferred_element_type=f32
         ).astype(bf16)
 
-    first = pl.multiple_of(step * BLK, BLK)
     neighbours = jnp.concatenate([nb0_ref[...], nb1_ref[...]], axis=1)
     base = lax.axis_index("space") * CELLS + first
-    combined = gathered(neighbours, base, lat_ref[pl.ds(first, BLK + 2 * HALO)])
+    edges = edge_matrix(neighbours, base, BLK + 2 * HALO)
+    edges_ref[...] = edges
+
+    @pl.when(step == 0)
+    def _():
+        for copy in copies[0:2] + copies[STEPS:]:
+            copy.wait()
+
+    @pl.when(step == 1)
+    def _():
+        copies[2].wait()
+
+    @pl.when(step == 2)
+    def _():
+        copies[3].wait()
+
+    combined = gathered(edges, lat[pl.ds(first, BLK + 2 * HALO)])
     decode(
-        combined, gain_ref[...], mix_ref[...], out_t_ref[...],
+        combined, gain_ref[...], mix[...], out_t_ref[...],
         normed_ref, hidden_ref, deriv_ref, inv_ref, pred_ref, send_ref,
     )
 
+    @pl.when(step == STEPS - 2)
+    def _():
+        ends_ref[0:BLK] = lat[0:BLK]
+        ends_ref[BLK:] = lat[CELLS - BLK :]
+        mix_out[...] = mix[...]
+
 
 def rim_cells_kernel(
-    nb0_ref, nb1_ref, last_ref, head_ref, low_ref, high_ref, gain_ref, mix_ref, out_t_ref,
+    nb0_ref, nb1_ref, ends_ref, near_ref, far_ref, gain_ref, mix_ref, out_t_ref,
     *refs,
 ):
-    start = lax.axis_index("space") * CELLS
-    window = jnp.concatenate([last_ref[...], high_ref[...]], axis=0)
-    last = gathered(nb0_ref[...], start + CELLS - BLK, window)
-    window = jnp.concatenate([low_ref[...], head_ref[...]], axis=0)
-    head = gathered(nb1_ref[...], start - HALO, window)
+    edges_ref, *refs = refs[len(refs) // 2 :]
+    space = lax.axis_index("space")
+    start = space * CELLS
+    first_core = lax.rem(space, 2) == 0
+    low = jnp.where(first_core, far_ref[...], near_ref[...])
+    high = jnp.where(first_core, near_ref[...], far_ref[...])
+    last_edges = edge_matrix(nb0_ref[...], start + CELLS - BLK, BLK + HALO)
+    head_edges = edge_matrix(nb1_ref[...], start - HALO, BLK + HALO)
+    edges_ref[0:HALO, 0 : BLK + HALO] = last_edges
+    edges_ref[HALO:, 0 : BLK + HALO] = head_edges
+    last = gathered(last_edges, jnp.concatenate([ends_ref[BLK:], high], axis=0))
+    head = gathered(head_edges, jnp.concatenate([low, ends_ref[0:BLK]], axis=0))
     combined = jnp.concatenate([last, head], axis=0)
-    decode(combined, gain_ref[...], mix_ref[...], out_t_ref[...], *refs[6:])
-
-
-def forward(neighbours, center, low, high, gain, w_mix, w_out):
+    decode(combined, gain_ref[...], mix_ref[...], out_t_ref[...], *refs)
+
+
+def in_hbm(value):
+    return pltpu.with_memory_space_constraint(value, pltpu.HBM)
+
+
+def forward(neighbours, center, near, far, gain, w_mix, w_out):
     shapes = [
-        jax.ShapeDtypeStruct((CELLS, D), bf16),
-        jax.ShapeDtypeStruct((CELLS, D), bf16),
-        jax.ShapeDtypeStruct((CELLS, D), bf16),
-        jax.ShapeDtypeStruct((CELLS, 1), f32),
-        jax.ShapeDtypeStruct((ROWS, CELLS), f32),
-        jax.ShapeDtypeStruct((MEMBERS, ROWS, PIECE), bf16),
+        pltpu.HBM((CELLS, BLK + 2 * HALO), bf16),
+        pltpu.HBM((CELLS, D), bf16),
+        pltpu.HBM((CELLS, D), bf16),
+        pltpu.HBM((CELLS, D), bf16),
+        pltpu.HBM((CELLS, 1), f32),
+        pltpu.HBM((ROWS, CELLS), f32),
+        pltpu.HBM((MEMBERS, ROWS, PIECE), bf16),
     ]
 
     def blocks(at):
         rows = pl.BlockSpec((BLK, D), lambda i: (at(i), 0))
         return [
+            pl.BlockSpec((BLK, BLK + 2 * HALO), lambda i: (at(i), 0)),
             rows,
             rows,
             rows,
@@ -141,46 +190,56 @@
             flops=steps * 4 * BLK * D * D, bytes_accessed=steps * 3 << 20, transcendentals=steps * BLK * D
         )
 
-    out_t, *arrays = pl.pallas_call(
+    neighbours, gain = in_hbm(neighbours), in_hbm(gain)
+    out_t, ends, mix, *arrays = pl.pallas_call(
         interior_kernel,
         grid=(STEPS - 1,),
         in_specs=[
             edges_at(lambda i: 2 * i + 1),
             edges_at(lambda i: 2 * i + 2),
-            whole((CELLS, D)),
             whole((1, D)),
-            whole((D, D)),
-            whole((D, VARS)),
+            whole((VARS, D)),
+            pl.BlockSpec(memory_space=pltpu.HBM),
+            pl.BlockSpec(memory_space=pltpu.HBM),
         ],
-        out_specs=[whole((ROWS, D))] + blocks(lambda i: i),
-        out_shape=[jax.ShapeDtypeStruct((ROWS, D), bf16)] + shapes,
+        out_specs=[whole((ROWS, D)), whole((2 * BLK, D)), whole((D, D))] + blocks(lambda i: i),
+        out_shape=[
+            jax.ShapeDtypeStruct((ROWS, D), bf16),
+            jax.ShapeDtypeStruct((2 * BLK, D), bf16),
+            jax.ShapeDtypeStruct((D, D), bf16),
+        ]
+        + shapes,
+        scratch_shapes=[
+            pltpu.VMEM((CELLS, D), bf16),
+            pltpu.VMEM((D, D), bf16),
+            pltpu.SemaphoreType.DMA((2 * STEPS,)),
+        ],
         compiler_params=pltpu.CompilerParams(vmem_limit_bytes=VMEM_LIMIT),
         cost_estimate=cost(STEPS - 1),
         name="interior",
-    )(neighbours, neighbours, center, gain, w_mix, w_out)
+    )(neighbours, neighbours, gain, in_hbm(w_out), in_hbm(center), in_hbm(w_mix))
     arrays = pl.pallas_call(
         rim_cells_kernel,
         grid=(1,),
         in_specs=[
             edges_at(lambda i: MEMBERS - 1),
             edges_at(lambda i: 0),
-            pl.BlockSpec((BLK, D), lambda i: (STEPS - 1, 0)),
-            pl.BlockSpec((BLK, D), lambda i: (0, 0)),
+            whole((2 * BLK, D)),
             whole((HALO, D)),
             whole((HALO, D)),
             whole((1, D)),
             whole((D, D)),
             whole((ROWS, D)),
         ]
-        + [pl.BlockSpec(memory_space=pl.ANY)] * len(shapes),
+        + [pl.BlockSpec(memory_space=pltpu.HBM)] * len(shapes),
         out_specs=blocks(lambda i: STEPS - 1),
         out_shape=shapes,
-        input_output_aliases={9 + i: i for i in range(len(shapes))},
+        input_output_aliases={8 + i: i for i in range(len(shapes))},
         compiler_params=pltpu.CompilerParams(vmem_limit_bytes=VMEM_LIMIT),
         cost_estimate=cost(1),
         name="rim_cells",
-    )(neighbours, neighbours, center, center, low, high, gain, w_mix, out_t, *arrays)
-    return out_t, arrays
+    )(neighbours, neighbours, ends, near, far, gain, mix, out_t, *arrays)
+    return out_t, mix, arrays
 
 
 def pair_kernel(pred_ref, obs_ref, area_ref, weight_ref, back_ref):
@@ -228,13 +287,13 @@
 def pair_terms(preds, observed, area, weight):
     return pl.pallas_call(
         pair_kernel,
-        out_shape=jax.ShapeDtypeStruct((MEMBERS, ROWS, PIECE), bf16),
+        out_shape=pltpu.HBM((MEMBERS, ROWS, PIECE), bf16),
         cost_estimate=pl.CostEstimate(
             flops=1 << 24, bytes_accessed=1 << 20, transcendentals=1 << 20
         ),
         compiler_params=pltpu.CompilerParams(vmem_limit_bytes=VMEM_LIMIT),
         name="pairs",
-    )(preds, observed, area, weight)
+    )(preds, in_hbm(observed), area, weight)
 
 
 def weights_kernel(
@@ -334,12 +393,15 @@
             flops=3 * CELLS * D * D, bytes_accessed=14 << 20, transcendentals=0
         ),
         name="weights",
-    )(pos, pair, pred, observed, observed, area, area, weight, w_out, deriv, hidden, normed)
+    )(
+        pos, pair, in_hbm(pred), in_hbm(observed), in_hbm(observed), area, area, weight, w_out,
+        in_hbm(deriv), in_hbm(hidden), in_hbm(normed),
+    )
 
 
 def latent_kernel(
-    nb0_ref, nb1_ref, g_ref, out_ref, pre_ref, mix_ref, gain_ref, normed_ref, inv_ref,
-    grad_ref, low_ref, high_ref, carry, tail,
+    edges_ref, g_ref, out_ref, pre_ref, mix_ref, gain_ref, normed_ref, inv_ref,
+    grad_ref, near_ref, far_ref, carry, tail,
 ):
     step = pl.program_id(0)
     d_hidden = lax.dot_general(
@@ -353,31 +415,27 @@
     mean = jnp.mean(normed * d_normed, axis=1, keepdims=True)
     d_combined = d_hidden + inv_ref[...] * (d_normed * gain - normed * (1.0 / gain) * mean)
     d_combined = d_combined.astype(bf16)
-    start = lax.axis_index("space") * CELLS
-
-    def spread(neighbours, base, cells, width):
-        edges = edge_matrix(neighbours, base, width, 1.0 / NBRS)
-        row = lax.broadcasted_iota(jnp.int32, edges.shape, 0)
-        column = lax.broadcasted_iota(jnp.int32, edges.shape, 1)
-        edges = (edges + jnp.where(column == row + HALO, 1.0, 0.0)).astype(bf16)
-        return lax.dot_general(
+
+    def spread(edges, cells):
+        return (1.0 / NBRS) * lax.dot_general(
             edges, cells, (((0,), (0,)), ((), ())), preferred_element_type=f32
         )
 
     @pl.when(step == 0)
     def _():
-        last = spread(nb0_ref[...], start + CELLS - BLK, d_combined[0:HALO], BLK + HALO)
+        last = spread(edges_ref[0:HALO, 0 : BLK + HALO], d_combined[0:HALO])
         tail[...] = last[0:BLK]
-        high_ref[...] = last[BLK:].astype(bf16)
-        head = spread(nb1_ref[...], start - HALO, d_combined[HALO:], BLK + HALO)
-        low_ref[...] = head[0:HALO].astype(bf16)
+        head = spread(edges_ref[HALO:, 0 : BLK + HALO], d_combined[HALO:])
         carry[...] = head[HALO:]
+        high, low = last[BLK:].astype(bf16), head[0:HALO].astype(bf16)
+        first_core = lax.rem(lax.axis_index("space"), 2) == 0
+        near_ref[...] = jnp.where(first_core, high, low)
+        far_ref[...] = jnp.where(first_core, low, high)
 
     @pl.when(step > 0)
     def _():
         first = pl.multiple_of((step - 1) * BLK, BLK)
-        neighbours = jnp.concatenate([nb0_ref[...], nb1_ref[...]], axis=1)
-        part = spread(neighbours, start + first, d_combined, BLK + 2 * HALO)
+        part = spread(edges_ref[...], d_combined)
         grad_ref[pl.ds(first, BLK)] = (part[0:BLK] + carry[...]).astype(bf16)
         carry[...] = part[BLK:]
 
@@ -386,7 +444,7 @@
         grad_ref[CELLS - BLK :] = (carry[...] + tail[...]).astype(bf16)
 
 
-def latent_parts(neighbours, g, w_out, d_pre, w_mix, gain, normed, inverse):
+def latent_parts(edges, g, w_out, d_pre, w_mix, gain, normed, inverse):
     at = lambda i: lax.rem(i + STEPS - 1, STEPS)
     rows = pl.BlockSpec((BLK, D), lambda i: (at(i), 0))
     rim = jax.ShapeDtypeStruct((HALO, D), bf16)
@@ -394,8 +452,7 @@
         latent_kernel,
         grid=(STEPS,),
         in_specs=[
-            pl.BlockSpec((NBRS, PIECE), lambda i: (0, 2 * at(i) + 1)),
-            pl.BlockSpec((NBRS, PIECE), lambda i: (0, lax.rem(2 * at(i) + 2, MEMBERS))),
+            pl.BlockSpec((BLK, BLK + 2 * HALO), lambda i: (at(i), 0)),
             pl.BlockSpec((ROWS, BLK), lambda i: (0, at(i))),
             whole((ROWS, D)),
             rows,
@@ -412,16 +469,16 @@
             flops=4 * CELLS * D * D, bytes_accessed=10 << 20, transcendentals=0
         ),
         name="latent",
-    )(neighbours, neighbours, g, w_out, d_pre, w_mix, gain, normed, inverse)
-
-
-def rim_kernel(grad_ref, low_ref, high_ref, out_ref):
-    step = pl.program_id(0)
-    other = jnp.where(step == 0, low_ref[...], high_ref[...])
+    )(edges, g, w_out, d_pre, w_mix, gain, normed, inverse)
+
+
+def rim_kernel(grad_ref, near_ref, far_ref, out_ref):
+    first_core = lax.rem(lax.axis_index("space"), 2) == 0
+    other = jnp.where((pl.program_id(0) == 0) == first_core, far_ref[...], near_ref[...])
     out_ref[...] = (grad_ref[...].astype(f32) + other.astype(f32)).astype(bf16)
 
 
-def add_rims(grad, low, high):
+def add_rims(grad, near, far):
     rim = pl.BlockSpec((HALO, D), lambda i: (i * (CELLS // HALO - 1), 0))
     return pl.pallas_call(
         rim_kernel,
@@ -430,9 +487,10 @@
         out_specs=rim,
         out_shape=jax.ShapeDtypeStruct((CELLS, D), bf16),
         input_output_aliases={0: 0},
+        compiler_params=pltpu.CompilerParams(vmem_limit_bytes=VMEM_LIMIT),
         cost_estimate=pl.CostEstimate(flops=1 << 18, bytes_accessed=3 << 19, transcendentals=0),
         name="rims",
-    )(grad, low, high)
+    )(grad, near, far)
 
 
 def along(value, axis, move):
@@ -440,12 +498,13 @@
     return lax.ppermute(value, axis, [pair for pair in pairs if pair[1] is not None])
 
 
-def next_band(i):
-    return i + 1 if i < 31 else None
-
-
-def last_band(i):
-    return i - 1 if i > 0 else None
+def other_core(i):
+    return i ^ 1
+
+
+def other_chip(i):
+    there = i + 1 if i % 2 else i - 1
+    return there if 0 <= there < 32 else None
 
 
 def summed(parts):
@@ -459,43 +518,43 @@
     space = lax.axis_index("space")
     pos = jnp.stack([space // 8, space // 2 % 4, space % 2]).astype(jnp.int32)
     center = latent[0]
-    low = along(center[CELLS - HALO :], "space", next_band)
-    high = along(center[:HALO], "space", last_band)
+    first_core = space % 2 == 0
+    head, tail = center[:HALO], center[CELLS - HALO :]
+    far = along(jnp.where(first_core, head, tail), "space", other_chip)
+    near = along(jnp.where(first_core, tail, head), "space", other_core)
     gain = norm_gain.reshape(1, D)
     area = cell_area.reshape(1, CELLS)
     observed = jnp.pad(observed, ((0, ROWS - VARS), (0, 0)))
     weight = jnp.pad(var_weight, (0, ROWS - VARS)).reshape(ROWS, 1)
 
-    out_t, arrays = forward(neighbours, center, low, high, gain, w_mix, w_out)
-    normed, hidden, deriv, inverse, pred, pieces = arrays
+    out_t, mix, arrays = forward(neighbours, center, near, far, gain, w_mix, w_out.T)
+    edges, normed, hidden, deriv, inverse, pred, pieces = arrays
     pieces = lax.all_to_all(pieces, "member", 0, 0, tiled=True)
     pairs = pair_terms(pieces, observed, area, weight)
     pairs = lax.all_to_all(pairs, "member", 0, 0, tiled=True)
     g, d_pre, losses, keep, send = weight_parts(
         pos, pairs, pred, observed, area, weight, out_t, deriv, hidden, normed
     )
-    got = along(send, "space", lambda i: i ^ 1)
+    got = along(send, "space", other_core)
 
     def over_x(k):
         return along(summed([keep[k], got[k]]).astype(bf16), "space", lambda i: (i + 8 * k) % 32)
 
     arrived = [over_x(k) for k in (1, 2, 3)]
-    grad, low_rim, high_rim = latent_parts(
-        neighbours, g, out_t, d_pre, w_mix, gain, normed, inverse
-    )
+    grad, near, far = latent_parts(edges, g, out_t, d_pre, w_mix, gain, normed, inverse)
     arrived, grad = lax.optimization_barrier((arrived, grad))
-    from_above = along(low_rim, "space", last_band)
-    from_below = along(high_rim, "space", next_band)
+    far = along(far, "space", other_chip)
+    near = along(near, "space", other_core)
     share = summed([keep[0], got[0]] + arrived).astype(bf16)
 
     def over_z(k):
         return along(share[k], "space", lambda i: i // 8 * 8 + (i + 2 * k) % 8)
 
     arrived = [over_z(k) for k in (1, 2, 3)]
-    arrived, from_above, from_below = lax.optimization_barrier((arrived, from_above, from_below))
+    arrived, near, far = lax.optimization_barrier((arrived, near, far))
     share = summed([share[0]] + arrived).astype(bf16)
     arrived = [along(share, "member", lambda i: (i + 2 * k) % 8) for k in (1, 2, 3)]
-    grad = add_rims(grad, from_below, from_above)
+    grad = add_rims(grad, near, far)
     arrived, grad = lax.optimization_barrier((arrived, grad))
     share = summed([share] + arrived).astype(bf16)
     totals = summed([share, along(share, "member", lambda i: i ^ 1)])

time: 137 us -> 121 us (0.88)
  the two profiles are of different devices: /device:TPU:8 before, /device:TPU:2 now
where the time goes in v3:
time: 121 us; the launch traced here: 120 us
  starting transfers between devices  39.6 us (33%)
  waiting for transfers between devices  38.8 us (32%)
  Pallas kernels  36.5 us (30%)
  other arithmetic  2.92 us (2%)
    ppermute x15, starting transfers between devices, along(): lax.ppermute(value, axis, [pair for pair in pairs if pair[1] is not None])  27.8 us
    ppermute x15, waiting for transfers between devices, along(): lax.ppermute(value, axis, [pair for pair in pairs if pair[1] is not None])  17.7 us
    pallas_call x1, Pallas kernels, forward(): pl.pallas_call(interior_kernel, grid=(STEPS - 1,), in_specs=[edges_at(lam...  11.4 us
    all_to_all x1, waiting for transfers between devices, shards(): pairs = lax.all_to_all(pairs, 'member', 0, 0, tiled=True)  10.9 us
    all_to_all x1, waiting for transfers between devices, shards(): pieces = lax.all_to_all(pieces, 'member', 0, 0, tiled=True)  10.2 us
    pallas_call x1, Pallas kernels, weight_parts(): pl.pallas_call(weights_kernel, grid_spec=pltpu.PrefetchScalarGridSpec(num...  9.59 us
    all_to_all x1, starting transfers between devices, shards(): pieces = lax.all_to_all(pieces, 'member', 0, 0, tiled=True)  8.39 us
    pallas_call x1, Pallas kernels, latent_parts(): pl.pallas_call(latent_kernel, grid=(STEPS,), in_specs=[pl.BlockSpec((BLK,...  7.72 us
  transfers between devices with their start and end apart: 17, of which 9 were waited for; matrix products, arithmetic and copies ran while one was open for 1% of the time, Pallas kernels for 17%

profile of v3, /device:TPU:2, one launch (start us, length us, event | category | flops | bytes accessed | tf_op | source)
XLA Modules:
  0.0 119.7 jit_solution(4466096262250801333)
XLA Ops:
  0.6 1.1 select_bitcast_fusion
  1.8 6.6 %collective-permute-start.1 = (bf16[128,1024]{1,0:T(8,128)(2,1)S(1)}, bf16[128,1024]{1,0:T(8,128)(2,1)S(1)}, u32[]{:S(2)}, u32[]{:S(2)}) collective-permute-start(bf16[128,1024]{1,0:T(8,128)(2,1)S(1)} %get-tuple-element.83), channel_id=1, source_target_pairs={{1,2},{2,1},{3,4},{4,3},{5,6},{6,5},{7,8},{8,7},{9,10},{10,9},{11,... | collective-permute-start | bytes 786440 | tf_op jit(solution)/shard_map/ppermute | solution.py:498
  8.4 11.4 %interior.1 = (bf16[112,1024]{1,0:T(8,128)(2,1)S(1)}, bf16[512,1024]{1,0:T(8,128)(2,1)S(1)}, bf16[1024,1024]{1,0:T(8,128)(2,1)S(1)}, bf16[1024,512]{1,0:T(8,128)...) custom-call(s32[4,1024]{1,0:T(4,128)} %nb1_ref.3, ...), custom_call_target="tpu_custom_call" | custom-call | flops 3221225472 | bytes 9437184 | tf_op jit(solution)/shard_map/interior/pallas_call | solution.py:194
  19.9 3.6 %rim_cells.1 = (bf16[1024,512]{1,0:T(8,128)(2,1)}, bf16[1024,1024]{1,0:T(8,128)(2,1)}, bf16[1024,1024]{1,0:T(8,128)(2,1)}, bf16[1024,1024]{1,0:T(8,128)(2,1)}, f...) custom-call(s32[4,1024]{1,0:T(4,128)} %nb1_ref.3, ...), custom_call_target="tpu_custom_call", output_to_operand_aliasing={{0}: (8, {}), {1}: (9, {}), {2}: (10, {}), {3}: (11, {}), {... | custom-call | flops 1073741824 | bytes 3145728 | tf_op jit(solution)/shard_map/rim_cells/pallas_call | solution.py:221
  23.5 8.4 %all-to-all-start = ((bf16[8,112,128]{2,1,0:T(8,128)(2,1)}), bf16[8,112,128]{2,1,0:T(8,128)(2,1)S(1)}, u32[]{:S(2)}, u32[]{:S(2)}) async-start(bf16[8,112,128]{2,1,0:T(8,128)(2,1)} %get-tuple-element.52), calls=%async_computation | async-start | bytes 458752 | tf_op jit(solution)/shard_map/all_to_all | solution.py:532
  32.8 10.2 %all-to-all-done.pred_ref = bf16[8,112,128]{2,1,0:T(8,128)(2,1)S(1)} async-done(((bf16[8,112,128]{2,1,0:T(8,128)(2,1)}), bf16[8,112,128]{2,1,0:T(8,128)(2,1)S(1)}, u32[]{:S(2)}, u32[]{:S(2)}) %all-to-all-start) | async-done | bytes 229408 | tf_op jit(solution)/shard_map/all_to_all | solution.py:532
  43.0 2.4 %pairs.1 = bf16[8,112,128]{2,1,0:T(8,128)(2,1)} custom-call(bf16[8,112,128]{2,1,0:T(8,128)(2,1)S(1)} %all-to-all-done.pred_ref, f32[112,1024]{1,0:T(8,128)} %pad.8.obs_ref.obs0_ref.obs1_ref, f32[1,1024]{1,0:T(1,128)S(1)} %bitcast.43, f32[112,1]{1,0:T(8,128)S(1)} %copy.20.weight_ref), custom_call_target="tpu_custom_call" | custom-call | flops 16777216 | bytes 1048576 | tf_op jit(solution)/shard_map/pairs/pallas_call | solution.py:288
  45.3 3.4 %all-to-all-start.1 = ((bf16[8,112,128]{2,1,0:T(8,128)(2,1)}), bf16[8,112,128]{2,1,0:T(8,128)(2,1)S(1)}, u32[]{:S(2)}, u32[]{:S(2)}) async-start(bf16[8,112,128]{2,1,0:T(8,128)(2,1)} %pairs.1), calls=%async_computation.1 | async-start | bytes 458752 | tf_op jit(solution)/shard_map/all_to_all | solution.py:534
  48.9 10.9 %all-to-all-done.1.pair_ref = bf16[8,112,128]{2,1,0:T(8,128)(2,1)S(1)} async-done(((bf16[8,112,128]{2,1,0:T(8,128)(2,1)}), bf16[8,112,128]{2,1,0:T(8,128)(2,1)S(1)}, u32[]{:S(2)}, u32[]{:S(2)}) %all-to-all-start.1) | async-done | bytes 229408 | tf_op jit(solution)/shard_map/all_to_all | solution.py:534
  59.8 9.6 %weights.1 = (bf16[112,1024]{1,0:T(8,128)(2,1)S(1)}, bf16[1024,1024]{1,0:T(8,128)(2,1)S(1)}, f32[1,1024]{1,0:T(1,128)}, bf16[4,4,32,1152]{3,2,1,0:T(8,128)(2,1)S(1)}, bf16[4,4,32,1152]{3,2,1,0:T(8,128)(2,1)S(1)}) custom-call(s32[3]{0:T(128)S(1)} %pad_add_fusion.pos_ref, bf16[8,112,128]{2,1,0:T(8,128)(2,1)S(1)} %all-to-all-done.1.pair_ref, ...), custom_call_target="tpu_custom_call" | custom-call | flops 3221225472 | bytes 14680064 | tf_op jit(solution)/shard_map/weights/pallas_call | solution.py:363
  69.5 2.8 %collective-permute-done.2 = bf16[4,4,32,1152]{3,2,1,0:T(8,128)(2,1)S(1)} collective-permute-done((bf16[4,4,32,1152]{3,2,1,0:T(8,128)(2,1)S(1)}, bf16[4,4,32,1152]{3,2,1,0:T(8,128)(2,1)S(1)}, u32[]{:S(2)}, u32[]{:S(2)}) %collective-permute-start.2) | collective-permute-done | bytes 1179680 | tf_op jit(solution)/shard_map/ppermute | solution.py:498
  72.6 1.6 %collective-permute-start.3 = (bf16[4,32,1152]{2,1,0:T(8,128)(2,1)S(1)}, bf16[4,32,1152]{2,1,0:T(8,128)(2,1)S(1)}, u32[]{:S(2)}, u32[]{:S(2)}) collective-permute-start(bf16[4,32,1152]{2,1,0:T(8,128)(2,1)S(1)} %get-tuple-element.82), channel_id=1, source_target_pairs={{0,8},{1,9},{2,10},{3,11},{4,12},{5,13},{6,14},{7,15},{8,16},{9,17... | collective-permute-start | bytes 884744 | tf_op jit(solution)/shard_map/ppermute | solution.py:498
  74.1 1.1 collective-permute-start.4
  75.2 2.5 %collective-permute-start.5 = (bf16[4,32,1152]{2,1,0:T(8,128)(2,1)S(1)}, bf16[4,32,1152]{2,1,0:T(8,128)(2,1)S(1)}, u32[]{:S(2)}, u32[]{:S(2)}) collective-permute-start(bf16[4,32,1152]{2,1,0:T(8,128)(2,1)S(1)} %get-tuple-element.80), channel_id=1, source_target_pairs={{0,24},{1,25},{2,26},{3,27},{4,28},{5,29},{6,30},{7,31},{8,0},{9,1... | collective-permute-start | bytes 884744 | tf_op jit(solution)/shard_map/ppermute | solution.py:498
  77.7 7.7 %latent.1 = (bf16[1024,1024]{1,0:T(8,128)(2,1)}, bf16[128,1024]{1,0:T(8,128)(2,1)S(1)}, bf16[128,1024]{1,0:T(8,128)(2,1)S(1)}) custom-call(bf16[1024,512]{1,0:T(8,128)(2,1)S(1)} %copy-done.1, bf16[112,1024]{1,0:T(8,128)(2,1)S(1)} %get-tuple-element.61.g_ref, bf16[112,1024]{1,0:T(8,128)(2,1)S(1)} %get-tuple-element.44.out_t_ref.out_ref, ...), custom_call_target="tpu_custom_call" | custom-call | flops 4294967296 | bytes 10485760 | tf_op jit(solution)/shard_map/latent/pallas_call | solution.py:451
  85.5 6.1 %collective-permute-start.10 = (bf16[128,1024]{1,0:T(8,128)(2,1)S(1)}, bf16[128,1024]{1,0:T(8,128)(2,1)S(1)}, u32[]{:S(2)}, u32[]{:S(2)}) collective-permute-start(bf16[128,1024]{1,0:T(8,128)(2,1)S(1)} %get-tuple-element.69), channel_id=1, source_target_pairs={{1,2},{2,1},{3,4},{4,3},{5,6},{6,5},{7,8},{8,7},{9,10},{10,9},{11,... | collective-permute-start | bytes 786440 | tf_op jit(solution)/shard_map/ppermute | solution.py:498
  91.9 1.1 collective-permute-start.6
  92.9 1.5 %collective-permute-start.7 = (bf16[32,1152]{1,0:T(8,128)(2,1)S(1)}, bf16[32,1152]{1,0:T(8,128)(2,1)S(1)}, u32[]{:S(2)}, u32[]{:S(2)}) collective-permute-start(bf16[32,1152]{1,0:T(8,128)(2,1)S(1)} %get-tuple-element.86), channel_id=1, source_target_pairs={{0,4},{1,5},{2,6},{3,7},{4,0},{5,1},{6,2},{7,3},{8,12},{9,13},{10,... | collective-permute-start | bytes 221192 | tf_op jit(solution)/shard_map/ppermute | solution.py:498
  94.4 2.6 %collective-permute-start.8 = (bf16[32,1152]{1,0:T(8,128)(2,1)S(1)}, bf16[32,1152]{1,0:T(8,128)(2,1)S(1)}, u32[]{:S(2)}, u32[]{:S(2)}) collective-permute-start(bf16[32,1152]{1,0:T(8,128)(2,1)S(1)} %get-tuple-element.85), channel_id=1, source_target_pairs={{0,6},{1,7},{2,0},{3,1},{4,2},{5,3},{6,4},{7,5},{8,14},{9,15},{10,... | collective-permute-start | bytes 221192 | tf_op jit(solution)/shard_map/ppermute | solution.py:498
  97.8 2.0 %collective-permute-done.6 = bf16[32,1152]{1,0:T(8,128)(2,1)S(1)} collective-permute-done((bf16[32,1152]{1,0:T(8,128)(2,1)S(1)}, bf16[32,1152]{1,0:T(8,128)(2,1)S(1)}, u32[]{:S(2)}, u32[]{:S(2)}) %collective-permute-start.6) | collective-permute-done | bytes 73760 | tf_op jit(solution)/shard_map/ppermute | solution.py:498
  99.8 2.5 %collective-permute-done.7 = bf16[32,1152]{1,0:T(8,128)(2,1)S(1)} collective-permute-done((bf16[32,1152]{1,0:T(8,128)(2,1)S(1)}, bf16[32,1152]{1,0:T(8,128)(2,1)S(1)}, u32[]{:S(2)}, u32[]{:S(2)}) %collective-permute-start.7) | collective-permute-done | bytes 73760 | tf_op jit(solution)/shard_map/ppermute | solution.py:498
  102.9 2.3 %collective-permute-start.12 = (bf16[32,1152]{1,0:T(8,128)(2,1)S(1)}, bf16[32,1152]{1,0:T(8,128)(2,1)S(1)}, u32[]{:S(2)}, u32[]{:S(2)}) collective-permute-start(bf16[32,1152]{1,0:T(8,128)(2,1)S(1)} %fusion.8), channel_id=1, source_target_pairs={{0,128},{32,160},{64,192},{96,224},{128,0},{160,32},{192,64},{224,... | collective-permute-start | bytes 221192 | tf_op jit(solution)/shard_map/ppermute | solution.py:498
  106.1 1.8 %rims.1 = bf16[1024,1024]{1,0:T(8,128)(2,1)} custom-call(bf16[1024,1024]{1,0:T(8,128)(2,1)} %get-tuple-element.73.grad_ref, bf16[128,1024]{1,0:T(8,128)(2,1)S(1)} %collective-permute-done.9.near_ref, bf16[128,1024]{1,0:T(8,128)(2,1)S(1)} %collective-permute-done.10.far_ref), custom_call_target="tpu_custom_call", output_to_operand_aliasing={{}: (0, {})} | custom-call | flops 262144 | bytes 1572864 | tf_op jit(solution)/shard_map/rims/pallas_call | solution.py:483
  110.5 7.9 %collective-permute-done.14 = bf16[32,1152]{1,0:T(8,128)(2,1)S(1)} collective-permute-done((bf16[32,1152]{1,0:T(8,128)(2,1)S(1)}, bf16[32,1152]{1,0:T(8,128)(2,1)S(1)}, u32[]{:S(2)}, u32[]{:S(2)}) %collective-permute-start.14) | collective-permute-done | bytes 73760 | tf_op jit(solution)/shard_map/ppermute | solution.py:498
  (45 shorter events, 7.8 us)
Async XLA Ops:
  1.7 18.1 %collective-permute-start = (bf16[128,1024]{1,0:T(8,128)(2,1)S(1)}, bf16[128,1024]{1,0:T(8,128)(2,1)S(1)}, u32[]{:S(2)}, u32[]{:S(2)}) collective-permute-start(bf16[128,1024]{1,0:T(8,128)(2,1)S(1)} %get-tuple-element.84), channel_id=1, source_target_pairs={{0,1},{1,0},{2,3},{3,2},{4,5},{5,4},{6,7},{7,6},{8,9},{9,8},{10,11... | collective-permute-start | bytes 786440 | tf_op jit(solution)/shard_map/ppermute | solution.py:498
  1.8 18.0 %collective-permute-start.1 = (bf16[128,1024]{1,0:T(8,128)(2,1)S(1)}, bf16[128,1024]{1,0:T(8,128)(2,1)S(1)}, u32[]{:S(2)}, u32[]{:S(2)}) collective-permute-start(bf16[128,1024]{1,0:T(8,128)(2,1)S(1)} %get-tuple-element.83), channel_id=1, source_target_pairs={{1,2},{2,1},{3,4},{4,3},{5,6},{6,5},{7,8},{8,7},{9,10},{10,9},{11,... | collective-permute-start | bytes 786440 | tf_op jit(solution)/shard_map/ppermute | solution.py:498
  19.8 12.1 %copy-start.7 = (f32[100]{0:T(128)S(1)}, f32[100]{0:T(128)}, u32[]{:S(2)}) copy-start(f32[100]{0:T(128)} %param.15) | copy-start | bytes 1204
  19.8 12.2 %copy-start.6 = (f32[100,1024]{1,0:T(8,128)S(1)}, f32[100,1024]{1,0:T(8,128)}, u32[]{:S(2)}) copy-start(f32[100,1024]{1,0:T(8,128)} %param.13) | copy-start | bytes 1228804
  19.8 23.2 %copy-start.5 = (f32[1024]{0:T(1024)S(1)}, f32[1024]{0:T(1024)}, u32[]{:S(2)}) copy-start(f32[1024]{0:T(1024)} %param.14) | copy-start | bytes 12292
  23.5 19.5 %all-to-all-start = ((bf16[8,112,128]{2,1,0:T(8,128)(2,1)}), bf16[8,112,128]{2,1,0:T(8,128)(2,1)S(1)}, u32[]{:S(2)}, u32[]{:S(2)}) async-start(bf16[8,112,128]{2,1,0:T(8,128)(2,1)} %get-tuple-element.52), calls=%async_computation | async-start | bytes 458752 | tf_op jit(solution)/shard_map/all_to_all | solution.py:532
  45.3 14.4 %all-to-all-start.1 = ((bf16[8,112,128]{2,1,0:T(8,128)(2,1)}), bf16[8,112,128]{2,1,0:T(8,128)(2,1)S(1)}, u32[]{:S(2)}, u32[]{:S(2)}) async-start(bf16[8,112,128]{2,1,0:T(8,128)(2,1)} %pairs.1), calls=%async_computation.1 | async-start | bytes 458752 | tf_op jit(solution)/shard_map/all_to_all | solution.py:534
  59.8 17.9 %copy-start.1 = (bf16[1024,512]{1,0:T(8,128)(2,1)S(1)}, bf16[1024,512]{1,0:T(8,128)(2,1)}, u32[]{:S(2)}) copy-start(bf16[1024,512]{1,0:T(8,128)(2,1)} %get-tuple-element.60.edges_ref) | copy-start | bytes 3145732
  59.8 17.9 %copy-start.4 = (bf16[1024,1024]{1,0:T(8,128)(2,1)S(1)}, bf16[1024,1024]{1,0:T(8,128)(2,1)}, u32[]{:S(2)}) copy-start(bf16[1024,1024]{1,0:T(8,128)(2,1)} %mix_ref.1) | copy-start | bytes 6291460
  69.4 8.3 %copy-start.2 = (f32[1024,1]{1,0:T(8,128)S(1)}, f32[1024,1]{1,0:T(8,128)}, u32[]{:S(2)}) copy-start(f32[1024,1]{1,0:T(8,128)} %get-tuple-element.63.inv_ref) | copy-start | bytes 12292
  69.4 8.3 %copy-start.3 = (f32[1024]{0:T(1024)S(1)}, f32[1024]{0:T(1024)}, u32[]{:S(2)}) copy-start(f32[1024]{0:T(1024)} %param.10) | copy-start | bytes 12292
  69.4 2.9 %collective-permute-start.2 = (bf16[4,4,32,1152]{3,2,1,0:T(8,128)(2,1)S(1)}, bf16[4,4,32,1152]{3,2,1,0:T(8,128)(2,1)S(1)}, u32[]{:S(2)}, u32[]{:S(2)}) collective-permute-start(bf16[4,4,32,1152]{3,2,1,0:T(8,128)(2,1)S(1)} %get-tuple-element.59), channel_id=1, source_target_pairs={{0,1},{1,0},{2,3},{3,2},{4,5},{5,4},{6,7},{7,6},{8,9},{9,8},{10,11... | collective-permute-start | bytes 3538952 | tf_op jit(solution)/shard_map/ppermute | solution.py:498
  72.6 19.1 %collective-permute-start.3 = (bf16[4,32,1152]{2,1,0:T(8,128)(2,1)S(1)}, bf16[4,32,1152]{2,1,0:T(8,128)(2,1)S(1)}, u32[]{:S(2)}, u32[]{:S(2)}) collective-permute-start(bf16[4,32,1152]{2,1,0:T(8,128)(2,1)S(1)} %get-tuple-element.82), channel_id=1, source_target_pairs={{0,8},{1,9},{2,10},{3,11},{4,12},{5,13},{6,14},{7,15},{8,16},{9,17... | collective-permute-start | bytes 884744 | tf_op jit(solution)/shard_map/ppermute | solution.py:498
  74.1 17.5 %collective-permute-start.4 = (bf16[4,32,1152]{2,1,0:T(8,128)(2,1)S(1)}, bf16[4,32,1152]{2,1,0:T(8,128)(2,1)S(1)}, u32[]{:S(2)}, u32[]{:S(2)}) collective-permute-start(bf16[4,32,1152]{2,1,0:T(8,128)(2,1)S(1)} %get-tuple-element.81), channel_id=1, source_target_pairs={{0,16},{1,17},{2,18},{3,19},{4,20},{5,21},{6,22},{7,23},{8,24},{9,... | collective-permute-start | bytes 884744 | tf_op jit(solution)/shard_map/ppermute | solution.py:498
  75.2 16.5 %collective-permute-start.5 = (bf16[4,32,1152]{2,1,0:T(8,128)(2,1)S(1)}, bf16[4,32,1152]{2,1,0:T(8,128)(2,1)S(1)}, u32[]{:S(2)}, u32[]{:S(2)}) collective-permute-start(bf16[4,32,1152]{2,1,0:T(8,128)(2,1)S(1)} %get-tuple-element.80), channel_id=1, source_target_pairs={{0,24},{1,25},{2,26},{3,27},{4,28},{5,29},{6,30},{7,31},{8,0},{9,1... | collective-permute-start | bytes 884744 | tf_op jit(solution)/shard_map/ppermute | solution.py:498
  85.5 11.5 %collective-permute-start.9 = (bf16[128,1024]{1,0:T(8,128)(2,1)S(1)}, bf16[128,1024]{1,0:T(8,128)(2,1)S(1)}, u32[]{:S(2)}, u32[]{:S(2)}) collective-permute-start(bf16[128,1024]{1,0:T(8,128)(2,1)S(1)} %get-tuple-element.68), channel_id=1, source_target_pairs={{0,1},{1,0},{2,3},{3,2},{4,5},{5,4},{6,7},{7,6},{8,9},{9,8},{10,11... | collective-permute-start | bytes 786440 | tf_op jit(solution)/shard_map/ppermute | solution.py:498
  85.5 12.3 %collective-permute-start.10 = (bf16[128,1024]{1,0:T(8,128)(2,1)S(1)}, bf16[128,1024]{1,0:T(8,128)(2,1)S(1)}, u32[]{:S(2)}, u32[]{:S(2)}) collective-permute-start(bf16[128,1024]{1,0:T(8,128)(2,1)S(1)} %get-tuple-element.69), channel_id=1, source_target_pairs={{1,2},{2,1},{3,4},{4,3},{5,6},{6,5},{7,8},{8,7},{9,10},{10,9},{11,... | collective-permute-start | bytes 786440 | tf_op jit(solution)/shard_map/ppermute | solution.py:498
  91.9 7.9 %collective-permute-start.6 = (bf16[32,1152]{1,0:T(8,128)(2,1)S(1)}, bf16[32,1152]{1,0:T(8,128)(2,1)S(1)}, u32[]{:S(2)}, u32[]{:S(2)}) collective-permute-start(bf16[32,1152]{1,0:T(8,128)(2,1)S(1)} %get-tuple-element.87), channel_id=1, source_target_pairs={{0,2},{1,3},{2,4},{3,5},{4,6},{5,7},{6,0},{7,1},{8,10},{9,11},{10,... | collective-permute-start | bytes 221192 | tf_op jit(solution)/shard_map/ppermute | solution.py:498
  92.9 9.3 %collective-permute-start.7 = (bf16[32,1152]{1,0:T(8,128)(2,1)S(1)}, bf16[32,1152]{1,0:T(8,128)(2,1)S(1)}, u32[]{:S(2)}, u32[]{:S(2)}) collective-permute-start(bf16[32,1152]{1,0:T(8,128)(2,1)S(1)} %get-tuple-element.86), channel_id=1, source_target_pairs={{0,4},{1,5},{2,6},{3,7},{4,0},{5,1},{6,2},{7,3},{8,12},{9,13},{10,... | collective-permute-start | bytes 221192 | tf_op jit(solution)/shard_map/ppermute | solution.py:498
  94.4 7.9 %collective-permute-start.8 = (bf16[32,1152]{1,0:T(8,128)(2,1)S(1)}, bf16[32,1152]{1,0:T(8,128)(2,1)S(1)}, u32[]{:S(2)}, u32[]{:S(2)}) collective-permute-start(bf16[32,1152]{1,0:T(8,128)(2,1)S(1)} %get-tuple-element.85), channel_id=1, source_target_pairs={{0,6},{1,7},{2,0},{3,1},{4,2},{5,3},{6,4},{7,5},{8,14},{9,15},{10,... | collective-permute-start | bytes 221192 | tf_op jit(solution)/shard_map/ppermute | solution.py:498
  102.3 5.7 %collective-permute-start.11 = (bf16[32,1152]{1,0:T(8,128)(2,1)S(1)}, bf16[32,1152]{1,0:T(8,128)(2,1)S(1)}, u32[]{:S(2)}, u32[]{:S(2)}) collective-permute-start(bf16[32,1152]{1,0:T(8,128)(2,1)S(1)} %fusion.8), channel_id=1, source_target_pairs={{0,64},{32,96},{64,128},{96,160},{128,192},{160,224},{192,0},{224,... | collective-permute-start | bytes 221192 | tf_op jit(solution)/shard_map/ppermute | solution.py:498
  102.9 5.9 %collective-permute-start.12 = (bf16[32,1152]{1,0:T(8,128)(2,1)S(1)}, bf16[32,1152]{1,0:T(8,128)(2,1)S(1)}, u32[]{:S(2)}, u32[]{:S(2)}) collective-permute-start(bf16[32,1152]{1,0:T(8,128)(2,1)S(1)} %fusion.8), channel_id=1, source_target_pairs={{0,128},{32,160},{64,192},{96,224},{128,0},{160,32},{192,64},{224,... | collective-permute-start | bytes 221192 | tf_op jit(solution)/shard_map/ppermute | solution.py:498
  105.2 4.4 %collective-permute-start.13 = (bf16[32,1152]{1,0:T(8,128)(2,1)S(1)}, bf16[32,1152]{1,0:T(8,128)(2,1)S(1)}, u32[]{:S(2)}, u32[]{:S(2)}) collective-permute-start(bf16[32,1152]{1,0:T(8,128)(2,1)S(1)} %fusion.8), channel_id=1, source_target_pairs={{0,192},{32,224},{64,0},{96,32},{128,64},{160,96},{192,128},{224,1... | collective-permute-start | bytes 221192 | tf_op jit(solution)/shard_map/ppermute | solution.py:498
  109.7 8.7 %collective-permute-start.14 = (bf16[32,1152]{1,0:T(8,128)(2,1)S(1)}, bf16[32,1152]{1,0:T(8,128)(2,1)S(1)}, u32[]{:S(2)}, u32[]{:S(2)}) collective-permute-start(bf16[32,1152]{1,0:T(8,128)(2,1)S(1)} %add_convert_fusion.3), channel_id=1, source_target_pairs={{0,32},{32,0},{64,96},{96,64},{128,160},{160,128},{192,224},{224,1... | collective-permute-start | bytes 221192 | tf_op jit(solution)/shard_map/ppermute | solution.py:498
  (1 other events, 8.3 us)

commit v4 on v3

--- a/solution.py
+++ b/solution.py
@@ -243,14 +243,12 @@
 
 
 def pair_kernel(pred_ref, obs_ref, area_ref, weight_ref, back_ref):
-    piece = lax.rem(lax.axis_index("member") + 1, MEMBERS)
-    first = pl.multiple_of(piece * PIECE, PIECE)
-    area = area_ref[:, pl.ds(first, PIECE)]
+    area = area_ref[...]
     loss = jnp.zeros((16, PIECE), f32)
     for tile in range(ROWS // 16):
         rows = slice(16 * tile, 16 * tile + 16)
         preds = [pred_ref[m, rows].astype(f32) for m in range(MEMBERS)]
-        observed = obs_ref[rows, pl.ds(first, PIECE)]
+        observed = obs_ref[rows]
         slopes = [jnp.zeros((16, PIECE), f32)] * MEMBERS
         near = jnp.zeros((16, PIECE), f32)
         apart = jnp.zeros((16, PIECE), f32)
@@ -285,8 +283,17 @@
 
 
 def pair_terms(preds, observed, area, weight):
+    column = lambda i: (0, lax.rem(lax.axis_index("member") + 1, MEMBERS))
     return pl.pallas_call(
         pair_kernel,
+        grid=(1,),
+        in_specs=[
+            whole((MEMBERS, ROWS, PIECE)),
+            pl.BlockSpec((ROWS, PIECE), column),
+            pl.BlockSpec((1, PIECE), column),
+            whole((ROWS, 1)),
+        ],
+        out_specs=whole((MEMBERS, ROWS, PIECE)),
         out_shape=pltpu.HBM((MEMBERS, ROWS, PIECE), bf16),
         cost_estimate=pl.CostEstimate(
             flops=1 << 24, bytes_accessed=1 << 20, transcendentals=1 << 20
@@ -298,7 +305,7 @@
 
 def weights_kernel(
     pos_ref, pair_ref, pred_ref, obs0_ref, obs1_ref, area0_ref, area1_ref, weight_ref, out_ref, deriv_ref, hidden_ref, normed_ref,
-    g_ref, pre_ref, loss_ref, keep_ref, send_ref, pre_all, out_sum,
+    g_ref, pre_ref, loss_ref, keep_ref, send_ref, pre_all, g_all,
 ):
     step = pl.program_id(0)
 
@@ -323,25 +330,17 @@
         )
         d_pre = (d_hidden * deriv_ref[...].astype(f32)).astype(bf16)
         pre_ref[...] = d_pre
-        pre_all[pl.ds(pl.multiple_of(step * BLK, BLK), BLK)] = d_pre
-        part = jnp.dot(g, hidden_ref[...], preferred_element_type=f32)
-
-        @pl.when(step == 0)
-        def _():
-            out_sum[0:ROWS] = part
-            out_sum[ROWS:] = jnp.zeros((128 - ROWS, D), f32)
-
-        @pl.when(step > 0)
-        def _():
-            out_sum[0:ROWS] += part
+        rows = pl.ds(pl.multiple_of(step * BLK, BLK), BLK)
+        pre_all[rows] = d_pre
+        g_all[:, rows] = g
 
     @pl.when(step >= STEPS)
     def _():
-        x_at = lax.rem(pos_ref[0] + step - STEPS, 4)
         mix = lax.dot_general(
             normed_ref[...], pre_all[...], (((0,), (0,)), ((), ())), preferred_element_type=f32
         ).astype(bf16)
-        out = out_sum[:, pl.ds(pl.multiple_of(x_at * BLK, BLK), BLK)].T.astype(bf16)
+        out = jnp.dot(g_all[...], hidden_ref[...], preferred_element_type=f32)
+        out = jnp.concatenate([out, jnp.zeros((128 - ROWS, BLK), f32)], axis=0).T.astype(bf16)
         mine = pos_ref[2] == 0
         for z in range(4):
             at = lax.rem(z + 4 - pos_ref[1], 4)
@@ -357,6 +356,7 @@
     later = lambda i: jnp.maximum(i - STEPS, 0)
     rows = pl.BlockSpec((BLK, D), lambda i, pos: (first(i), 0))
     columns = pl.BlockSpec((ROWS, BLK), lambda i, pos: (0, first(i)))
+    features = pl.BlockSpec((CELLS, BLK), lambda i, pos: (0, lax.rem(pos[0] + later(i), 4)))
     left = lambda i, pos: (0, 2 * first(i) + 1)
     right = lambda i, pos: (0, lax.rem(2 * first(i) + 2, MEMBERS))
     share = pl.BlockSpec((1, 4, 32, WIDE), lambda i, pos: (later(i), 0, 0, 0))
@@ -375,11 +375,11 @@
                 whole((ROWS, 1)),
                 whole((ROWS, D)),
                 rows,
-                rows,
-                pl.BlockSpec((CELLS, BLK), lambda i, pos: (0, lax.rem(pos[0] + later(i), 4))),
+                features,
+                features,
             ],
             out_specs=[columns, rows, whole((1, CELLS)), share, share],
-            scratch_shapes=[pltpu.VMEM((CELLS, D), bf16), pltpu.VMEM((128, D), f32)],
+            scratch_shapes=[pltpu.VMEM((CELLS, D), bf16), pltpu.VMEM((ROWS, CELLS), bf16)],
         ),
         out_shape=[
             jax.ShapeDtypeStruct((ROWS, CELLS), bf16),
@@ -550,14 +550,12 @@
     def over_z(k):
         return along(share[k], "space", lambda i: i // 8 * 8 + (i + 2 * k) % 8)
 
-    arrived = [over_z(k) for k in (1, 2, 3)]
+    share = summed([share[0]] + [over_z(k) for k in (1, 2, 3)]).astype(bf16)
+    arrived = [along(share, "member", lambda i: (i + 2 * k) % 8) for k in (1, 2, 3)]
     arrived, near, far = lax.optimization_barrier((arrived, near, far))
-    share = summed([share[0]] + arrived).astype(bf16)
-    arrived = [along(share, "member", lambda i: (i + 2 * k) % 8) for k in (1, 2, 3)]
-    grad = add_rims(grad, near, far)
-    arrived, grad = lax.optimization_barrier((arrived, grad))
     share = summed([share] + arrived).astype(bf16)
     totals = summed([share, along(share, "member", lambda i: i ^ 1)])
+    grad = add_rims(grad, near, far)
     grad_scale = 1.0 / math.sqrt(MEMBERS * CELLS * 32)
     return (
         losses.reshape(CELLS),

time: 121 us -> 119 us (0.983)
  starting transfers between devices: 39.6 us -> 38.1 us
    ppermute x15, starting transfers between devices: 27.8 us -> 26.3 us  [along(): lax.ppermute(value, axis, [pair for pair in pairs if pair[1] is not None])]
  transfers between devices with their start and end apart: 17 -> 17, of which waited for: 9 -> 10; matrix products, arithmetic and copies ran while one was open for 1% -> 1% of each run, Pallas kernels for 17% -> 18%
where the time goes in v4:
time: 119 us
  waiting for transfers between devices  39.5 us (33%)
  starting transfers between devices  38.1 us (32%)
  Pallas kernels  36.4 us (31%)
  other arithmetic  2.93 us (2%)
    ppermute x15, starting transfers between devices, along(): lax.ppermute(value, axis, [pair for pair in pairs if pair[1] is not None])  26.3 us
    ppermute x15, waiting for transfers between devices, along(): lax.ppermute(value, axis, [pair for pair in pairs if pair[1] is not None])  18.4 us
    pallas_call x1, Pallas kernels, forward(): pl.pallas_call(interior_kernel, grid=(STEPS - 1,), in_specs=[edges_at(lam...  11.4 us
    all_to_all x1, waiting for transfers between devices, shards(): pairs = lax.all_to_all(pairs, 'member', 0, 0, tiled=True)  10.9 us
    all_to_all x1, waiting for transfers between devices, shards(): pieces = lax.all_to_all(pieces, 'member', 0, 0, tiled=True)  10.2 us
    pallas_call x1, Pallas kernels, weight_parts(): pl.pallas_call(weights_kernel, grid_spec=pltpu.PrefetchScalarGridSpec(num...  9.74 us
    all_to_all x1, starting transfers between devices, shards(): pieces = lax.all_to_all(pieces, 'member', 0, 0, tiled=True)  8.39 us
    pallas_call x1, Pallas kernels, latent_parts(): pl.pallas_call(latent_kernel, grid=(STEPS,), in_specs=[pl.BlockSpec((BLK,...  7.72 us
  transfers between devices with their start and end apart: 17, of which 10 were waited for; matrix products, arithmetic and copies ran while one was open for 1% of the time, Pallas kernels for 18%

profile of v4, /device:TPU:2, one launch (start us, length us, event | category | flops | bytes accessed | tf_op | source)
XLA Modules:
  0.0 118.7 jit_solution(10945811426011047699)
XLA Ops:
  0.6 1.1 select_bitcast_fusion
  1.8 6.6 %collective-permute-start.1 = (bf16[128,1024]{1,0:T(8,128)(2,1)S(1)}, bf16[128,1024]{1,0:T(8,128)(2,1)S(1)}, u32[]{:S(2)}, u32[]{:S(2)}) collective-permute-start(bf16[128,1024]{1,0:T(8,128)(2,1)S(1)} %get-tuple-element.75), channel_id=1, source_target_pairs={{1,2},{2,1},{3,4},{4,3},{5,6},{6,5},{7,8},{8,7},{9,10},{10,9},{11,... | collective-permute-start | bytes 786440 | tf_op jit(solution)/shard_map/ppermute | solution.py:498
  8.4 11.4 %interior.1 = (bf16[112,1024]{1,0:T(8,128)(2,1)S(1)}, bf16[512,1024]{1,0:T(8,128)(2,1)S(1)}, bf16[1024,1024]{1,0:T(8,128)(2,1)S(1)}, bf16[1024,512]{1,0:T(8,128)...) custom-call(s32[4,1024]{1,0:T(4,128)} %nb1_ref.3, ...), custom_call_target="tpu_custom_call" | custom-call | flops 3221225472 | bytes 9437184 | tf_op jit(solution)/shard_map/interior/pallas_call | solution.py:194
  19.9 3.6 %rim_cells.1 = (bf16[1024,512]{1,0:T(8,128)(2,1)}, bf16[1024,1024]{1,0:T(8,128)(2,1)}, bf16[1024,1024]{1,0:T(8,128)(2,1)}, bf16[1024,1024]{1,0:T(8,128)(2,1)}, f...) custom-call(s32[4,1024]{1,0:T(4,128)} %nb1_ref.3, ...), custom_call_target="tpu_custom_call", output_to_operand_aliasing={{0}: (8, {}), {1}: (9, {}), {2}: (10, {}), {3}: (11, {}), {... | custom-call | flops 1073741824 | bytes 3145728 | tf_op jit(solution)/shard_map/rim_cells/pallas_call | solution.py:221
  23.5 8.4 %all-to-all-start = ((bf16[8,112,128]{2,1,0:T(8,128)(2,1)}), bf16[8,112,128]{2,1,0:T(8,128)(2,1)S(1)}, u32[]{:S(2)}, u32[]{:S(2)}) async-start(bf16[8,112,128]{2,1,0:T(8,128)(2,1)} %get-tuple-element.48), calls=%async_computation | async-start | bytes 458752 | tf_op jit(solution)/shard_map/all_to_all | solution.py:532
  32.8 10.2 %all-to-all-done.pred_ref = bf16[8,112,128]{2,1,0:T(8,128)(2,1)S(1)} async-done(((bf16[8,112,128]{2,1,0:T(8,128)(2,1)}), bf16[8,112,128]{2,1,0:T(8,128)(2,1)S(1)}, u32[]{:S(2)}, u32[]{:S(2)}) %all-to-all-start) | async-done | bytes 229408 | tf_op jit(solution)/shard_map/all_to_all | solution.py:532
  43.0 2.2 %pairs.1 = bf16[8,112,128]{2,1,0:T(8,128)(2,1)} custom-call(bf16[8,112,128]{2,1,0:T(8,128)(2,1)S(1)} %all-to-all-done.pred_ref, f32[112,1024]{1,0:T(8,128)} %pad.8.obs_ref.obs0_ref.obs1_ref, f32[1,1024]{1,0:T(1,128)S(1)} %bitcast.43, f32[112,1]{1,0:T(8,128)S(1)} %copy.20.weight_ref), custom_call_target="tpu_custom_call" | custom-call | flops 16777216 | bytes 1048576 | tf_op jit(solution)/shard_map/pairs/pallas_call | solution.py:287
  45.1 3.4 %all-to-all-start.1 = ((bf16[8,112,128]{2,1,0:T(8,128)(2,1)}), bf16[8,112,128]{2,1,0:T(8,128)(2,1)S(1)}, u32[]{:S(2)}, u32[]{:S(2)}) async-start(bf16[8,112,128]{2,1,0:T(8,128)(2,1)} %pairs.1), calls=%async_computation.1 | async-start | bytes 458752 | tf_op jit(solution)/shard_map/all_to_all | solution.py:534
  48.7 10.9 %all-to-all-done.1.pair_ref = bf16[8,112,128]{2,1,0:T(8,128)(2,1)S(1)} async-done(((bf16[8,112,128]{2,1,0:T(8,128)(2,1)}), bf16[8,112,128]{2,1,0:T(8,128)(2,1)S(1)}, u32[]{:S(2)}, u32[]{:S(2)}) %all-to-all-start.1) | async-done | bytes 229408 | tf_op jit(solution)/shard_map/all_to_all | solution.py:534
  59.6 9.7 %weights.1 = (bf16[112,1024]{1,0:T(8,128)(2,1)S(1)}, bf16[1024,1024]{1,0:T(8,128)(2,1)S(1)}, f32[1,1024]{1,0:T(1,128)}, bf16[4,4,32,1152]{3,2,1,0:T(8,128)(2,1)S(1)}, bf16[4,4,32,1152]{3,2,1,0:T(8,128)(2,1)S(1)}) custom-call(s32[3]{0:T(128)S(1)} %pad_add_fusion.pos_ref, bf16[8,112,128]{2,1,0:T(8,128)(2,1)S(1)} %all-to-all-done.1.pair_ref, ...), custom_call_target="tpu_custom_call" | custom-call | flops 3221225472 | bytes 14680064 | tf_op jit(solution)/shard_map/weights/pallas_call | solution.py:363
  69.4 2.8 %collective-permute-done.2 = bf16[4,4,32,1152]{3,2,1,0:T(8,128)(2,1)S(1)} collective-permute-done((bf16[4,4,32,1152]{3,2,1,0:T(8,128)(2,1)S(1)}, bf16[4,4,32,1152]{3,2,1,0:T(8,128)(2,1)S(1)}, u32[]{:S(2)}, u32[]{:S(2)}) %collective-permute-start.2) | collective-permute-done | bytes 1179680 | tf_op jit(solution)/shard_map/ppermute | solution.py:498
  72.5 1.6 %collective-permute-start.3 = (bf16[4,32,1152]{2,1,0:T(8,128)(2,1)S(1)}, bf16[4,32,1152]{2,1,0:T(8,128)(2,1)S(1)}, u32[]{:S(2)}, u32[]{:S(2)}) collective-permute-start(bf16[4,32,1152]{2,1,0:T(8,128)(2,1)S(1)} %get-tuple-element.74), channel_id=1, source_target_pairs={{0,8},{1,9},{2,10},{3,11},{4,12},{5,13},{6,14},{7,15},{8,16},{9,17... | collective-permute-start | bytes 884744 | tf_op jit(solution)/shard_map/ppermute | solution.py:498
  75.1 2.5 %collective-permute-start.5 = (bf16[4,32,1152]{2,1,0:T(8,128)(2,1)S(1)}, bf16[4,32,1152]{2,1,0:T(8,128)(2,1)S(1)}, u32[]{:S(2)}, u32[]{:S(2)}) collective-permute-start(bf16[4,32,1152]{2,1,0:T(8,128)(2,1)S(1)} %get-tuple-element.72), channel_id=1, source_target_pairs={{0,24},{1,25},{2,26},{3,27},{4,28},{5,29},{6,30},{7,31},{8,0},{9,1... | collective-permute-start | bytes 884744 | tf_op jit(solution)/shard_map/ppermute | solution.py:498
  77.7 7.7 %latent.1 = (bf16[1024,1024]{1,0:T(8,128)(2,1)}, bf16[128,1024]{1,0:T(8,128)(2,1)S(1)}, bf16[128,1024]{1,0:T(8,128)(2,1)S(1)}) custom-call(bf16[1024,512]{1,0:T(8,128)(2,1)S(1)} %copy-done.1, bf16[112,1024]{1,0:T(8,128)(2,1)S(1)} %get-tuple-element.57.g_ref, bf16[112,1024]{1,0:T(8,128)(2,1)S(1)} %get-tuple-element.40.out_t_ref.out_ref, ...), custom_call_target="tpu_custom_call" | custom-call | flops 4294967296 | bytes 10485760 | tf_op jit(solution)/shard_map/latent/pallas_call | solution.py:451
  85.5 4.7 %collective-permute-done.5 = bf16[4,32,1152]{2,1,0:T(8,128)(2,1)S(1)} collective-permute-done((bf16[4,32,1152]{2,1,0:T(8,128)(2,1)S(1)}, bf16[4,32,1152]{2,1,0:T(8,128)(2,1)S(1)}, u32[]{:S(2)}, u32[]{:S(2)}) %collective-permute-start.5) | collective-permute-done | bytes 294944 | tf_op jit(solution)/shard_map/ppermute | solution.py:498
  90.4 3.4 %collective-permute-start.8 = (bf16[32,1152]{1,0:T(8,128)(2,1)S(1)}, bf16[32,1152]{1,0:T(8,128)(2,1)S(1)}, u32[]{:S(2)}, u32[]{:S(2)}) collective-permute-start(bf16[32,1152]{1,0:T(8,128)(2,1)S(1)} %get-tuple-element.78), channel_id=1, source_target_pairs={{0,6},{1,7},{2,0},{3,1},{4,2},{5,3},{6,4},{7,5},{8,14},{9,15},{10,... | collective-permute-start | bytes 221192 | tf_op jit(solution)/shard_map/ppermute | solution.py:498
  94.3 1.7 %collective-permute-start.6 = (bf16[32,1152]{1,0:T(8,128)(2,1)S(1)}, bf16[32,1152]{1,0:T(8,128)(2,1)S(1)}, u32[]{:S(2)}, u32[]{:S(2)}) collective-permute-start(bf16[32,1152]{1,0:T(8,128)(2,1)S(1)} %get-tuple-element.77), channel_id=1, source_target_pairs={{0,2},{1,3},{2,4},{3,5},{4,6},{5,7},{6,0},{7,1},{8,10},{9,11},{10,... | collective-permute-start | bytes 221192 | tf_op jit(solution)/shard_map/ppermute | solution.py:498
  96.0 4.1 %collective-permute-start.13 = (bf16[128,1024]{1,0:T(8,128)(2,1)S(1)}, bf16[128,1024]{1,0:T(8,128)(2,1)S(1)}, u32[]{:S(2)}, u32[]{:S(2)}) collective-permute-start(bf16[128,1024]{1,0:T(8,128)(2,1)S(1)} %get-tuple-element.66), channel_id=1, source_target_pairs={{1,2},{2,1},{3,4},{4,3},{5,6},{6,5},{7,8},{8,7},{9,10},{10,9},{11,... | collective-permute-start | bytes 786440 | tf_op jit(solution)/shard_map/ppermute | solution.py:498
  100.2 1.2 %collective-permute-done.7 = bf16[32,1152]{1,0:T(8,128)(2,1)S(1)} collective-permute-done((bf16[32,1152]{1,0:T(8,128)(2,1)S(1)}, bf16[32,1152]{1,0:T(8,128)(2,1)S(1)}, u32[]{:S(2)}, u32[]{:S(2)}) %collective-permute-start.7) | collective-permute-done | bytes 73760 | tf_op jit(solution)/shard_map/ppermute | solution.py:498
  101.8 2.1 %collective-permute-start.10 = (bf16[32,1152]{1,0:T(8,128)(2,1)S(1)}, bf16[32,1152]{1,0:T(8,128)(2,1)S(1)}, u32[]{:S(2)}, u32[]{:S(2)}) collective-permute-start(bf16[32,1152]{1,0:T(8,128)(2,1)S(1)} %fusion.8), channel_id=1, source_target_pairs={{0,128},{32,160},{64,192},{96,224},{128,0},{160,32},{192,64},{224,... | collective-permute-start | bytes 221192 | tf_op jit(solution)/shard_map/ppermute | solution.py:498
  103.8 1.5 %collective-permute-start.11 = (bf16[32,1152]{1,0:T(8,128)(2,1)S(1)}, bf16[32,1152]{1,0:T(8,128)(2,1)S(1)}, u32[]{:S(2)}, u32[]{:S(2)}) collective-permute-start(bf16[32,1152]{1,0:T(8,128)(2,1)S(1)} %fusion.8), channel_id=1, source_target_pairs={{0,192},{32,224},{64,0},{96,32},{128,64},{160,96},{192,128},{224,1... | collective-permute-start | bytes 221192 | tf_op jit(solution)/shard_map/ppermute | solution.py:498
  105.3 2.0 %collective-permute-done.13.far_ref = bf16[128,1024]{1,0:T(8,128)(2,1)S(1)} collective-permute-done((bf16[128,1024]{1,0:T(8,128)(2,1)S(1)}, bf16[128,1024]{1,0:T(8,128)(2,1)S(1)}, u32[]{:S(2)}, u32[]{:S(2)}) %collective-permute-start.13) | collective-permute-done | bytes 262176 | tf_op jit(solution)/shard_map/ppermute | solution.py:498
  109.6 1.8 %rims.1 = bf16[1024,1024]{1,0:T(8,128)(2,1)} custom-call(bf16[1024,1024]{1,0:T(8,128)(2,1)} %get-tuple-element.61.grad_ref, bf16[128,1024]{1,0:T(8,128)(2,1)S(1)} %collective-permute-done.12.near_ref, bf16[128,1024]{1,0:T(8,128)(2,1)S(1)} %collective-permute-done.13.far_ref), custom_call_target="tpu_custom_call", output_to_operand_aliasing={{}: (0, {})} | custom-call | flops 262144 | bytes 1572864 | tf_op jit(solution)/shard_map/rims/pallas_call | solution.py:483
  111.4 6.1 %collective-permute-done.14 = bf16[32,1152]{1,0:T(8,128)(2,1)S(1)} collective-permute-done((bf16[32,1152]{1,0:T(8,128)(2,1)S(1)}, bf16[32,1152]{1,0:T(8,128)(2,1)S(1)}, u32[]{:S(2)}, u32[]{:S(2)}) %collective-permute-start.14) | collective-permute-done | bytes 73760 | tf_op jit(solution)/shard_map/ppermute | solution.py:498
  (45 shorter events, 7.2 us)
Async XLA Ops:
  1.7 18.1 %collective-permute-start = (bf16[128,1024]{1,0:T(8,128)(2,1)S(1)}, bf16[128,1024]{1,0:T(8,128)(2,1)S(1)}, u32[]{:S(2)}, u32[]{:S(2)}) collective-permute-start(bf16[128,1024]{1,0:T(8,128)(2,1)S(1)} %get-tuple-element.76), channel_id=1, source_target_pairs={{0,1},{1,0},{2,3},{3,2},{4,5},{5,4},{6,7},{7,6},{8,9},{9,8},{10,11... | collective-permute-start | bytes 786440 | tf_op jit(solution)/shard_map/ppermute | solution.py:498
  1.8 18.0 %collective-permute-start.1 = (bf16[128,1024]{1,0:T(8,128)(2,1)S(1)}, bf16[128,1024]{1,0:T(8,128)(2,1)S(1)}, u32[]{:S(2)}, u32[]{:S(2)}) collective-permute-start(bf16[128,1024]{1,0:T(8,128)(2,1)S(1)} %get-tuple-element.75), channel_id=1, source_target_pairs={{1,2},{2,1},{3,4},{4,3},{5,6},{6,5},{7,8},{8,7},{9,10},{10,9},{11,... | collective-permute-start | bytes 786440 | tf_op jit(solution)/shard_map/ppermute | solution.py:498
  19.8 12.1 %copy-start.7 = (f32[100]{0:T(128)S(1)}, f32[100]{0:T(128)}, u32[]{:S(2)}) copy-start(f32[100]{0:T(128)} %param.15) | copy-start | bytes 1204
  19.8 12.2 %copy-start.6 = (f32[100,1024]{1,0:T(8,128)S(1)}, f32[100,1024]{1,0:T(8,128)}, u32[]{:S(2)}) copy-start(f32[100,1024]{1,0:T(8,128)} %param.13) | copy-start | bytes 1228804
  19.8 23.2 %copy-start.5 = (f32[1024]{0:T(1024)S(1)}, f32[1024]{0:T(1024)}, u32[]{:S(2)}) copy-start(f32[1024]{0:T(1024)} %param.14) | copy-start | bytes 12292
  23.5 19.5 %all-to-all-start = ((bf16[8,112,128]{2,1,0:T(8,128)(2,1)}), bf16[8,112,128]{2,1,0:T(8,128)(2,1)S(1)}, u32[]{:S(2)}, u32[]{:S(2)}) async-start(bf16[8,112,128]{2,1,0:T(8,128)(2,1)} %get-tuple-element.48), calls=%async_computation | async-start | bytes 458752 | tf_op jit(solution)/shard_map/all_to_all | solution.py:532
  45.1 14.4 %all-to-all-start.1 = ((bf16[8,112,128]{2,1,0:T(8,128)(2,1)}), bf16[8,112,128]{2,1,0:T(8,128)(2,1)S(1)}, u32[]{:S(2)}, u32[]{:S(2)}) async-start(bf16[8,112,128]{2,1,0:T(8,128)(2,1)} %pairs.1), calls=%async_computation.1 | async-start | bytes 458752 | tf_op jit(solution)/shard_map/all_to_all | solution.py:534
  59.6 18.1 %copy-start.1 = (bf16[1024,512]{1,0:T(8,128)(2,1)S(1)}, bf16[1024,512]{1,0:T(8,128)(2,1)}, u32[]{:S(2)}) copy-start(bf16[1024,512]{1,0:T(8,128)(2,1)} %get-tuple-element.56.edges_ref) | copy-start | bytes 3145732
  59.6 18.1 %copy-start.4 = (bf16[1024,1024]{1,0:T(8,128)(2,1)S(1)}, bf16[1024,1024]{1,0:T(8,128)(2,1)}, u32[]{:S(2)}) copy-start(bf16[1024,1024]{1,0:T(8,128)(2,1)} %mix_ref.1) | copy-start | bytes 6291460
  69.3 8.3 %copy-start.2 = (f32[1024,1]{1,0:T(8,128)S(1)}, f32[1024,1]{1,0:T(8,128)}, u32[]{:S(2)}) copy-start(f32[1024,1]{1,0:T(8,128)} %get-tuple-element.59.inv_ref) | copy-start | bytes 12292
  69.3 8.3 %copy-start.3 = (f32[1024]{0:T(1024)S(1)}, f32[1024]{0:T(1024)}, u32[]{:S(2)}) copy-start(f32[1024]{0:T(1024)} %param.10) | copy-start | bytes 12292
  69.3 2.9 %collective-permute-start.2 = (bf16[4,4,32,1152]{3,2,1,0:T(8,128)(2,1)S(1)}, bf16[4,4,32,1152]{3,2,1,0:T(8,128)(2,1)S(1)}, u32[]{:S(2)}, u32[]{:S(2)}) collective-permute-start(bf16[4,4,32,1152]{3,2,1,0:T(8,128)(2,1)S(1)} %get-tuple-element.55), channel_id=1, source_target_pairs={{0,1},{1,0},{2,3},{3,2},{4,5},{5,4},{6,7},{7,6},{8,9},{9,8},{10,11... | collective-permute-start | bytes 3538952 | tf_op jit(solution)/shard_map/ppermute | solution.py:498
  72.5 12.9 %collective-permute-start.3 = (bf16[4,32,1152]{2,1,0:T(8,128)(2,1)S(1)}, bf16[4,32,1152]{2,1,0:T(8,128)(2,1)S(1)}, u32[]{:S(2)}, u32[]{:S(2)}) collective-permute-start(bf16[4,32,1152]{2,1,0:T(8,128)(2,1)S(1)} %get-tuple-element.74), channel_id=1, source_target_pairs={{0,8},{1,9},{2,10},{3,11},{4,12},{5,13},{6,14},{7,15},{8,16},{9,17... | collective-permute-start | bytes 884744 | tf_op jit(solution)/shard_map/ppermute | solution.py:498
  74.1 11.4 %collective-permute-start.4 = (bf16[4,32,1152]{2,1,0:T(8,128)(2,1)S(1)}, bf16[4,32,1152]{2,1,0:T(8,128)(2,1)S(1)}, u32[]{:S(2)}, u32[]{:S(2)}) collective-permute-start(bf16[4,32,1152]{2,1,0:T(8,128)(2,1)S(1)} %get-tuple-element.73), channel_id=1, source_target_pairs={{0,16},{1,17},{2,18},{3,19},{4,20},{5,21},{6,22},{7,23},{8,24},{9,... | collective-permute-start | bytes 884744 | tf_op jit(solution)/shard_map/ppermute | solution.py:498
  75.1 15.1 %collective-permute-start.5 = (bf16[4,32,1152]{2,1,0:T(8,128)(2,1)S(1)}, bf16[4,32,1152]{2,1,0:T(8,128)(2,1)S(1)}, u32[]{:S(2)}, u32[]{:S(2)}) collective-permute-start(bf16[4,32,1152]{2,1,0:T(8,128)(2,1)S(1)} %get-tuple-element.72), channel_id=1, source_target_pairs={{0,24},{1,25},{2,26},{3,27},{4,28},{5,29},{6,30},{7,31},{8,0},{9,1... | collective-permute-start | bytes 884744 | tf_op jit(solution)/shard_map/ppermute | solution.py:498
  90.4 9.7 %collective-permute-start.8 = (bf16[32,1152]{1,0:T(8,128)(2,1)S(1)}, bf16[32,1152]{1,0:T(8,128)(2,1)S(1)}, u32[]{:S(2)}, u32[]{:S(2)}) collective-permute-start(bf16[32,1152]{1,0:T(8,128)(2,1)S(1)} %get-tuple-element.78), channel_id=1, source_target_pairs={{0,6},{1,7},{2,0},{3,1},{4,2},{5,3},{6,4},{7,5},{8,14},{9,15},{10,... | collective-permute-start | bytes 221192 | tf_op jit(solution)/shard_map/ppermute | solution.py:498
  93.8 7.6 %collective-permute-start.7 = (bf16[32,1152]{1,0:T(8,128)(2,1)S(1)}, bf16[32,1152]{1,0:T(8,128)(2,1)S(1)}, u32[]{:S(2)}, u32[]{:S(2)}) collective-permute-start(bf16[32,1152]{1,0:T(8,128)(2,1)S(1)} %get-tuple-element.79), channel_id=1, source_target_pairs={{0,4},{1,5},{2,6},{3,7},{4,0},{5,1},{6,2},{7,3},{8,12},{9,13},{10,... | collective-permute-start | bytes 221192 | tf_op jit(solution)/shard_map/ppermute | solution.py:498
  94.3 7.1 %collective-permute-start.6 = (bf16[32,1152]{1,0:T(8,128)(2,1)S(1)}, bf16[32,1152]{1,0:T(8,128)(2,1)S(1)}, u32[]{:S(2)}, u32[]{:S(2)}) collective-permute-start(bf16[32,1152]{1,0:T(8,128)(2,1)S(1)} %get-tuple-element.77), channel_id=1, source_target_pairs={{0,2},{1,3},{2,4},{3,5},{4,6},{5,7},{6,0},{7,1},{8,10},{9,11},{10,... | collective-permute-start | bytes 221192 | tf_op jit(solution)/shard_map/ppermute | solution.py:498
  96.0 9.3 %collective-permute-start.12 = (bf16[128,1024]{1,0:T(8,128)(2,1)S(1)}, bf16[128,1024]{1,0:T(8,128)(2,1)S(1)}, u32[]{:S(2)}, u32[]{:S(2)}) collective-permute-start(bf16[128,1024]{1,0:T(8,128)(2,1)S(1)} %get-tuple-element.65), channel_id=1, source_target_pairs={{0,1},{1,0},{2,3},{3,2},{4,5},{5,4},{6,7},{7,6},{8,9},{9,8},{10,11... | collective-permute-start | bytes 786440 | tf_op jit(solution)/shard_map/ppermute | solution.py:498
  96.0 11.3 %collective-permute-start.13 = (bf16[128,1024]{1,0:T(8,128)(2,1)S(1)}, bf16[128,1024]{1,0:T(8,128)(2,1)S(1)}, u32[]{:S(2)}, u32[]{:S(2)}) collective-permute-start(bf16[128,1024]{1,0:T(8,128)(2,1)S(1)} %get-tuple-element.66), channel_id=1, source_target_pairs={{1,2},{2,1},{3,4},{4,3},{5,6},{6,5},{7,8},{8,7},{9,10},{10,9},{11,... | collective-permute-start | bytes 786440 | tf_op jit(solution)/shard_map/ppermute | solution.py:498
  101.5 6.8 %collective-permute-start.9 = (bf16[32,1152]{1,0:T(8,128)(2,1)S(1)}, bf16[32,1152]{1,0:T(8,128)(2,1)S(1)}, u32[]{:S(2)}, u32[]{:S(2)}) collective-permute-start(bf16[32,1152]{1,0:T(8,128)(2,1)S(1)} %fusion.8), channel_id=1, source_target_pairs={{0,64},{32,96},{64,128},{96,160},{128,192},{160,224},{192,0},{224,... | collective-permute-start | bytes 221192 | tf_op jit(solution)/shard_map/ppermute | solution.py:498
  101.8 6.4 %collective-permute-start.10 = (bf16[32,1152]{1,0:T(8,128)(2,1)S(1)}, bf16[32,1152]{1,0:T(8,128)(2,1)S(1)}, u32[]{:S(2)}, u32[]{:S(2)}) collective-permute-start(bf16[32,1152]{1,0:T(8,128)(2,1)S(1)} %fusion.8), channel_id=1, source_target_pairs={{0,128},{32,160},{64,192},{96,224},{128,0},{160,32},{192,64},{224,... | collective-permute-start | bytes 221192 | tf_op jit(solution)/shard_map/ppermute | solution.py:498
  103.8 4.9 %collective-permute-start.11 = (bf16[32,1152]{1,0:T(8,128)(2,1)S(1)}, bf16[32,1152]{1,0:T(8,128)(2,1)S(1)}, u32[]{:S(2)}, u32[]{:S(2)}) collective-permute-start(bf16[32,1152]{1,0:T(8,128)(2,1)S(1)} %fusion.8), channel_id=1, source_target_pairs={{0,192},{32,224},{64,0},{96,32},{128,64},{160,96},{192,128},{224,1... | collective-permute-start | bytes 221192 | tf_op jit(solution)/shard_map/ppermute | solution.py:498
  108.8 8.7 %collective-permute-start.14 = (bf16[32,1152]{1,0:T(8,128)(2,1)S(1)}, bf16[32,1152]{1,0:T(8,128)(2,1)S(1)}, u32[]{:S(2)}, u32[]{:S(2)}) collective-permute-start(bf16[32,1152]{1,0:T(8,128)(2,1)S(1)} %add_convert_fusion.3), channel_id=1, source_target_pairs={{0,32},{32,0},{64,96},{96,64},{128,160},{160,128},{192,224},{224,1... | collective-permute-start | bytes 221192 | tf_op jit(solution)/shard_map/ppermute | solution.py:498
  (1 other events, 8.3 us)

commit v5 on v4

--- a/solution.py
+++ b/solution.py
@@ -56,7 +56,7 @@
     normed = (combined * inverse * gain).astype(bf16)
     normed_ref[...] = normed
     inv_ref[...] = inverse
-    x = jnp.dot(normed, mix, preferred_element_type=f32)
+    x = jnp.dot(normed, mix(), preferred_element_type=f32)
     square = x * x
     tanh = jnp.tanh(x * (root_two_pi + (root_two_pi * cubic) * square))
     half = 0.5 + 0.5 * tanh
@@ -75,10 +75,10 @@
 
 def interior_kernel(
     nb0_ref, nb1_ref, gain_ref, out_ref, lat_hbm, mix_hbm,
-    out_t_ref, ends_ref, mix_out, edges_ref, normed_ref, hidden_ref, deriv_ref, inv_ref, pred_ref,
+    out_t_ref, lat, mix, normed_ref, hidden_ref, deriv_ref, inv_ref, pred_ref,
     *refs,
 ):
-    send_ref, lat, mix, sems = refs
+    send_ref, sems = refs
     step = pl.program_id(0)
     copies = [
         pltpu.make_async_copy(
@@ -107,11 +107,10 @@
     neighbours = jnp.concatenate([nb0_ref[...], nb1_ref[...]], axis=1)
     base = lax.axis_index("space") * CELLS + first
     edges = edge_matrix(neighbours, base, BLK + 2 * HALO)
-    edges_ref[...] = edges
 
     @pl.when(step == 0)
     def _():
-        for copy in copies[0:2] + copies[STEPS:]:
+        for copy in copies[0:2]:
             copy.wait()
 
     @pl.when(step == 1)
@@ -121,25 +120,27 @@
     @pl.when(step == 2)
     def _():
         copies[3].wait()
+
+    def loaded_mix():
+        @pl.when(step == 0)
+        def _():
+            for copy in copies[STEPS:]:
+                copy.wait()
+
+        return mix[...]
 
     combined = gathered(edges, lat[pl.ds(first, BLK + 2 * HALO)])
     decode(
-        combined, gain_ref[...], mix[...], out_t_ref[...],
+        combined, gain_ref[...], loaded_mix, out_t_ref[...],
         normed_ref, hidden_ref, deriv_ref, inv_ref, pred_ref, send_ref,
     )
 
-    @pl.when(step == STEPS - 2)
-    def _():
-        ends_ref[0:BLK] = lat[0:BLK]
-        ends_ref[BLK:] = lat[CELLS - BLK :]
-        mix_out[...] = mix[...]
-
 
 def rim_cells_kernel(
-    nb0_ref, nb1_ref, ends_ref, near_ref, far_ref, gain_ref, mix_ref, out_t_ref,
+    nb0_ref, nb1_ref, lat_ref, near_ref, far_ref, gain_ref, mix_ref, out_t_ref,
     *refs,
 ):
-    edges_ref, *refs = refs[len(refs) // 2 :]
+    refs = refs[len(refs) // 2 :]
     space = lax.axis_index("space")
     start = space * CELLS
     first_core = lax.rem(space, 2) == 0
@@ -147,12 +148,10 @@
     high = jnp.where(first_core, near_ref[...], far_ref[...])
     last_edges = edge_matrix(nb0_ref[...], start + CELLS - BLK, BLK + HALO)
     head_edges = edge_matrix(nb1_ref[...], start - HALO, BLK + HALO)
-    edges_ref[0:HALO, 0 : BLK + HALO] = last_edges
-    edges_ref[HALO:, 0 : BLK + HALO] = head_edges
-    last = gathered(last_edges, jnp.concatenate([ends_ref[BLK:], high], axis=0))
-    head = gathered(head_edges, jnp.concatenate([low, ends_ref[0:BLK]], axis=0))
+    last = gathered(last_edges, jnp.concatenate([lat_ref[CELLS - BLK :], high], axis=0))
+    head = gathered(head_edges, jnp.concatenate([low, lat_ref[0:BLK]], axis=0))
     combined = jnp.concatenate([last, head], axis=0)
-    decode(combined, gain_ref[...], mix_ref[...], out_t_ref[...], *refs)
+    decode(combined, gain_ref[...], lambda: mix_ref[...], out_t_ref[...], *refs)
 
 
 def in_hbm(value):
@@ -161,7 +160,6 @@
 
 def forward(neighbours, center, near, far, gain, w_mix, w_out):
     shapes = [
-        pltpu.HBM((CELLS, BLK + 2 * HALO), bf16),
         pltpu.HBM((CELLS, D), bf16),
         pltpu.HBM((CELLS, D), bf16),
         pltpu.HBM((CELLS, D), bf16),
@@ -173,7 +171,6 @@
     def blocks(at):
         rows = pl.BlockSpec((BLK, D), lambda i: (at(i), 0))
         return [
-            pl.BlockSpec((BLK, BLK + 2 * HALO), lambda i: (at(i), 0)),
             rows,
             rows,
             rows,
@@ -191,7 +188,7 @@
         )
 
     neighbours, gain = in_hbm(neighbours), in_hbm(gain)
-    out_t, ends, mix, *arrays = pl.pallas_call(
+    out_t, lat, mix, *arrays = pl.pallas_call(
         interior_kernel,
         grid=(STEPS - 1,),
         in_specs=[
@@ -202,16 +199,14 @@
             pl.BlockSpec(memory_space=pltpu.HBM),
             pl.BlockSpec(memory_space=pltpu.HBM),
         ],
-        out_specs=[whole((ROWS, D)), whole((2 * BLK, D)), whole((D, D))] + blocks(lambda i: i),
+        out_specs=[pl.BlockSpec(memory_space=pltpu.VMEM)] * 3 + blocks(lambda i: i),
         out_shape=[
             jax.ShapeDtypeStruct((ROWS, D), bf16),
-            jax.ShapeDtypeStruct((2 * BLK, D), bf16),
+            jax.ShapeDtypeStruct((CELLS, D), bf16),
             jax.ShapeDtypeStruct((D, D), bf16),
         ]
         + shapes,
         scratch_shapes=[
-            pltpu.VMEM((CELLS, D), bf16),
-            pltpu.VMEM((D, D), bf16),
             pltpu.SemaphoreType.DMA((2 * STEPS,)),
         ],
         compiler_params=pltpu.CompilerParams(vmem_limit_bytes=VMEM_LIMIT),
@@ -224,12 +219,9 @@
         in_specs=[
             edges_at(lambda i: MEMBERS - 1),
             edges_at(lambda i: 0),
-            whole((2 * BLK, D)),
-            whole((HALO, D)),
-            whole((HALO, D)),
+            *[pl.BlockSpec(memory_space=pltpu.VMEM)] * 3,
             whole((1, D)),
-            whole((D, D)),
-            whole((ROWS, D)),
+            *[pl.BlockSpec(memory_space=pltpu.VMEM)] * 2,
         ]
         + [pl.BlockSpec(memory_space=pltpu.HBM)] * len(shapes),
         out_specs=blocks(lambda i: STEPS - 1),
@@ -238,7 +230,7 @@
         compiler_params=pltpu.CompilerParams(vmem_limit_bytes=VMEM_LIMIT),
         cost_estimate=cost(1),
         name="rim_cells",
-    )(neighbours, neighbours, ends, near, far, gain, mix, out_t, *arrays)
+    )(neighbours, neighbours, lat, near, far, gain, mix, out_t, *arrays)
     return out_t, mix, arrays
 
 
@@ -304,7 +296,8 @@
 
 
 def weights_kernel(
-    pos_ref, pair_ref, pred_ref, obs0_ref, obs1_ref, area0_ref, area1_ref, weight_ref, out_ref, deriv_ref, hidden_ref, normed_ref,
+    pos_ref, pair_ref, pred_ref, obs0_ref, obs1_ref, area0_ref, area1_ref, weight_ref, out_ref, deriv_ref,
+    hidden0_ref, hidden1_ref, normed0_ref, normed1_ref,
     g_ref, pre_ref, loss_ref, keep_ref, send_ref, pre_all, g_all,
 ):
     step = pl.program_id(0)
@@ -336,19 +329,20 @@
 
     @pl.when(step >= STEPS)
     def _():
-        mix = lax.dot_general(
-            normed_ref[...], pre_all[...], (((0,), (0,)), ((), ())), preferred_element_type=f32
-        ).astype(bf16)
-        out = jnp.dot(g_all[...], hidden_ref[...], preferred_element_type=f32)
-        out = jnp.concatenate([out, jnp.zeros((128 - ROWS, BLK), f32)], axis=0).T.astype(bf16)
         mine = pos_ref[2] == 0
-        for z in range(4):
-            at = lax.rem(z + 4 - pos_ref[1], 4)
-            for source, lanes in ((mix, slice(0, D)), (out, slice(D, WIDE))):
-                even = source[64 * z : 64 * z + 32]
-                odd = source[64 * z + 32 : 64 * z + 64]
-                keep_ref[0, at, :, lanes] = jnp.where(mine, even, odd)
-                send_ref[0, at, :, lanes] = jnp.where(mine, odd, even)
+        for x, hidden_ref, normed_ref in ((0, hidden0_ref, normed0_ref), (1, hidden1_ref, normed1_ref)):
+            mix = lax.dot_general(
+                normed_ref[...], pre_all[...], (((0,), (0,)), ((), ())), preferred_element_type=f32
+            ).astype(bf16)
+            out = jnp.dot(g_all[...], hidden_ref[...], preferred_element_type=f32)
+            out = jnp.concatenate([out, jnp.zeros((128 - ROWS, BLK), f32)], axis=0).T.astype(bf16)
+            for z in range(4):
+                at = lax.rem(z + 4 - pos_ref[1], 4)
+                for source, lanes in ((mix, slice(0, D)), (out, slice(D, WIDE))):
+                    even = source[64 * z : 64 * z + 32]
+                    odd = source[64 * z + 32 : 64 * z + 64]
+                    keep_ref[x, at, :, lanes] = jnp.where(mine, even, odd)
+                    send_ref[x, at, :, lanes] = jnp.where(mine, odd, even)
 
 
 def weight_parts(pos, pair, pred, observed, area, weight, w_out, deriv, hidden, normed):
@@ -356,15 +350,18 @@
     later = lambda i: jnp.maximum(i - STEPS, 0)
     rows = pl.BlockSpec((BLK, D), lambda i, pos: (first(i), 0))
     columns = pl.BlockSpec((ROWS, BLK), lambda i, pos: (0, first(i)))
-    features = pl.BlockSpec((CELLS, BLK), lambda i, pos: (0, lax.rem(pos[0] + later(i), 4)))
+    features = [
+        pl.BlockSpec((CELLS, BLK), lambda i, pos, k=k: (0, lax.rem(pos[0] + 2 * later(i) + k, 4)))
+        for k in (0, 1)
+    ]
     left = lambda i, pos: (0, 2 * first(i) + 1)
     right = lambda i, pos: (0, lax.rem(2 * first(i) + 2, MEMBERS))
-    share = pl.BlockSpec((1, 4, 32, WIDE), lambda i, pos: (later(i), 0, 0, 0))
+    share = pl.BlockSpec((2, 4, 32, WIDE), lambda i, pos: (later(i), 0, 0, 0))
     return pl.pallas_call(
         weights_kernel,
         grid_spec=pltpu.PrefetchScalarGridSpec(
             num_scalar_prefetch=1,
-            grid=(2 * STEPS,),
+            grid=(STEPS + 2,),
             in_specs=[
                 pl.BlockSpec((BLK // PIECE, ROWS, PIECE), lambda i, pos: (first(i), 0, 0)),
                 columns,
@@ -375,8 +372,8 @@
                 whole((ROWS, 1)),
                 whole((ROWS, D)),
                 rows,
-                features,
-                features,
+                *features,
+                *features,
             ],
             out_specs=[columns, rows, whole((1, CELLS)), share, share],
             scratch_shapes=[pltpu.VMEM((CELLS, D), bf16), pltpu.VMEM((ROWS, CELLS), bf16)],
@@ -395,12 +392,12 @@
         name="weights",
     )(
         pos, pair, in_hbm(pred), in_hbm(observed), in_hbm(observed), area, area, weight, w_out,
-        in_hbm(deriv), in_hbm(hidden), in_hbm(normed),
+        in_hbm(deriv), in_hbm(hidden), in_hbm(hidden), in_hbm(normed), in_hbm(normed),
     )
 
 
 def latent_kernel(
-    edges_ref, g_ref, out_ref, pre_ref, mix_ref, gain_ref, normed_ref, inv_ref,
+    nb0_ref, nb1_ref, g_ref, out_ref, pre_ref, mix_ref, gain_ref, normed_ref, inv_ref,
     grad_ref, near_ref, far_ref, carry, tail,
 ):
     step = pl.program_id(0)
@@ -416,6 +413,8 @@
     d_combined = d_hidden + inv_ref[...] * (d_normed * gain - normed * (1.0 / gain) * mean)
     d_combined = d_combined.astype(bf16)
 
+    start = lax.axis_index("space") * CELLS
+
     def spread(edges, cells):
         return (1.0 / NBRS) * lax.dot_general(
             edges, cells, (((0,), (0,)), ((), ())), preferred_element_type=f32
@@ -423,9 +422,11 @@
 
     @pl.when(step == 0)
     def _():
-        last = spread(edges_ref[0:HALO, 0 : BLK + HALO], d_combined[0:HALO])
+        edges = edge_matrix(nb0_ref[...], start + CELLS - BLK, BLK + HALO)
+        last = spread(edges, d_combined[0:HALO])
         tail[...] = last[0:BLK]
-        head = spread(edges_ref[HALO:, 0 : BLK + HALO], d_combined[HALO:])
+        edges = edge_matrix(nb1_ref[...], start - HALO, BLK + HALO)
+        head = spread(edges, d_combined[HALO:])
         carry[...] = head[HALO:]
         high, low = last[BLK:].astype(bf16), head[0:HALO].astype(bf16)
         first_core = lax.rem(lax.axis_index("space"), 2) == 0
@@ -435,7 +436,8 @@
     @pl.when(step > 0)
     def _():
         first = pl.multiple_of((step - 1) * BLK, BLK)
-        part = spread(edges_ref[...], d_combined)
+        neighbours = jnp.concatenate([nb0_ref[...], nb1_ref[...]], axis=1)
+        part = spread(edge_matrix(neighbours, start + first, BLK + 2 * HALO), d_combined)
         grad_ref[pl.ds(first, BLK)] = (part[0:BLK] + carry[...]).astype(bf16)
         carry[...] = part[BLK:]
 
@@ -444,7 +446,7 @@
         grad_ref[CELLS - BLK :] = (carry[...] + tail[...]).astype(bf16)
 
 
-def latent_parts(edges, g, w_out, d_pre, w_mix, gain, normed, inverse):
+def latent_parts(neighbours, g, w_out, d_pre, w_mix, gain, normed, inverse):
     at = lambda i: lax.rem(i + STEPS - 1, STEPS)
     rows = pl.BlockSpec((BLK, D), lambda i: (at(i), 0))
     rim = jax.ShapeDtypeStruct((HALO, D), bf16)
@@ -452,7 +454,8 @@
         latent_kernel,
         grid=(STEPS,),
         in_specs=[
-            pl.BlockSpec((BLK, BLK + 2 * HALO), lambda i: (at(i), 0)),
+            pl.BlockSpec((NBRS, PIECE), lambda i: (0, 2 * at(i) + 1)),
+            pl.BlockSpec((NBRS, PIECE), lambda i: (0, lax.rem(2 * at(i) + 2, MEMBERS))),
             pl.BlockSpec((ROWS, BLK), lambda i: (0, at(i))),
             whole((ROWS, D)),
             rows,
@@ -469,7 +472,7 @@
             flops=4 * CELLS * D * D, bytes_accessed=10 << 20, transcendentals=0
         ),
         name="latent",
-    )(edges, g, w_out, d_pre, w_mix, gain, normed, inverse)
+    )(neighbours, neighbours, g, w_out, d_pre, w_mix, gain, normed, inverse)
 
 
 def rim_kernel(grad_ref, near_ref, far_ref, out_ref):
@@ -528,7 +531,7 @@
     weight = jnp.pad(var_weight, (0, ROWS - VARS)).reshape(ROWS, 1)
 
     out_t, mix, arrays = forward(neighbours, center, near, far, gain, w_mix, w_out.T)
-    edges, normed, hidden, deriv, inverse, pred, pieces = arrays
+    normed, hidden, deriv, inverse, pred, pieces = arrays
     pieces = lax.all_to_all(pieces, "member", 0, 0, tiled=True)
     pairs = pair_terms(pieces, observed, area, weight)
     pairs = lax.all_to_all(pairs, "member", 0, 0, tiled=True)
@@ -537,15 +540,18 @@
     )
     got = along(send, "space", other_core)
 
-    def over_x(k):
-        return along(summed([keep[k], got[k]]).astype(bf16), "space", lambda i: (i + 8 * k) % 32)
-
-    arrived = [over_x(k) for k in (1, 2, 3)]
-    grad, near, far = latent_parts(edges, g, out_t, d_pre, w_mix, gain, normed, inverse)
+    def own(k):
+        return summed([keep[k], got[k]]).astype(bf16)
+
+    def over_x(k, value):
+        return along(value, "space", lambda i: (i + 8 * k) % 32)
+
+    arrived = [over_x(k, own(k)) for k in (1, 2, 3)]
+    grad, near, far = latent_parts(neighbours, g, out_t, d_pre, w_mix, gain, normed, inverse)
     arrived, grad = lax.optimization_barrier((arrived, grad))
     far = along(far, "space", other_chip)
     near = along(near, "space", other_core)
-    share = summed([keep[0], got[0]] + arrived).astype(bf16)
+    share = summed([own(0)] + arrived).astype(bf16)
 
     def over_z(k):
         return along(share[k], "space", lambda i: i // 8 * 8 + (i + 2 * k) % 8)

time: 119 us -> 118 us (level)
  waiting for transfers between devices: 39.5 us -> 37.7 us
    ppermute x15, waiting for transfers between devices: 18.4 us -> 16.6 us  [along(): lax.ppermute(value, axis, [pair for pair in pairs if pair[1] is not None])]
    pallas_call x1, Pallas kernels: 7.72 us -> 9.46 us  [latent_parts(): pl.pallas_call(latent_kernel, grid=(STEPS,), in_specs=[pl.BlockSpec((NBRS...]
  transfers between devices with their start and end apart: 17 -> 17, of which waited for: 10 -> 9; matrix products, arithmetic and copies ran while one was open for 1% -> 1% of each run, Pallas kernels for 18% -> 19%
where the time goes in v5:
time: 118 us; the launch traced here: 117 us
  starting transfers between devices  38.1 us (32%)
  waiting for transfers between devices  37.7 us (32%)
  Pallas kernels  36.7 us (31%)
  other arithmetic  2.92 us (2%)
    ppermute x15, starting transfers between devices, along(): lax.ppermute(value, axis, [pair for pair in pairs if pair[1] is not None])  26.3 us
    ppermute x15, waiting for transfers between devices, along(): lax.ppermute(value, axis, [pair for pair in pairs if pair[1] is not None])  16.6 us
    all_to_all x1, waiting for transfers between devices, shards(): pairs = lax.all_to_all(pairs, 'member', 0, 0, tiled=True)  10.9 us
    pallas_call x1, Pallas kernels, forward(): pl.pallas_call(interior_kernel, grid=(STEPS - 1,), in_specs=[edges_at(lam...  10.7 us
    all_to_all x1, waiting for transfers between devices, shards(): pieces = lax.all_to_all(pieces, 'member', 0, 0, tiled=True)  10.2 us
    pallas_call x1, Pallas kernels, latent_parts(): pl.pallas_call(latent_kernel, grid=(STEPS,), in_specs=[pl.BlockSpec((NBRS...  9.46 us
    pallas_call x1, Pallas kernels, weight_parts(): pl.pallas_call(weights_kernel, grid_spec=pltpu.PrefetchScalarGridSpec(num...  8.96 us
    all_to_all x1, starting transfers between devices, shards(): pieces = lax.all_to_all(pieces, 'member', 0, 0, tiled=True)  8.4 us
  transfers between devices with their start and end apart: 17, of which 9 were waited for; matrix products, arithmetic and copies ran while one was open for 1% of the time, Pallas kernels for 19%

profile of v5, /device:TPU:2, one launch (start us, length us, event | category | flops | bytes accessed | tf_op | source)
XLA Modules:
  0.0 117.3 jit_solution(4456561283004040091)
XLA Ops:
  1.8 6.6 %collective-permute-start.1 = (bf16[128,1024]{1,0:T(8,128)(2,1)S(1)}, bf16[128,1024]{1,0:T(8,128)(2,1)S(1)}, u32[]{:S(2)}, u32[]{:S(2)}) collective-permute-start(bf16[128,1024]{1,0:T(8,128)(2,1)S(1)} %get-tuple-element.71), channel_id=1, source_target_pairs={{1,2},{2,1},{3,4},{4,3},{5,6},{6,5},{7,8},{8,7},{9,10},{10,9},{11,... | collective-permute-start | bytes 786440 | tf_op jit(solution)/shard_map/ppermute | solution.py:501
  8.4 10.7 %interior.1 = (bf16[112,1024]{1,0:T(8,128)(2,1)S(1)}, bf16[1024,1024]{1,0:T(8,128)(2,1)S(1)}, bf16[1024,1024]{1,0:T(8,128)(2,1)S(1)}, bf16[1024,1024]{1,0:T(8,12...) custom-call(s32[4,1024]{1,0:T(4,128)} %nb1_ref.5, ...), custom_call_target="tpu_custom_call" | custom-call | flops 3221225472 | bytes 9437184 | tf_op jit(solution)/shard_map/interior/pallas_call | solution.py:191
  19.2 3.6 %rim_cells.1 = (bf16[1024,1024]{1,0:T(8,128)(2,1)}, bf16[1024,1024]{1,0:T(8,128)(2,1)}, bf16[1024,1024]{1,0:T(8,128)(2,1)}, f32[1024,1]{1,0:T(8,128)}, f32[112,1...) custom-call(s32[4,1024]{1,0:T(4,128)} %nb1_ref.5, ...), custom_call_target="tpu_custom_call", output_to_operand_aliasing={{0}: (8, {}), {1}: (9, {}), {2}: (10, {}), {3}: (11, {}), {... | custom-call | flops 1073741824 | bytes 3145728 | tf_op jit(solution)/shard_map/rim_cells/pallas_call | solution.py:216
  22.8 8.4 %all-to-all-start = ((bf16[8,112,128]{2,1,0:T(8,128)(2,1)}), bf16[8,112,128]{2,1,0:T(8,128)(2,1)S(1)}, u32[]{:S(2)}, u32[]{:S(2)}) async-start(bf16[8,112,128]{2,1,0:T(8,128)(2,1)} %get-tuple-element.45), calls=%async_computation | async-start | bytes 458752 | tf_op jit(solution)/shard_map/all_to_all | solution.py:535
  32.2 10.2 %all-to-all-done.pred_ref = bf16[8,112,128]{2,1,0:T(8,128)(2,1)S(1)} async-done(((bf16[8,112,128]{2,1,0:T(8,128)(2,1)}), bf16[8,112,128]{2,1,0:T(8,128)(2,1)S(1)}, u32[]{:S(2)}, u32[]{:S(2)}) %all-to-all-start) | async-done | bytes 229408 | tf_op jit(solution)/shard_map/all_to_all | solution.py:535
  42.3 2.1 %pairs.1 = bf16[8,112,128]{2,1,0:T(8,128)(2,1)} custom-call(bf16[8,112,128]{2,1,0:T(8,128)(2,1)S(1)} %all-to-all-done.pred_ref, f32[112,1024]{1,0:T(8,128)} %pad.8.obs_ref.obs0_ref.obs1_ref, f32[1,1024]{1,0:T(1,128)S(1)} %bitcast.37, f32[112,1]{1,0:T(8,128)S(1)} %copy.19.weight_ref), custom_call_target="tpu_custom_call" | custom-call | flops 16777216 | bytes 1048576 | tf_op jit(solution)/shard_map/pairs/pallas_call | solution.py:279
  44.5 3.4 %all-to-all-start.1 = ((bf16[8,112,128]{2,1,0:T(8,128)(2,1)}), bf16[8,112,128]{2,1,0:T(8,128)(2,1)S(1)}, u32[]{:S(2)}, u32[]{:S(2)}) async-start(bf16[8,112,128]{2,1,0:T(8,128)(2,1)} %pairs.1), calls=%async_computation.1 | async-start | bytes 458752 | tf_op jit(solution)/shard_map/all_to_all | solution.py:537
  48.0 10.9 %all-to-all-done.1.pair_ref = bf16[8,112,128]{2,1,0:T(8,128)(2,1)S(1)} async-done(((bf16[8,112,128]{2,1,0:T(8,128)(2,1)}), bf16[8,112,128]{2,1,0:T(8,128)(2,1)S(1)}, u32[]{:S(2)}, u32[]{:S(2)}) %all-to-all-start.1) | async-done | bytes 229408 | tf_op jit(solution)/shard_map/all_to_all | solution.py:537
  58.9 9.0 %weights.1 = (bf16[112,1024]{1,0:T(8,128)(2,1)S(1)}, bf16[1024,1024]{1,0:T(8,128)(2,1)S(1)}, f32[1,1024]{1,0:T(1,128)}, bf16[4,4,32,1152]{3,2,1,0:T(8,128)(2,1)S(1)}, bf16[4,4,32,1152]{3,2,1,0:T(8,128)(2,1)S(1)}) custom-call(s32[3]{0:T(128)S(1)} %pad_add_fusion.pos_ref, bf16[8,112,128]{2,1,0:T(8,128)(2,1)S(1)} %all-to-all-done.1.pair_ref, ...), custom_call_target="tpu_custom_call" | custom-call | flops 3221225472 | bytes 14680064 | tf_op jit(solution)/shard_map/weights/pallas_call | solution.py:360
  68.0 2.8 %collective-permute-done.2 = bf16[4,4,32,1152]{3,2,1,0:T(8,128)(2,1)S(1)} collective-permute-done((bf16[4,4,32,1152]{3,2,1,0:T(8,128)(2,1)S(1)}, bf16[4,4,32,1152]{3,2,1,0:T(8,128)(2,1)S(1)}, u32[]{:S(2)}, u32[]{:S(2)}) %collective-permute-start.2) | collective-permute-done | bytes 1179680 | tf_op jit(solution)/shard_map/ppermute | solution.py:501
  71.0 1.6 %collective-permute-start.3 = (bf16[4,32,1152]{2,1,0:T(8,128)(2,1)S(1)}, bf16[4,32,1152]{2,1,0:T(8,128)(2,1)S(1)}, u32[]{:S(2)}, u32[]{:S(2)}) collective-permute-start(bf16[4,32,1152]{2,1,0:T(8,128)(2,1)S(1)} %get-tuple-element.70), channel_id=1, source_target_pairs={{0,8},{1,9},{2,10},{3,11},{4,12},{5,13},{6,14},{7,15},{8,16},{9,17... | collective-permute-start | bytes 884744 | tf_op jit(solution)/shard_map/ppermute | solution.py:501
  72.6 1.1 collective-permute-start.4
  73.7 2.5 %collective-permute-start.5 = (bf16[4,32,1152]{2,1,0:T(8,128)(2,1)S(1)}, bf16[4,32,1152]{2,1,0:T(8,128)(2,1)S(1)}, u32[]{:S(2)}, u32[]{:S(2)}) collective-permute-start(bf16[4,32,1152]{2,1,0:T(8,128)(2,1)S(1)} %get-tuple-element.68), channel_id=1, source_target_pairs={{0,24},{1,25},{2,26},{3,27},{4,28},{5,29},{6,30},{7,31},{8,0},{9,1... | collective-permute-start | bytes 884744 | tf_op jit(solution)/shard_map/ppermute | solution.py:501
  76.2 9.5 %latent.1 = (bf16[1024,1024]{1,0:T(8,128)(2,1)}, bf16[128,1024]{1,0:T(8,128)(2,1)S(1)}, bf16[128,1024]{1,0:T(8,128)(2,1)S(1)}) custom-call(s32[4,1024]{1,0:T(4,128)S(1)} %copy-done.2, s32[4,1024]{1,0:T(4,128)S(1)} %copy-done.2, bf16[112,1024]{1,0:T(8,128)(2,1)S(1)} %get-tuple-element.53.g_ref, bf16[112,1024]{1,0:T(8,128)(2,1)S(1)} %get-tuple-element.38.out_t_ref.out_ref, ...), custom_call_target="tpu_custom_call" | custom-call | flops 4294967296 | bytes 10485760 | tf_op jit(solution)/shard_map/latent/pallas_call | solution.py:453
  85.7 3.1 %collective-permute-done.5 = bf16[4,32,1152]{2,1,0:T(8,128)(2,1)S(1)} collective-permute-done((bf16[4,32,1152]{2,1,0:T(8,128)(2,1)S(1)}, bf16[4,32,1152]{2,1,0:T(8,128)(2,1)S(1)}, u32[]{:S(2)}, u32[]{:S(2)}) %collective-permute-start.5) | collective-permute-done | bytes 294944 | tf_op jit(solution)/shard_map/ppermute | solution.py:501
  89.0 3.3 %collective-permute-start.8 = (bf16[32,1152]{1,0:T(8,128)(2,1)S(1)}, bf16[32,1152]{1,0:T(8,128)(2,1)S(1)}, u32[]{:S(2)}, u32[]{:S(2)}) collective-permute-start(bf16[32,1152]{1,0:T(8,128)(2,1)S(1)} %get-tuple-element.74), channel_id=1, source_target_pairs={{0,6},{1,7},{2,0},{3,1},{4,2},{5,3},{6,4},{7,5},{8,14},{9,15},{10,... | collective-permute-start | bytes 221192 | tf_op jit(solution)/shard_map/ppermute | solution.py:501
  92.9 1.7 %collective-permute-start.6 = (bf16[32,1152]{1,0:T(8,128)(2,1)S(1)}, bf16[32,1152]{1,0:T(8,128)(2,1)S(1)}, u32[]{:S(2)}, u32[]{:S(2)}) collective-permute-start(bf16[32,1152]{1,0:T(8,128)(2,1)S(1)} %get-tuple-element.73), channel_id=1, source_target_pairs={{0,2},{1,3},{2,4},{3,5},{4,6},{5,7},{6,0},{7,1},{8,10},{9,11},{10,... | collective-permute-start | bytes 221192 | tf_op jit(solution)/shard_map/ppermute | solution.py:501
  94.6 4.1 %collective-permute-start.13 = (bf16[128,1024]{1,0:T(8,128)(2,1)S(1)}, bf16[128,1024]{1,0:T(8,128)(2,1)S(1)}, u32[]{:S(2)}, u32[]{:S(2)}) collective-permute-start(bf16[128,1024]{1,0:T(8,128)(2,1)S(1)} %get-tuple-element.62), channel_id=1, source_target_pairs={{1,2},{2,1},{3,4},{4,3},{5,6},{6,5},{7,8},{8,7},{9,10},{10,9},{11,... | collective-permute-start | bytes 786440 | tf_op jit(solution)/shard_map/ppermute | solution.py:501
  98.7 1.2 %collective-permute-done.7 = bf16[32,1152]{1,0:T(8,128)(2,1)S(1)} collective-permute-done((bf16[32,1152]{1,0:T(8,128)(2,1)S(1)}, bf16[32,1152]{1,0:T(8,128)(2,1)S(1)}, u32[]{:S(2)}, u32[]{:S(2)}) %collective-permute-start.7) | collective-permute-done | bytes 73760 | tf_op jit(solution)/shard_map/ppermute | solution.py:501
  100.3 2.1 %collective-permute-start.10 = (bf16[32,1152]{1,0:T(8,128)(2,1)S(1)}, bf16[32,1152]{1,0:T(8,128)(2,1)S(1)}, u32[]{:S(2)}, u32[]{:S(2)}) collective-permute-start(bf16[32,1152]{1,0:T(8,128)(2,1)S(1)} %fusion.9), channel_id=1, source_target_pairs={{0,128},{32,160},{64,192},{96,224},{128,0},{160,32},{192,64},{224,... | collective-permute-start | bytes 221192 | tf_op jit(solution)/shard_map/ppermute | solution.py:501
  102.4 1.5 %collective-permute-start.11 = (bf16[32,1152]{1,0:T(8,128)(2,1)S(1)}, bf16[32,1152]{1,0:T(8,128)(2,1)S(1)}, u32[]{:S(2)}, u32[]{:S(2)}) collective-permute-start(bf16[32,1152]{1,0:T(8,128)(2,1)S(1)} %fusion.9), channel_id=1, source_target_pairs={{0,192},{32,224},{64,0},{96,32},{128,64},{160,96},{192,128},{224,1... | collective-permute-start | bytes 221192 | tf_op jit(solution)/shard_map/ppermute | solution.py:501
  103.9 2.0 %collective-permute-done.13.far_ref = bf16[128,1024]{1,0:T(8,128)(2,1)S(1)} collective-permute-done((bf16[128,1024]{1,0:T(8,128)(2,1)S(1)}, bf16[128,1024]{1,0:T(8,128)(2,1)S(1)}, u32[]{:S(2)}, u32[]{:S(2)}) %collective-permute-start.13) | collective-permute-done | bytes 262176 | tf_op jit(solution)/shard_map/ppermute | solution.py:501
  108.1 1.8 %rims.1 = bf16[1024,1024]{1,0:T(8,128)(2,1)} custom-call(bf16[1024,1024]{1,0:T(8,128)(2,1)} %get-tuple-element.57.grad_ref, bf16[128,1024]{1,0:T(8,128)(2,1)S(1)} %collective-permute-done.12.near_ref, bf16[128,1024]{1,0:T(8,128)(2,1)S(1)} %collective-permute-done.13.far_ref), custom_call_target="tpu_custom_call", output_to_operand_aliasing={{}: (0, {})} | custom-call | flops 262144 | bytes 1572864 | tf_op jit(solution)/shard_map/rims/pallas_call | solution.py:486
  109.9 6.1 %collective-permute-done.14 = bf16[32,1152]{1,0:T(8,128)(2,1)S(1)} collective-permute-done((bf16[32,1152]{1,0:T(8,128)(2,1)S(1)}, bf16[32,1152]{1,0:T(8,128)(2,1)S(1)}, u32[]{:S(2)}, u32[]{:S(2)}) %collective-permute-start.14) | collective-permute-done | bytes 73760 | tf_op jit(solution)/shard_map/ppermute | solution.py:501
  (45 shorter events, 7.2 us)
Async XLA Ops:
  1.7 17.4 %collective-permute-start = (bf16[128,1024]{1,0:T(8,128)(2,1)S(1)}, bf16[128,1024]{1,0:T(8,128)(2,1)S(1)}, u32[]{:S(2)}, u32[]{:S(2)}) collective-permute-start(bf16[128,1024]{1,0:T(8,128)(2,1)S(1)} %get-tuple-element.72), channel_id=1, source_target_pairs={{0,1},{1,0},{2,3},{3,2},{4,5},{5,4},{6,7},{7,6},{8,9},{9,8},{10,11... | collective-permute-start | bytes 786440 | tf_op jit(solution)/shard_map/ppermute | solution.py:501
  1.8 17.3 %collective-permute-start.1 = (bf16[128,1024]{1,0:T(8,128)(2,1)S(1)}, bf16[128,1024]{1,0:T(8,128)(2,1)S(1)}, u32[]{:S(2)}, u32[]{:S(2)}) collective-permute-start(bf16[128,1024]{1,0:T(8,128)(2,1)S(1)} %get-tuple-element.71), channel_id=1, source_target_pairs={{1,2},{2,1},{3,4},{4,3},{5,6},{6,5},{7,8},{8,7},{9,10},{10,9},{11,... | collective-permute-start | bytes 786440 | tf_op jit(solution)/shard_map/ppermute | solution.py:501
  19.1 12.1 %copy-start.7 = (f32[100]{0:T(128)S(1)}, f32[100]{0:T(128)}, u32[]{:S(2)}) copy-start(f32[100]{0:T(128)} %param.15) | copy-start | bytes 1204
  19.2 12.2 %copy-start.6 = (f32[100,1024]{1,0:T(8,128)S(1)}, f32[100,1024]{1,0:T(8,128)}, u32[]{:S(2)}) copy-start(f32[100,1024]{1,0:T(8,128)} %param.13) | copy-start | bytes 1228804
  19.2 23.2 %copy-start.3 = (f32[1024]{0:T(1024)S(1)}, f32[1024]{0:T(1024)}, u32[]{:S(2)}) copy-start(f32[1024]{0:T(1024)} %param.14) | copy-start | bytes 12292
  22.8 19.5 %all-to-all-start = ((bf16[8,112,128]{2,1,0:T(8,128)(2,1)}), bf16[8,112,128]{2,1,0:T(8,128)(2,1)S(1)}, u32[]{:S(2)}, u32[]{:S(2)}) async-start(bf16[8,112,128]{2,1,0:T(8,128)(2,1)} %get-tuple-element.45), calls=%async_computation | async-start | bytes 458752 | tf_op jit(solution)/shard_map/all_to_all | solution.py:535
  44.5 14.4 %all-to-all-start.1 = ((bf16[8,112,128]{2,1,0:T(8,128)(2,1)}), bf16[8,112,128]{2,1,0:T(8,128)(2,1)S(1)}, u32[]{:S(2)}, u32[]{:S(2)}) async-start(bf16[8,112,128]{2,1,0:T(8,128)(2,1)} %pairs.1), calls=%async_computation.1 | async-start | bytes 458752 | tf_op jit(solution)/shard_map/all_to_all | solution.py:537
  58.9 17.3 %copy-start.5 = (bf16[1024,1024]{1,0:T(8,128)(2,1)S(1)}, bf16[1024,1024]{1,0:T(8,128)(2,1)}, u32[]{:S(2)}) copy-start(bf16[1024,1024]{1,0:T(8,128)(2,1)} %mix_ref.1) | copy-start | bytes 6291460
  67.9 8.4 %copy-start = (bf16[1024,1024]{1,0:T(8,128)(2,1)S(1)}, bf16[1024,1024]{1,0:T(8,128)(2,1)}, u32[]{:S(2)}) copy-start(bf16[1024,1024]{1,0:T(8,128)(2,1)} %get-tuple-element.49.normed0_ref.normed1_ref.normed_ref) | copy-start | bytes 6291460
  67.9 8.4 %copy-start.1 = (f32[1024,1]{1,0:T(8,128)S(1)}, f32[1024,1]{1,0:T(8,128)}, u32[]{:S(2)}) copy-start(f32[1024,1]{1,0:T(8,128)} %get-tuple-element.55.inv_ref) | copy-start | bytes 12292
  67.9 8.4 %copy-start.2 = (s32[4,1024]{1,0:T(4,128)S(1)}, s32[4,1024]{1,0:T(4,128)}, u32[]{:S(2)}) copy-start(s32[4,1024]{1,0:T(4,128)} %nb1_ref.5) | copy-start | bytes 49156
  67.9 2.9 %collective-permute-start.2 = (bf16[4,4,32,1152]{3,2,1,0:T(8,128)(2,1)S(1)}, bf16[4,4,32,1152]{3,2,1,0:T(8,128)(2,1)S(1)}, u32[]{:S(2)}, u32[]{:S(2)}) collective-permute-start(bf16[4,4,32,1152]{3,2,1,0:T(8,128)(2,1)S(1)} %get-tuple-element.52), channel_id=1, source_target_pairs={{0,1},{1,0},{2,3},{3,2},{4,5},{5,4},{6,7},{7,6},{8,9},{9,8},{10,11... | collective-permute-start | bytes 3538952 | tf_op jit(solution)/shard_map/ppermute | solution.py:501
  71.0 14.7 %collective-permute-start.3 = (bf16[4,32,1152]{2,1,0:T(8,128)(2,1)S(1)}, bf16[4,32,1152]{2,1,0:T(8,128)(2,1)S(1)}, u32[]{:S(2)}, u32[]{:S(2)}) collective-permute-start(bf16[4,32,1152]{2,1,0:T(8,128)(2,1)S(1)} %get-tuple-element.70), channel_id=1, source_target_pairs={{0,8},{1,9},{2,10},{3,11},{4,12},{5,13},{6,14},{7,15},{8,16},{9,17... | collective-permute-start | bytes 884744 | tf_op jit(solution)/shard_map/ppermute | solution.py:501
  72.6 13.1 %collective-permute-start.4 = (bf16[4,32,1152]{2,1,0:T(8,128)(2,1)S(1)}, bf16[4,32,1152]{2,1,0:T(8,128)(2,1)S(1)}, u32[]{:S(2)}, u32[]{:S(2)}) collective-permute-start(bf16[4,32,1152]{2,1,0:T(8,128)(2,1)S(1)} %get-tuple-element.69), channel_id=1, source_target_pairs={{0,16},{1,17},{2,18},{3,19},{4,20},{5,21},{6,22},{7,23},{8,24},{9,... | collective-permute-start | bytes 884744 | tf_op jit(solution)/shard_map/ppermute | solution.py:501
  73.7 15.1 %collective-permute-start.5 = (bf16[4,32,1152]{2,1,0:T(8,128)(2,1)S(1)}, bf16[4,32,1152]{2,1,0:T(8,128)(2,1)S(1)}, u32[]{:S(2)}, u32[]{:S(2)}) collective-permute-start(bf16[4,32,1152]{2,1,0:T(8,128)(2,1)S(1)} %get-tuple-element.68), channel_id=1, source_target_pairs={{0,24},{1,25},{2,26},{3,27},{4,28},{5,29},{6,30},{7,31},{8,0},{9,1... | collective-permute-start | bytes 884744 | tf_op jit(solution)/shard_map/ppermute | solution.py:501
  89.0 9.7 %collective-permute-start.8 = (bf16[32,1152]{1,0:T(8,128)(2,1)S(1)}, bf16[32,1152]{1,0:T(8,128)(2,1)S(1)}, u32[]{:S(2)}, u32[]{:S(2)}) collective-permute-start(bf16[32,1152]{1,0:T(8,128)(2,1)S(1)} %get-tuple-element.74), channel_id=1, source_target_pairs={{0,6},{1,7},{2,0},{3,1},{4,2},{5,3},{6,4},{7,5},{8,14},{9,15},{10,... | collective-permute-start | bytes 221192 | tf_op jit(solution)/shard_map/ppermute | solution.py:501
  92.3 7.6 %collective-permute-start.7 = (bf16[32,1152]{1,0:T(8,128)(2,1)S(1)}, bf16[32,1152]{1,0:T(8,128)(2,1)S(1)}, u32[]{:S(2)}, u32[]{:S(2)}) collective-permute-start(bf16[32,1152]{1,0:T(8,128)(2,1)S(1)} %get-tuple-element.75), channel_id=1, source_target_pairs={{0,4},{1,5},{2,6},{3,7},{4,0},{5,1},{6,2},{7,3},{8,12},{9,13},{10,... | collective-permute-start | bytes 221192 | tf_op jit(solution)/shard_map/ppermute | solution.py:501
  92.9 7.1 %collective-permute-start.6 = (bf16[32,1152]{1,0:T(8,128)(2,1)S(1)}, bf16[32,1152]{1,0:T(8,128)(2,1)S(1)}, u32[]{:S(2)}, u32[]{:S(2)}) collective-permute-start(bf16[32,1152]{1,0:T(8,128)(2,1)S(1)} %get-tuple-element.73), channel_id=1, source_target_pairs={{0,2},{1,3},{2,4},{3,5},{4,6},{5,7},{6,0},{7,1},{8,10},{9,11},{10,... | collective-permute-start | bytes 221192 | tf_op jit(solution)/shard_map/ppermute | solution.py:501
  94.6 9.3 %collective-permute-start.12 = (bf16[128,1024]{1,0:T(8,128)(2,1)S(1)}, bf16[128,1024]{1,0:T(8,128)(2,1)S(1)}, u32[]{:S(2)}, u32[]{:S(2)}) collective-permute-start(bf16[128,1024]{1,0:T(8,128)(2,1)S(1)} %get-tuple-element.61), channel_id=1, source_target_pairs={{0,1},{1,0},{2,3},{3,2},{4,5},{5,4},{6,7},{7,6},{8,9},{9,8},{10,11... | collective-permute-start | bytes 786440 | tf_op jit(solution)/shard_map/ppermute | solution.py:501
  94.6 11.3 %collective-permute-start.13 = (bf16[128,1024]{1,0:T(8,128)(2,1)S(1)}, bf16[128,1024]{1,0:T(8,128)(2,1)S(1)}, u32[]{:S(2)}, u32[]{:S(2)}) collective-permute-start(bf16[128,1024]{1,0:T(8,128)(2,1)S(1)} %get-tuple-element.62), channel_id=1, source_target_pairs={{1,2},{2,1},{3,4},{4,3},{5,6},{6,5},{7,8},{8,7},{9,10},{10,9},{11,... | collective-permute-start | bytes 786440 | tf_op jit(solution)/shard_map/ppermute | solution.py:501
  100.0 6.7 %collective-permute-start.9 = (bf16[32,1152]{1,0:T(8,128)(2,1)S(1)}, bf16[32,1152]{1,0:T(8,128)(2,1)S(1)}, u32[]{:S(2)}, u32[]{:S(2)}) collective-permute-start(bf16[32,1152]{1,0:T(8,128)(2,1)S(1)} %fusion.9), channel_id=1, source_target_pairs={{0,64},{32,96},{64,128},{96,160},{128,192},{160,224},{192,0},{224,... | collective-permute-start | bytes 221192 | tf_op jit(solution)/shard_map/ppermute | solution.py:501
  100.3 6.4 %collective-permute-start.10 = (bf16[32,1152]{1,0:T(8,128)(2,1)S(1)}, bf16[32,1152]{1,0:T(8,128)(2,1)S(1)}, u32[]{:S(2)}, u32[]{:S(2)}) collective-permute-start(bf16[32,1152]{1,0:T(8,128)(2,1)S(1)} %fusion.9), channel_id=1, source_target_pairs={{0,128},{32,160},{64,192},{96,224},{128,0},{160,32},{192,64},{224,... | collective-permute-start | bytes 221192 | tf_op jit(solution)/shard_map/ppermute | solution.py:501
  102.4 4.9 %collective-permute-start.11 = (bf16[32,1152]{1,0:T(8,128)(2,1)S(1)}, bf16[32,1152]{1,0:T(8,128)(2,1)S(1)}, u32[]{:S(2)}, u32[]{:S(2)}) collective-permute-start(bf16[32,1152]{1,0:T(8,128)(2,1)S(1)} %fusion.9), channel_id=1, source_target_pairs={{0,192},{32,224},{64,0},{96,32},{128,64},{160,96},{192,128},{224,1... | collective-permute-start | bytes 221192 | tf_op jit(solution)/shard_map/ppermute | solution.py:501
  107.4 8.7 %collective-permute-start.14 = (bf16[32,1152]{1,0:T(8,128)(2,1)S(1)}, bf16[32,1152]{1,0:T(8,128)(2,1)S(1)}, u32[]{:S(2)}, u32[]{:S(2)}) collective-permute-start(bf16[32,1152]{1,0:T(8,128)(2,1)S(1)} %add_convert_fusion.4), channel_id=1, source_target_pairs={{0,32},{32,0},{64,96},{96,64},{128,160},{160,128},{192,224},{224,1... | collective-permute-start | bytes 221192 | tf_op jit(solution)/shard_map/ppermute | solution.py:501
  (1 other events, 8.3 us)

commit v6 on v5

--- a/solution.py
+++ b/solution.py
@@ -16,6 +16,8 @@
 CELLS = 1024
 BLK = 256
 STEPS = CELLS // BLK
+HALF = 2 * BLK
+HALVES = CELLS // HALF
 PIECE = CELLS // MEMBERS
 WIDE = D + 128
 
@@ -296,21 +298,24 @@
 
 
 def weights_kernel(
-    pos_ref, pair_ref, pred_ref, obs0_ref, obs1_ref, area0_ref, area1_ref, weight_ref, out_ref, deriv_ref,
+    pos_ref, pair_ref, pred_ref, obs0_ref, obs1_ref, obs2_ref, obs3_ref,
+    area0_ref, area1_ref, area2_ref, area3_ref, weight_ref, out_ref, deriv_ref,
     hidden0_ref, hidden1_ref, normed0_ref, normed1_ref,
     g_ref, pre_ref, loss_ref, keep_ref, send_ref, pre_all, g_all,
 ):
     step = pl.program_id(0)
 
-    @pl.when(step < STEPS)
-    def _():
-        pair = jnp.concatenate([pair_ref[j] for j in range(BLK // PIECE)], axis=1).astype(f32)
+    @pl.when(step < HALVES)
+    def _():
+        pair = jnp.concatenate([pair_ref[j] for j in range(HALF // PIECE)], axis=1).astype(f32)
         loss = jnp.sum(pair[VARS : VARS + 3], axis=0, keepdims=True)
-        for j in range(BLK // PIECE):
-            at = lax.rem(2 * step + 1 + j, MEMBERS) * PIECE
+        for j in range(HALF // PIECE):
+            at = lax.rem(HALF // PIECE * step + 1 + j, MEMBERS) * PIECE
             loss_ref[:, pl.ds(pl.multiple_of(at, PIECE), PIECE)] = loss[:, j * PIECE : (j + 1) * PIECE]
-        area = jnp.concatenate([area0_ref[...], area1_ref[...]], axis=1)
-        gap = pred_ref[...] - jnp.concatenate([obs0_ref[...], obs1_ref[...]], axis=1)
+        areas = (area0_ref, area1_ref, area2_ref, area3_ref)
+        area = jnp.concatenate([ref[...] for ref in areas], axis=1)
+        observed = (obs0_ref, obs1_ref, obs2_ref, obs3_ref)
+        gap = pred_ref[...] - jnp.concatenate([ref[...] for ref in observed], axis=1)
         slope = gap * lax.rsqrt(gap * gap + smoothing * smoothing)
         g = (
             weight_ref[...]
@@ -323,11 +328,11 @@
         )
         d_pre = (d_hidden * deriv_ref[...].astype(f32)).astype(bf16)
         pre_ref[...] = d_pre
-        rows = pl.ds(pl.multiple_of(step * BLK, BLK), BLK)
+        rows = pl.ds(pl.multiple_of(step * HALF, HALF), HALF)
         pre_all[rows] = d_pre
         g_all[:, rows] = g
 
-    @pl.when(step >= STEPS)
+    @pl.when(step >= HALVES)
     def _():
         mine = pos_ref[2] == 0
         for x, hidden_ref, normed_ref in ((0, hidden0_ref, normed0_ref), (1, hidden1_ref, normed1_ref)):
@@ -346,29 +351,29 @@
 
 
 def weight_parts(pos, pair, pred, observed, area, weight, w_out, deriv, hidden, normed):
-    first = lambda i: jnp.minimum(i, STEPS - 1)
-    later = lambda i: jnp.maximum(i - STEPS, 0)
-    rows = pl.BlockSpec((BLK, D), lambda i, pos: (first(i), 0))
-    columns = pl.BlockSpec((ROWS, BLK), lambda i, pos: (0, first(i)))
+    first = lambda i: jnp.minimum(i, HALVES - 1)
+    later = lambda i: jnp.maximum(i - HALVES, 0)
+    rows = pl.BlockSpec((HALF, D), lambda i, pos: (first(i), 0))
+    columns = pl.BlockSpec((ROWS, HALF), lambda i, pos: (0, first(i)))
     features = [
         pl.BlockSpec((CELLS, BLK), lambda i, pos, k=k: (0, lax.rem(pos[0] + 2 * later(i) + k, 4)))
         for k in (0, 1)
     ]
-    left = lambda i, pos: (0, 2 * first(i) + 1)
-    right = lambda i, pos: (0, lax.rem(2 * first(i) + 2, MEMBERS))
+    pieces = HALF // PIECE
+    places = [
+        lambda i, pos, k=k: (0, lax.rem(pieces * first(i) + 1 + k, MEMBERS)) for k in range(pieces)
+    ]
     share = pl.BlockSpec((2, 4, 32, WIDE), lambda i, pos: (later(i), 0, 0, 0))
     return pl.pallas_call(
         weights_kernel,
         grid_spec=pltpu.PrefetchScalarGridSpec(
             num_scalar_prefetch=1,
-            grid=(STEPS + 2,),
+            grid=(HALVES + 2,),
             in_specs=[
-                pl.BlockSpec((BLK // PIECE, ROWS, PIECE), lambda i, pos: (first(i), 0, 0)),
+                pl.BlockSpec((pieces, ROWS, PIECE), lambda i, pos: (first(i), 0, 0)),
                 columns,
-                pl.BlockSpec((ROWS, PIECE), left),
-                pl.BlockSpec((ROWS, PIECE), right),
-                pl.BlockSpec((1, PIECE), left),
-                pl.BlockSpec((1, PIECE), right),
+                *[pl.BlockSpec((ROWS, PIECE), place) for place in places],
+                *[pl.BlockSpec((1, PIECE), place) for place in places],
                 whole((ROWS, 1)),
                 whole((ROWS, D)),
                 rows,
@@ -391,7 +396,7 @@
         ),
         name="weights",
     )(
-        pos, pair, in_hbm(pred), in_hbm(observed), in_hbm(observed), area, area, weight, w_out,
+        pos, pair, in_hbm(pred), *[in_hbm(observed)] * pieces, *[area] * pieces, weight, w_out,
         in_hbm(deriv), in_hbm(hidden), in_hbm(hidden), in_hbm(normed), in_hbm(normed),
     )
 

time: 118 us -> 117 us (level)
  no operation moved by 1% of the time
where the time goes in v6:
time: 117 us; the launch traced here: 116 us
  starting transfers between devices  38 us (32%)
  waiting for transfers between devices  37.8 us (32%)
  Pallas kernels  35.9 us (31%)
  other arithmetic  2.92 us (2%)
    ppermute x15, starting transfers between devices, along(): lax.ppermute(value, axis, [pair for pair in pairs if pair[1] is not None])  26.2 us
    ppermute x15, waiting for transfers between devices, along(): lax.ppermute(value, axis, [pair for pair in pairs if pair[1] is not None])  16.7 us
    all_to_all x1, waiting for transfers between devices, shards(): pairs = lax.all_to_all(pairs, 'member', 0, 0, tiled=True)  10.9 us
    pallas_call x1, Pallas kernels, forward(): pl.pallas_call(interior_kernel, grid=(STEPS - 1,), in_specs=[edges_at(lam...  10.7 us
    all_to_all x1, waiting for transfers between devices, shards(): pieces = lax.all_to_all(pieces, 'member', 0, 0, tiled=True)  10.2 us
    pallas_call x1, Pallas kernels, latent_parts(): pl.pallas_call(latent_kernel, grid=(STEPS,), in_specs=[pl.BlockSpec((NBRS...  9.46 us
    all_to_all x1, starting transfers between devices, shards(): pieces = lax.all_to_all(pieces, 'member', 0, 0, tiled=True)  8.4 us
    pallas_call x1, Pallas kernels, weight_parts(): pl.pallas_call(weights_kernel, grid_spec=pltpu.PrefetchScalarGridSpec(num...  8.1 us
  transfers between devices with their start and end apart: 17, of which 9 were waited for; matrix products, arithmetic and copies ran while one was open for 1% of the time, Pallas kernels for 19%

profile of v6, /device:TPU:2, one launch (start us, length us, event | category | flops | bytes accessed | tf_op | source)
XLA Modules:
  0.0 116.4 jit_solution(6429658639660605521)
XLA Ops:
  0.6 1.1 select_bitcast_fusion
  1.8 6.6 %collective-permute-start.1 = (bf16[128,1024]{1,0:T(8,128)(2,1)S(1)}, bf16[128,1024]{1,0:T(8,128)(2,1)S(1)}, u32[]{:S(2)}, u32[]{:S(2)}) collective-permute-start(bf16[128,1024]{1,0:T(8,128)(2,1)S(1)} %get-tuple-element.71), channel_id=1, source_target_pairs={{1,2},{2,1},{3,4},{4,3},{5,6},{6,5},{7,8},{8,7},{9,10},{10,9},{11,... | collective-permute-start | bytes 786440 | tf_op jit(solution)/shard_map/ppermute | solution.py:506
  8.4 10.7 %interior.1 = (bf16[112,1024]{1,0:T(8,128)(2,1)S(1)}, bf16[1024,1024]{1,0:T(8,128)(2,1)S(1)}, bf16[1024,1024]{1,0:T(8,128)(2,1)S(1)}, bf16[1024,1024]{1,0:T(8,12...) custom-call(s32[4,1024]{1,0:T(4,128)} %nb1_ref.5, ...), custom_call_target="tpu_custom_call" | custom-call | flops 3221225472 | bytes 9437184 | tf_op jit(solution)/shard_map/interior/pallas_call | solution.py:193
  19.2 3.6 %rim_cells.1 = (bf16[1024,1024]{1,0:T(8,128)(2,1)}, bf16[1024,1024]{1,0:T(8,128)(2,1)}, bf16[1024,1024]{1,0:T(8,128)(2,1)}, f32[1024,1]{1,0:T(8,128)}, f32[112,1...) custom-call(s32[4,1024]{1,0:T(4,128)} %nb1_ref.5, ...), custom_call_target="tpu_custom_call", output_to_operand_aliasing={{0}: (8, {}), {1}: (9, {}), {2}: (10, {}), {3}: (11, {}), {... | custom-call | flops 1073741824 | bytes 3145728 | tf_op jit(solution)/shard_map/rim_cells/pallas_call | solution.py:218
  22.8 8.4 %all-to-all-start = ((bf16[8,112,128]{2,1,0:T(8,128)(2,1)}), bf16[8,112,128]{2,1,0:T(8,128)(2,1)S(1)}, u32[]{:S(2)}, u32[]{:S(2)}) async-start(bf16[8,112,128]{2,1,0:T(8,128)(2,1)} %get-tuple-element.45), calls=%async_computation | async-start | bytes 458752 | tf_op jit(solution)/shard_map/all_to_all | solution.py:540
  32.2 10.2 %all-to-all-done.pred_ref = bf16[8,112,128]{2,1,0:T(8,128)(2,1)S(1)} async-done(((bf16[8,112,128]{2,1,0:T(8,128)(2,1)}), bf16[8,112,128]{2,1,0:T(8,128)(2,1)S(1)}, u32[]{:S(2)}, u32[]{:S(2)}) %all-to-all-start) | async-done | bytes 229408 | tf_op jit(solution)/shard_map/all_to_all | solution.py:540
  42.3 2.1 %pairs.1 = bf16[8,112,128]{2,1,0:T(8,128)(2,1)} custom-call(bf16[8,112,128]{2,1,0:T(8,128)(2,1)S(1)} %all-to-all-done.pred_ref, f32[112,1024]{1,0:T(8,128)} %pad.8.obs_ref.obs0_ref.obs1_ref.obs2_ref.obs3_ref, f32[1,1024]{1,0:T(1,128)S(1)} %bitcast.37, f32[112,1]{1,0:T(8,128)S(1)} %copy.19.weight_ref), custom_call_target="tpu_custom_call" | custom-call | flops 16777216 | bytes 1048576 | tf_op jit(solution)/shard_map/pairs/pallas_call | solution.py:281
  44.5 3.4 %all-to-all-start.1 = ((bf16[8,112,128]{2,1,0:T(8,128)(2,1)}), bf16[8,112,128]{2,1,0:T(8,128)(2,1)S(1)}, u32[]{:S(2)}, u32[]{:S(2)}) async-start(bf16[8,112,128]{2,1,0:T(8,128)(2,1)} %pairs.1), calls=%async_computation.1 | async-start | bytes 458752 | tf_op jit(solution)/shard_map/all_to_all | solution.py:542
  48.0 10.9 %all-to-all-done.1.pair_ref = bf16[8,112,128]{2,1,0:T(8,128)(2,1)S(1)} async-done(((bf16[8,112,128]{2,1,0:T(8,128)(2,1)}), bf16[8,112,128]{2,1,0:T(8,128)(2,1)S(1)}, u32[]{:S(2)}, u32[]{:S(2)}) %all-to-all-start.1) | async-done | bytes 229408 | tf_op jit(solution)/shard_map/all_to_all | solution.py:542
  58.9 8.1 %weights.1 = (bf16[112,1024]{1,0:T(8,128)(2,1)S(1)}, bf16[1024,1024]{1,0:T(8,128)(2,1)S(1)}, f32[1,1024]{1,0:T(1,128)}, bf16[4,4,32,1152]{3,2,1,0:T(8,128)(2,1)S(1)}, bf16[4,4,32,1152]{3,2,1,0:T(8,128)(2,1)S(1)}) custom-call(s32[3]{0:T(128)S(1)} %pad_add_fusion.pos_ref, bf16[8,112,128]{2,1,0:T(8,128)(2,1)S(1)} %all-to-all-done.1.pair_ref, ...), custom_call_target="tpu_custom_call" | custom-call | flops 3221225472 | bytes 14680064 | tf_op jit(solution)/shard_map/weights/pallas_call | solution.py:367
  67.1 2.8 %collective-permute-done.2 = bf16[4,4,32,1152]{3,2,1,0:T(8,128)(2,1)S(1)} collective-permute-done((bf16[4,4,32,1152]{3,2,1,0:T(8,128)(2,1)S(1)}, bf16[4,4,32,1152]{3,2,1,0:T(8,128)(2,1)S(1)}, u32[]{:S(2)}, u32[]{:S(2)}) %collective-permute-start.2) | collective-permute-done | bytes 1179680 | tf_op jit(solution)/shard_map/ppermute | solution.py:506
  70.2 1.6 %collective-permute-start.3 = (bf16[4,32,1152]{2,1,0:T(8,128)(2,1)S(1)}, bf16[4,32,1152]{2,1,0:T(8,128)(2,1)S(1)}, u32[]{:S(2)}, u32[]{:S(2)}) collective-permute-start(bf16[4,32,1152]{2,1,0:T(8,128)(2,1)S(1)} %get-tuple-element.70), channel_id=1, source_target_pairs={{0,8},{1,9},{2,10},{3,11},{4,12},{5,13},{6,14},{7,15},{8,16},{9,17... | collective-permute-start | bytes 884744 | tf_op jit(solution)/shard_map/ppermute | solution.py:506
  72.8 2.5 %collective-permute-start.5 = (bf16[4,32,1152]{2,1,0:T(8,128)(2,1)S(1)}, bf16[4,32,1152]{2,1,0:T(8,128)(2,1)S(1)}, u32[]{:S(2)}, u32[]{:S(2)}) collective-permute-start(bf16[4,32,1152]{2,1,0:T(8,128)(2,1)S(1)} %get-tuple-element.68), channel_id=1, source_target_pairs={{0,24},{1,25},{2,26},{3,27},{4,28},{5,29},{6,30},{7,31},{8,0},{9,1... | collective-permute-start | bytes 884744 | tf_op jit(solution)/shard_map/ppermute | solution.py:506
  75.4 9.5 %latent.1 = (bf16[1024,1024]{1,0:T(8,128)(2,1)}, bf16[128,1024]{1,0:T(8,128)(2,1)S(1)}, bf16[128,1024]{1,0:T(8,128)(2,1)S(1)}) custom-call(s32[4,1024]{1,0:T(4,128)S(1)} %copy-done.2, s32[4,1024]{1,0:T(4,128)S(1)} %copy-done.2, bf16[112,1024]{1,0:T(8,128)(2,1)S(1)} %get-tuple-element.53.g_ref, bf16[112,1024]{1,0:T(8,128)(2,1)S(1)} %get-tuple-element.38.out_t_ref.out_ref, ...), custom_call_target="tpu_custom_call" | custom-call | flops 4294967296 | bytes 10485760 | tf_op jit(solution)/shard_map/latent/pallas_call | solution.py:458
  84.8 3.1 %collective-permute-done.5 = bf16[4,32,1152]{2,1,0:T(8,128)(2,1)S(1)} collective-permute-done((bf16[4,32,1152]{2,1,0:T(8,128)(2,1)S(1)}, bf16[4,32,1152]{2,1,0:T(8,128)(2,1)S(1)}, u32[]{:S(2)}, u32[]{:S(2)}) %collective-permute-start.5) | collective-permute-done | bytes 294944 | tf_op jit(solution)/shard_map/ppermute | solution.py:506
  88.1 3.3 %collective-permute-start.8 = (bf16[32,1152]{1,0:T(8,128)(2,1)S(1)}, bf16[32,1152]{1,0:T(8,128)(2,1)S(1)}, u32[]{:S(2)}, u32[]{:S(2)}) collective-permute-start(bf16[32,1152]{1,0:T(8,128)(2,1)S(1)} %get-tuple-element.74), channel_id=1, source_target_pairs={{0,6},{1,7},{2,0},{3,1},{4,2},{5,3},{6,4},{7,5},{8,14},{9,15},{10,... | collective-permute-start | bytes 221192 | tf_op jit(solution)/shard_map/ppermute | solution.py:506
  92.1 1.7 %collective-permute-start.6 = (bf16[32,1152]{1,0:T(8,128)(2,1)S(1)}, bf16[32,1152]{1,0:T(8,128)(2,1)S(1)}, u32[]{:S(2)}, u32[]{:S(2)}) collective-permute-start(bf16[32,1152]{1,0:T(8,128)(2,1)S(1)} %get-tuple-element.73), channel_id=1, source_target_pairs={{0,2},{1,3},{2,4},{3,5},{4,6},{5,7},{6,0},{7,1},{8,10},{9,11},{10,... | collective-permute-start | bytes 221192 | tf_op jit(solution)/shard_map/ppermute | solution.py:506
  93.7 4.1 %collective-permute-start.13 = (bf16[128,1024]{1,0:T(8,128)(2,1)S(1)}, bf16[128,1024]{1,0:T(8,128)(2,1)S(1)}, u32[]{:S(2)}, u32[]{:S(2)}) collective-permute-start(bf16[128,1024]{1,0:T(8,128)(2,1)S(1)} %get-tuple-element.62), channel_id=1, source_target_pairs={{1,2},{2,1},{3,4},{4,3},{5,6},{6,5},{7,8},{8,7},{9,10},{10,9},{11,... | collective-permute-start | bytes 786440 | tf_op jit(solution)/shard_map/ppermute | solution.py:506
  97.9 1.3 %collective-permute-done.7 = bf16[32,1152]{1,0:T(8,128)(2,1)S(1)} collective-permute-done((bf16[32,1152]{1,0:T(8,128)(2,1)S(1)}, bf16[32,1152]{1,0:T(8,128)(2,1)S(1)}, u32[]{:S(2)}, u32[]{:S(2)}) %collective-permute-start.7) | collective-permute-done | bytes 73760 | tf_op jit(solution)/shard_map/ppermute | solution.py:506
  99.5 2.1 %collective-permute-start.10 = (bf16[32,1152]{1,0:T(8,128)(2,1)S(1)}, bf16[32,1152]{1,0:T(8,128)(2,1)S(1)}, u32[]{:S(2)}, u32[]{:S(2)}) collective-permute-start(bf16[32,1152]{1,0:T(8,128)(2,1)S(1)} %fusion.9), channel_id=1, source_target_pairs={{0,128},{32,160},{64,192},{96,224},{128,0},{160,32},{192,64},{224,... | collective-permute-start | bytes 221192 | tf_op jit(solution)/shard_map/ppermute | solution.py:506
  101.6 1.5 %collective-permute-start.11 = (bf16[32,1152]{1,0:T(8,128)(2,1)S(1)}, bf16[32,1152]{1,0:T(8,128)(2,1)S(1)}, u32[]{:S(2)}, u32[]{:S(2)}) collective-permute-start(bf16[32,1152]{1,0:T(8,128)(2,1)S(1)} %fusion.9), channel_id=1, source_target_pairs={{0,192},{32,224},{64,0},{96,32},{128,64},{160,96},{192,128},{224,1... | collective-permute-start | bytes 221192 | tf_op jit(solution)/shard_map/ppermute | solution.py:506
  103.0 2.0 %collective-permute-done.13.far_ref = bf16[128,1024]{1,0:T(8,128)(2,1)S(1)} collective-permute-done((bf16[128,1024]{1,0:T(8,128)(2,1)S(1)}, bf16[128,1024]{1,0:T(8,128)(2,1)S(1)}, u32[]{:S(2)}, u32[]{:S(2)}) %collective-permute-start.13) | collective-permute-done | bytes 262176 | tf_op jit(solution)/shard_map/ppermute | solution.py:506
  107.2 1.8 %rims.1 = bf16[1024,1024]{1,0:T(8,128)(2,1)} custom-call(bf16[1024,1024]{1,0:T(8,128)(2,1)} %get-tuple-element.57.grad_ref, bf16[128,1024]{1,0:T(8,128)(2,1)S(1)} %collective-permute-done.12.near_ref, bf16[128,1024]{1,0:T(8,128)(2,1)S(1)} %collective-permute-done.13.far_ref), custom_call_target="tpu_custom_call", output_to_operand_aliasing={{}: (0, {})} | custom-call | flops 262144 | bytes 1572864 | tf_op jit(solution)/shard_map/rims/pallas_call | solution.py:491
  109.1 6.1 %collective-permute-done.14 = bf16[32,1152]{1,0:T(8,128)(2,1)S(1)} collective-permute-done((bf16[32,1152]{1,0:T(8,128)(2,1)S(1)}, bf16[32,1152]{1,0:T(8,128)(2,1)S(1)}, u32[]{:S(2)}, u32[]{:S(2)}) %collective-permute-start.14) | collective-permute-done | bytes 73760 | tf_op jit(solution)/shard_map/ppermute | solution.py:506
  (45 shorter events, 7.2 us)
Async XLA Ops:
  1.7 17.4 %collective-permute-start = (bf16[128,1024]{1,0:T(8,128)(2,1)S(1)}, bf16[128,1024]{1,0:T(8,128)(2,1)S(1)}, u32[]{:S(2)}, u32[]{:S(2)}) collective-permute-start(bf16[128,1024]{1,0:T(8,128)(2,1)S(1)} %get-tuple-element.72), channel_id=1, source_target_pairs={{0,1},{1,0},{2,3},{3,2},{4,5},{5,4},{6,7},{7,6},{8,9},{9,8},{10,11... | collective-permute-start | bytes 786440 | tf_op jit(solution)/shard_map/ppermute | solution.py:506
  1.8 17.3 %collective-permute-start.1 = (bf16[128,1024]{1,0:T(8,128)(2,1)S(1)}, bf16[128,1024]{1,0:T(8,128)(2,1)S(1)}, u32[]{:S(2)}, u32[]{:S(2)}) collective-permute-start(bf16[128,1024]{1,0:T(8,128)(2,1)S(1)} %get-tuple-element.71), channel_id=1, source_target_pairs={{1,2},{2,1},{3,4},{4,3},{5,6},{6,5},{7,8},{8,7},{9,10},{10,9},{11,... | collective-permute-start | bytes 786440 | tf_op jit(solution)/shard_map/ppermute | solution.py:506
  19.1 12.1 %copy-start.7 = (f32[100]{0:T(128)S(1)}, f32[100]{0:T(128)}, u32[]{:S(2)}) copy-start(f32[100]{0:T(128)} %param.15) | copy-start | bytes 1204
  19.2 12.2 %copy-start.6 = (f32[100,1024]{1,0:T(8,128)S(1)}, f32[100,1024]{1,0:T(8,128)}, u32[]{:S(2)}) copy-start(f32[100,1024]{1,0:T(8,128)} %param.13) | copy-start | bytes 1228804
  19.2 23.2 %copy-start.3 = (f32[1024]{0:T(1024)S(1)}, f32[1024]{0:T(1024)}, u32[]{:S(2)}) copy-start(f32[1024]{0:T(1024)} %param.14) | copy-start | bytes 12292
  22.8 19.5 %all-to-all-start = ((bf16[8,112,128]{2,1,0:T(8,128)(2,1)}), bf16[8,112,128]{2,1,0:T(8,128)(2,1)S(1)}, u32[]{:S(2)}, u32[]{:S(2)}) async-start(bf16[8,112,128]{2,1,0:T(8,128)(2,1)} %get-tuple-element.45), calls=%async_computation | async-start | bytes 458752 | tf_op jit(solution)/shard_map/all_to_all | solution.py:540
  44.5 14.4 %all-to-all-start.1 = ((bf16[8,112,128]{2,1,0:T(8,128)(2,1)}), bf16[8,112,128]{2,1,0:T(8,128)(2,1)S(1)}, u32[]{:S(2)}, u32[]{:S(2)}) async-start(bf16[8,112,128]{2,1,0:T(8,128)(2,1)} %pairs.1), calls=%async_computation.1 | async-start | bytes 458752 | tf_op jit(solution)/shard_map/all_to_all | solution.py:542
  58.9 16.4 %copy-start.5 = (bf16[1024,1024]{1,0:T(8,128)(2,1)S(1)}, bf16[1024,1024]{1,0:T(8,128)(2,1)}, u32[]{:S(2)}) copy-start(bf16[1024,1024]{1,0:T(8,128)(2,1)} %mix_ref.1) | copy-start | bytes 6291460
  67.0 8.3 %copy-start = (bf16[1024,1024]{1,0:T(8,128)(2,1)S(1)}, bf16[1024,1024]{1,0:T(8,128)(2,1)}, u32[]{:S(2)}) copy-start(bf16[1024,1024]{1,0:T(8,128)(2,1)} %get-tuple-element.49.normed0_ref.normed1_ref.normed_ref) | copy-start | bytes 6291460
  67.0 8.3 %copy-start.1 = (f32[1024,1]{1,0:T(8,128)S(1)}, f32[1024,1]{1,0:T(8,128)}, u32[]{:S(2)}) copy-start(f32[1024,1]{1,0:T(8,128)} %get-tuple-element.55.inv_ref) | copy-start | bytes 12292
  67.0 8.3 %copy-start.2 = (s32[4,1024]{1,0:T(4,128)S(1)}, s32[4,1024]{1,0:T(4,128)}, u32[]{:S(2)}) copy-start(s32[4,1024]{1,0:T(4,128)} %nb1_ref.5) | copy-start | bytes 49156
  67.0 2.9 %collective-permute-start.2 = (bf16[4,4,32,1152]{3,2,1,0:T(8,128)(2,1)S(1)}, bf16[4,4,32,1152]{3,2,1,0:T(8,128)(2,1)S(1)}, u32[]{:S(2)}, u32[]{:S(2)}) collective-permute-start(bf16[4,4,32,1152]{3,2,1,0:T(8,128)(2,1)S(1)} %get-tuple-element.52), channel_id=1, source_target_pairs={{0,1},{1,0},{2,3},{3,2},{4,5},{5,4},{6,7},{7,6},{8,9},{9,8},{10,11... | collective-permute-start | bytes 3538952 | tf_op jit(solution)/shard_map/ppermute | solution.py:506
  70.2 14.6 %collective-permute-start.3 = (bf16[4,32,1152]{2,1,0:T(8,128)(2,1)S(1)}, bf16[4,32,1152]{2,1,0:T(8,128)(2,1)S(1)}, u32[]{:S(2)}, u32[]{:S(2)}) collective-permute-start(bf16[4,32,1152]{2,1,0:T(8,128)(2,1)S(1)} %get-tuple-element.70), channel_id=1, source_target_pairs={{0,8},{1,9},{2,10},{3,11},{4,12},{5,13},{6,14},{7,15},{8,16},{9,17... | collective-permute-start | bytes 884744 | tf_op jit(solution)/shard_map/ppermute | solution.py:506
  71.8 13.1 %collective-permute-start.4 = (bf16[4,32,1152]{2,1,0:T(8,128)(2,1)S(1)}, bf16[4,32,1152]{2,1,0:T(8,128)(2,1)S(1)}, u32[]{:S(2)}, u32[]{:S(2)}) collective-permute-start(bf16[4,32,1152]{2,1,0:T(8,128)(2,1)S(1)} %get-tuple-element.69), channel_id=1, source_target_pairs={{0,16},{1,17},{2,18},{3,19},{4,20},{5,21},{6,22},{7,23},{8,24},{9,... | collective-permute-start | bytes 884744 | tf_op jit(solution)/shard_map/ppermute | solution.py:506
  72.8 15.1 %collective-permute-start.5 = (bf16[4,32,1152]{2,1,0:T(8,128)(2,1)S(1)}, bf16[4,32,1152]{2,1,0:T(8,128)(2,1)S(1)}, u32[]{:S(2)}, u32[]{:S(2)}) collective-permute-start(bf16[4,32,1152]{2,1,0:T(8,128)(2,1)S(1)} %get-tuple-element.68), channel_id=1, source_target_pairs={{0,24},{1,25},{2,26},{3,27},{4,28},{5,29},{6,30},{7,31},{8,0},{9,1... | collective-permute-start | bytes 884744 | tf_op jit(solution)/shard_map/ppermute | solution.py:506
  88.1 9.7 %collective-permute-start.8 = (bf16[32,1152]{1,0:T(8,128)(2,1)S(1)}, bf16[32,1152]{1,0:T(8,128)(2,1)S(1)}, u32[]{:S(2)}, u32[]{:S(2)}) collective-permute-start(bf16[32,1152]{1,0:T(8,128)(2,1)S(1)} %get-tuple-element.74), channel_id=1, source_target_pairs={{0,6},{1,7},{2,0},{3,1},{4,2},{5,3},{6,4},{7,5},{8,14},{9,15},{10,... | collective-permute-start | bytes 221192 | tf_op jit(solution)/shard_map/ppermute | solution.py:506
  91.5 7.7 %collective-permute-start.7 = (bf16[32,1152]{1,0:T(8,128)(2,1)S(1)}, bf16[32,1152]{1,0:T(8,128)(2,1)S(1)}, u32[]{:S(2)}, u32[]{:S(2)}) collective-permute-start(bf16[32,1152]{1,0:T(8,128)(2,1)S(1)} %get-tuple-element.75), channel_id=1, source_target_pairs={{0,4},{1,5},{2,6},{3,7},{4,0},{5,1},{6,2},{7,3},{8,12},{9,13},{10,... | collective-permute-start | bytes 221192 | tf_op jit(solution)/shard_map/ppermute | solution.py:506
  92.1 7.1 %collective-permute-start.6 = (bf16[32,1152]{1,0:T(8,128)(2,1)S(1)}, bf16[32,1152]{1,0:T(8,128)(2,1)S(1)}, u32[]{:S(2)}, u32[]{:S(2)}) collective-permute-start(bf16[32,1152]{1,0:T(8,128)(2,1)S(1)} %get-tuple-element.73), channel_id=1, source_target_pairs={{0,2},{1,3},{2,4},{3,5},{4,6},{5,7},{6,0},{7,1},{8,10},{9,11},{10,... | collective-permute-start | bytes 221192 | tf_op jit(solution)/shard_map/ppermute | solution.py:506
  93.7 9.3 %collective-permute-start.12 = (bf16[128,1024]{1,0:T(8,128)(2,1)S(1)}, bf16[128,1024]{1,0:T(8,128)(2,1)S(1)}, u32[]{:S(2)}, u32[]{:S(2)}) collective-permute-start(bf16[128,1024]{1,0:T(8,128)(2,1)S(1)} %get-tuple-element.61), channel_id=1, source_target_pairs={{0,1},{1,0},{2,3},{3,2},{4,5},{5,4},{6,7},{7,6},{8,9},{9,8},{10,11... | collective-permute-start | bytes 786440 | tf_op jit(solution)/shard_map/ppermute | solution.py:506
  93.7 11.3 %collective-permute-start.13 = (bf16[128,1024]{1,0:T(8,128)(2,1)S(1)}, bf16[128,1024]{1,0:T(8,128)(2,1)S(1)}, u32[]{:S(2)}, u32[]{:S(2)}) collective-permute-start(bf16[128,1024]{1,0:T(8,128)(2,1)S(1)} %get-tuple-element.62), channel_id=1, source_target_pairs={{1,2},{2,1},{3,4},{4,3},{5,6},{6,5},{7,8},{8,7},{9,10},{10,9},{11,... | collective-permute-start | bytes 786440 | tf_op jit(solution)/shard_map/ppermute | solution.py:506
  99.2 6.7 %collective-permute-start.9 = (bf16[32,1152]{1,0:T(8,128)(2,1)S(1)}, bf16[32,1152]{1,0:T(8,128)(2,1)S(1)}, u32[]{:S(2)}, u32[]{:S(2)}) collective-permute-start(bf16[32,1152]{1,0:T(8,128)(2,1)S(1)} %fusion.9), channel_id=1, source_target_pairs={{0,64},{32,96},{64,128},{96,160},{128,192},{160,224},{192,0},{224,... | collective-permute-start | bytes 221192 | tf_op jit(solution)/shard_map/ppermute | solution.py:506
  99.5 6.4 %collective-permute-start.10 = (bf16[32,1152]{1,0:T(8,128)(2,1)S(1)}, bf16[32,1152]{1,0:T(8,128)(2,1)S(1)}, u32[]{:S(2)}, u32[]{:S(2)}) collective-permute-start(bf16[32,1152]{1,0:T(8,128)(2,1)S(1)} %fusion.9), channel_id=1, source_target_pairs={{0,128},{32,160},{64,192},{96,224},{128,0},{160,32},{192,64},{224,... | collective-permute-start | bytes 221192 | tf_op jit(solution)/shard_map/ppermute | solution.py:506
  101.6 4.9 %collective-permute-start.11 = (bf16[32,1152]{1,0:T(8,128)(2,1)S(1)}, bf16[32,1152]{1,0:T(8,128)(2,1)S(1)}, u32[]{:S(2)}, u32[]{:S(2)}) collective-permute-start(bf16[32,1152]{1,0:T(8,128)(2,1)S(1)} %fusion.9), channel_id=1, source_target_pairs={{0,192},{32,224},{64,0},{96,32},{128,64},{160,96},{192,128},{224,1... | collective-permute-start | bytes 221192 | tf_op jit(solution)/shard_map/ppermute | solution.py:506
  106.5 8.6 %collective-permute-start.14 = (bf16[32,1152]{1,0:T(8,128)(2,1)S(1)}, bf16[32,1152]{1,0:T(8,128)(2,1)S(1)}, u32[]{:S(2)}, u32[]{:S(2)}) collective-permute-start(bf16[32,1152]{1,0:T(8,128)(2,1)S(1)} %add_convert_fusion.4), channel_id=1, source_target_pairs={{0,32},{32,0},{64,96},{96,64},{128,160},{160,128},{192,224},{224,1... | collective-permute-start | bytes 221192 | tf_op jit(solution)/shard_map/ppermute | solution.py:506
  (1 other events, 8.3 us)

commit v7 on v6

--- a/solution.py
+++ b/solution.py
@@ -28,6 +28,7 @@
 fair_shift = 0.05
 fair_weight = 1.0 - fair_shift / MEMBERS
 pair_coef = fair_weight / (2.0 * MEMBERS * (MEMBERS - 1))
+grad_scale = 1.0 / math.sqrt(MEMBERS * CELLS * 32)
 
 bf16 = jnp.bfloat16
 f32 = jnp.float32
@@ -501,6 +502,22 @@
     )(grad, near, far)
 
 
+def finish_kernel(one_ref, two_ref, mix_ref, out_ref):
+    total = (one_ref[...].astype(f32) + two_ref[...].astype(f32)) * grad_scale
+    mix_ref[...] = total[:, :D]
+    out_ref[...] = total[:, D : D + VARS]
+
+
+def scaled_sum(one, two):
+    return pl.pallas_call(
+        finish_kernel,
+        out_shape=[jax.ShapeDtypeStruct((32, D), f32), jax.ShapeDtypeStruct((32, VARS), f32)],
+        compiler_params=pltpu.CompilerParams(vmem_limit_bytes=VMEM_LIMIT),
+        cost_estimate=pl.CostEstimate(flops=1 << 17, bytes_accessed=1 << 18, transcendentals=0),
+        name="finish",
+    )(one, two)
+
+
 def along(value, axis, move):
     pairs = [(i, move(i)) for i in range(lax.axis_size(axis))]
     return lax.ppermute(value, axis, [pair for pair in pairs if pair[1] is not None])
@@ -565,15 +582,9 @@
     arrived = [along(share, "member", lambda i: (i + 2 * k) % 8) for k in (1, 2, 3)]
     arrived, near, far = lax.optimization_barrier((arrived, near, far))
     share = summed([share] + arrived).astype(bf16)
-    totals = summed([share, along(share, "member", lambda i: i ^ 1)])
+    mix_grad, out_grad = scaled_sum(share, along(share, "member", lambda i: i ^ 1))
     grad = add_rims(grad, near, far)
-    grad_scale = 1.0 / math.sqrt(MEMBERS * CELLS * 32)
-    return (
-        losses.reshape(CELLS),
-        grad[None],
-        totals[:, :D] * grad_scale,
-        totals[:, D : D + VARS] * grad_scale,
-    )
+    return losses.reshape(CELLS), grad[None], mix_grad, out_grad
 
 
 def solution(mesh):

time: 117 us -> 116 us (level)
  other arithmetic: 2.92 us -> 1.63 us
    mul x2 -> x0, other arithmetic: 1.27 us -> none  [the longest x1 0.67 us: shards(): totals[:, :D] * grad_scale]
where the time goes in v7:
time: 116 us
  starting transfers between devices  38.1 us (33%)
  waiting for transfers between devices  37.7 us (33%)
  Pallas kernels  36.5 us (31%)
  other arithmetic  1.63 us (1%)
    ppermute x15, starting transfers between devices, along(): lax.ppermute(value, axis, [pair for pair in pairs if pair[1] is not None])  26.3 us
    ppermute x15, waiting for transfers between devices, along(): lax.ppermute(value, axis, [pair for pair in pairs if pair[1] is not None])  16.6 us
    all_to_all x1, waiting for transfers between devices, shards(): pairs = lax.all_to_all(pairs, 'member', 0, 0, tiled=True)  10.9 us
    pallas_call x1, Pallas kernels, forward(): pl.pallas_call(interior_kernel, grid=(STEPS - 1,), in_specs=[edges_at(lam...  10.7 us
    all_to_all x1, waiting for transfers between devices, shards(): pieces = lax.all_to_all(pieces, 'member', 0, 0, tiled=True)  10.2 us
    pallas_call x1, Pallas kernels, latent_parts(): pl.pallas_call(latent_kernel, grid=(STEPS,), in_specs=[pl.BlockSpec((NBRS...  9.46 us
    all_to_all x1, starting transfers between devices, shards(): pieces = lax.all_to_all(pieces, 'member', 0, 0, tiled=True)  8.4 us
    pallas_call x1, Pallas kernels, weight_parts(): pl.pallas_call(weights_kernel, grid_spec=pltpu.PrefetchScalarGridSpec(num...  8.09 us
  transfers between devices with their start and end apart: 17, of which 9 were waited for; matrix products, arithmetic and copies ran while one was open for 1% of the time, Pallas kernels for 19%

profile of v7, /device:TPU:2, one launch (start us, length us, event | category | flops | bytes accessed | tf_op | source)
XLA Modules:
  0.0 115.8 jit_solution(15391875470506759886)
XLA Ops:
  0.6 1.1 select_bitcast_fusion
  1.8 6.6 %collective-permute-start.1 = (bf16[128,1024]{1,0:T(8,128)(2,1)S(1)}, bf16[128,1024]{1,0:T(8,128)(2,1)S(1)}, u32[]{:S(2)}, u32[]{:S(2)}) collective-permute-start(bf16[128,1024]{1,0:T(8,128)(2,1)S(1)} %get-tuple-element.75), channel_id=1, source_target_pairs={{1,2},{2,1},{3,4},{4,3},{5,6},{6,5},{7,8},{8,7},{9,10},{10,9},{11,... | collective-permute-start | bytes 786440 | tf_op jit(solution)/shard_map/ppermute | solution.py:523
  8.4 10.7 %interior.1 = (bf16[112,1024]{1,0:T(8,128)(2,1)S(1)}, bf16[1024,1024]{1,0:T(8,128)(2,1)S(1)}, bf16[1024,1024]{1,0:T(8,128)(2,1)S(1)}, bf16[1024,1024]{1,0:T(8,12...) custom-call(s32[4,1024]{1,0:T(4,128)} %nb1_ref.5, ...), custom_call_target="tpu_custom_call" | custom-call | flops 3221225472 | bytes 9437184 | tf_op jit(solution)/shard_map/interior/pallas_call | solution.py:194
  19.1 3.6 %rim_cells.1 = (bf16[1024,1024]{1,0:T(8,128)(2,1)}, bf16[1024,1024]{1,0:T(8,128)(2,1)}, bf16[1024,1024]{1,0:T(8,128)(2,1)}, f32[1024,1]{1,0:T(8,128)}, f32[112,1...) custom-call(s32[4,1024]{1,0:T(4,128)} %nb1_ref.5, ...), custom_call_target="tpu_custom_call", output_to_operand_aliasing={{0}: (8, {}), {1}: (9, {}), {2}: (10, {}), {3}: (11, {}), {... | custom-call | flops 1073741824 | bytes 3145728 | tf_op jit(solution)/shard_map/rim_cells/pallas_call | solution.py:219
  22.7 8.4 %all-to-all-start = ((bf16[8,112,128]{2,1,0:T(8,128)(2,1)}), bf16[8,112,128]{2,1,0:T(8,128)(2,1)S(1)}, u32[]{:S(2)}, u32[]{:S(2)}) async-start(bf16[8,112,128]{2,1,0:T(8,128)(2,1)} %get-tuple-element.47), calls=%async_computation | async-start | bytes 458752 | tf_op jit(solution)/shard_map/all_to_all | solution.py:557
  32.1 10.2 %all-to-all-done.pred_ref = bf16[8,112,128]{2,1,0:T(8,128)(2,1)S(1)} async-done(((bf16[8,112,128]{2,1,0:T(8,128)(2,1)}), bf16[8,112,128]{2,1,0:T(8,128)(2,1)S(1)}, u32[]{:S(2)}, u32[]{:S(2)}) %all-to-all-start) | async-done | bytes 229408 | tf_op jit(solution)/shard_map/all_to_all | solution.py:557
  42.3 2.1 %pairs.1 = bf16[8,112,128]{2,1,0:T(8,128)(2,1)} custom-call(bf16[8,112,128]{2,1,0:T(8,128)(2,1)S(1)} %all-to-all-done.pred_ref, f32[112,1024]{1,0:T(8,128)} %pad.8.obs_ref.obs0_ref.obs1_ref.obs2_ref.obs3_ref, f32[1,1024]{1,0:T(1,128)S(1)} %bitcast.37, f32[112,1]{1,0:T(8,128)S(1)} %copy.19.weight_ref), custom_call_target="tpu_custom_call" | custom-call | flops 16777216 | bytes 1048576 | tf_op jit(solution)/shard_map/pairs/pallas_call | solution.py:282
  44.4 3.4 %all-to-all-start.1 = ((bf16[8,112,128]{2,1,0:T(8,128)(2,1)}), bf16[8,112,128]{2,1,0:T(8,128)(2,1)S(1)}, u32[]{:S(2)}, u32[]{:S(2)}) async-start(bf16[8,112,128]{2,1,0:T(8,128)(2,1)} %pairs.1), calls=%async_computation.1 | async-start | bytes 458752 | tf_op jit(solution)/shard_map/all_to_all | solution.py:559
  47.9 10.9 %all-to-all-done.1.pair_ref = bf16[8,112,128]{2,1,0:T(8,128)(2,1)S(1)} async-done(((bf16[8,112,128]{2,1,0:T(8,128)(2,1)}), bf16[8,112,128]{2,1,0:T(8,128)(2,1)S(1)}, u32[]{:S(2)}, u32[]{:S(2)}) %all-to-all-start.1) | async-done | bytes 229408 | tf_op jit(solution)/shard_map/all_to_all | solution.py:559
  58.9 8.1 %weights.1 = (bf16[112,1024]{1,0:T(8,128)(2,1)S(1)}, bf16[1024,1024]{1,0:T(8,128)(2,1)S(1)}, f32[1,1024]{1,0:T(1,128)}, bf16[4,4,32,1152]{3,2,1,0:T(8,128)(2,1)S(1)}, bf16[4,4,32,1152]{3,2,1,0:T(8,128)(2,1)S(1)}) custom-call(s32[3]{0:T(128)S(1)} %pad_add_fusion.pos_ref, bf16[8,112,128]{2,1,0:T(8,128)(2,1)S(1)} %all-to-all-done.1.pair_ref, ...), custom_call_target="tpu_custom_call" | custom-call | flops 3221225472 | bytes 14680064 | tf_op jit(solution)/shard_map/weights/pallas_call | solution.py:368
  67.1 2.8 %collective-permute-done.2 = bf16[4,4,32,1152]{3,2,1,0:T(8,128)(2,1)S(1)} collective-permute-done((bf16[4,4,32,1152]{3,2,1,0:T(8,128)(2,1)S(1)}, bf16[4,4,32,1152]{3,2,1,0:T(8,128)(2,1)S(1)}, u32[]{:S(2)}, u32[]{:S(2)}) %collective-permute-start.2) | collective-permute-done | bytes 1179680 | tf_op jit(solution)/shard_map/ppermute | solution.py:523
  70.1 1.6 %collective-permute-start.3 = (bf16[4,32,1152]{2,1,0:T(8,128)(2,1)S(1)}, bf16[4,32,1152]{2,1,0:T(8,128)(2,1)S(1)}, u32[]{:S(2)}, u32[]{:S(2)}) collective-permute-start(bf16[4,32,1152]{2,1,0:T(8,128)(2,1)S(1)} %get-tuple-element.74), channel_id=1, source_target_pairs={{0,8},{1,9},{2,10},{3,11},{4,12},{5,13},{6,14},{7,15},{8,16},{9,17... | collective-permute-start | bytes 884744 | tf_op jit(solution)/shard_map/ppermute | solution.py:523
  72.8 2.5 %collective-permute-start.5 = (bf16[4,32,1152]{2,1,0:T(8,128)(2,1)S(1)}, bf16[4,32,1152]{2,1,0:T(8,128)(2,1)S(1)}, u32[]{:S(2)}, u32[]{:S(2)}) collective-permute-start(bf16[4,32,1152]{2,1,0:T(8,128)(2,1)S(1)} %get-tuple-element.72), channel_id=1, source_target_pairs={{0,24},{1,25},{2,26},{3,27},{4,28},{5,29},{6,30},{7,31},{8,0},{9,1... | collective-permute-start | bytes 884744 | tf_op jit(solution)/shard_map/ppermute | solution.py:523
  75.3 9.5 %latent.1 = (bf16[1024,1024]{1,0:T(8,128)(2,1)}, bf16[128,1024]{1,0:T(8,128)(2,1)S(1)}, bf16[128,1024]{1,0:T(8,128)(2,1)S(1)}) custom-call(s32[4,1024]{1,0:T(4,128)S(1)} %copy-done.2, s32[4,1024]{1,0:T(4,128)S(1)} %copy-done.2, bf16[112,1024]{1,0:T(8,128)(2,1)S(1)} %get-tuple-element.55.g_ref, bf16[112,1024]{1,0:T(8,128)(2,1)S(1)} %get-tuple-element.40.out_t_ref.out_ref, ...), custom_call_target="tpu_custom_call" | custom-call | flops 4294967296 | bytes 10485760 | tf_op jit(solution)/shard_map/latent/pallas_call | solution.py:459
  84.8 3.1 %collective-permute-done.5 = bf16[4,32,1152]{2,1,0:T(8,128)(2,1)S(1)} collective-permute-done((bf16[4,32,1152]{2,1,0:T(8,128)(2,1)S(1)}, bf16[4,32,1152]{2,1,0:T(8,128)(2,1)S(1)}, u32[]{:S(2)}, u32[]{:S(2)}) %collective-permute-start.5) | collective-permute-done | bytes 294944 | tf_op jit(solution)/shard_map/ppermute | solution.py:523
  88.1 3.3 %collective-permute-start.8 = (bf16[32,1152]{1,0:T(8,128)(2,1)S(1)}, bf16[32,1152]{1,0:T(8,128)(2,1)S(1)}, u32[]{:S(2)}, u32[]{:S(2)}) collective-permute-start(bf16[32,1152]{1,0:T(8,128)(2,1)S(1)} %get-tuple-element.78), channel_id=1, source_target_pairs={{0,6},{1,7},{2,0},{3,1},{4,2},{5,3},{6,4},{7,5},{8,14},{9,15},{10,... | collective-permute-start | bytes 221192 | tf_op jit(solution)/shard_map/ppermute | solution.py:523
  92.0 1.7 %collective-permute-start.6 = (bf16[32,1152]{1,0:T(8,128)(2,1)S(1)}, bf16[32,1152]{1,0:T(8,128)(2,1)S(1)}, u32[]{:S(2)}, u32[]{:S(2)}) collective-permute-start(bf16[32,1152]{1,0:T(8,128)(2,1)S(1)} %get-tuple-element.77), channel_id=1, source_target_pairs={{0,2},{1,3},{2,4},{3,5},{4,6},{5,7},{6,0},{7,1},{8,10},{9,11},{10,... | collective-permute-start | bytes 221192 | tf_op jit(solution)/shard_map/ppermute | solution.py:523
  93.7 4.1 %collective-permute-start.13 = (bf16[128,1024]{1,0:T(8,128)(2,1)S(1)}, bf16[128,1024]{1,0:T(8,128)(2,1)S(1)}, u32[]{:S(2)}, u32[]{:S(2)}) collective-permute-start(bf16[128,1024]{1,0:T(8,128)(2,1)S(1)} %get-tuple-element.64), channel_id=1, source_target_pairs={{1,2},{2,1},{3,4},{4,3},{5,6},{6,5},{7,8},{8,7},{9,10},{10,9},{11,... | collective-permute-start | bytes 786440 | tf_op jit(solution)/shard_map/ppermute | solution.py:523
  97.8 1.2 %collective-permute-done.7 = bf16[32,1152]{1,0:T(8,128)(2,1)S(1)} collective-permute-done((bf16[32,1152]{1,0:T(8,128)(2,1)S(1)}, bf16[32,1152]{1,0:T(8,128)(2,1)S(1)}, u32[]{:S(2)}, u32[]{:S(2)}) %collective-permute-start.7) | collective-permute-done | bytes 73760 | tf_op jit(solution)/shard_map/ppermute | solution.py:523
  99.4 2.0 %collective-permute-start.10 = (bf16[32,1152]{1,0:T(8,128)(2,1)S(1)}, bf16[32,1152]{1,0:T(8,128)(2,1)S(1)}, u32[]{:S(2)}, u32[]{:S(2)}) collective-permute-start(bf16[32,1152]{1,0:T(8,128)(2,1)S(1)} %fusion.9), channel_id=1, source_target_pairs={{0,128},{32,160},{64,192},{96,224},{128,0},{160,32},{192,64},{224,... | collective-permute-start | bytes 221192 | tf_op jit(solution)/shard_map/ppermute | solution.py:523
  101.5 1.5 %collective-permute-start.11 = (bf16[32,1152]{1,0:T(8,128)(2,1)S(1)}, bf16[32,1152]{1,0:T(8,128)(2,1)S(1)}, u32[]{:S(2)}, u32[]{:S(2)}) collective-permute-start(bf16[32,1152]{1,0:T(8,128)(2,1)S(1)} %fusion.9), channel_id=1, source_target_pairs={{0,192},{32,224},{64,0},{96,32},{128,64},{160,96},{192,128},{224,1... | collective-permute-start | bytes 221192 | tf_op jit(solution)/shard_map/ppermute | solution.py:523
  103.0 2.0 %collective-permute-done.13.far_ref = bf16[128,1024]{1,0:T(8,128)(2,1)S(1)} collective-permute-done((bf16[128,1024]{1,0:T(8,128)(2,1)S(1)}, bf16[128,1024]{1,0:T(8,128)(2,1)S(1)}, u32[]{:S(2)}, u32[]{:S(2)}) %collective-permute-start.13) | collective-permute-done | bytes 262176 | tf_op jit(solution)/shard_map/ppermute | solution.py:523
  107.2 1.8 %rims.1 = bf16[1024,1024]{1,0:T(8,128)(2,1)} custom-call(bf16[1024,1024]{1,0:T(8,128)(2,1)} %get-tuple-element.59.grad_ref, bf16[128,1024]{1,0:T(8,128)(2,1)S(1)} %collective-permute-done.12.near_ref, bf16[128,1024]{1,0:T(8,128)(2,1)S(1)} %collective-permute-done.13.far_ref), custom_call_target="tpu_custom_call", output_to_operand_aliasing={{}: (0, {})} | custom-call | flops 262144 | bytes 1572864 | tf_op jit(solution)/shard_map/rims/pallas_call | solution.py:492
  109.0 6.1 %collective-permute-done.14.two_ref = bf16[32,1152]{1,0:T(8,128)(2,1)S(1)} collective-permute-done((bf16[32,1152]{1,0:T(8,128)(2,1)S(1)}, bf16[32,1152]{1,0:T(8,128)(2,1)S(1)}, u32[]{:S(2)}, u32[]{:S(2)}) %collective-permute-start.14) | collective-permute-done | bytes 73760 | tf_op jit(solution)/shard_map/ppermute | solution.py:523
  (43 shorter events, 6.6 us)
Async XLA Ops:
  1.7 17.4 %collective-permute-start = (bf16[128,1024]{1,0:T(8,128)(2,1)S(1)}, bf16[128,1024]{1,0:T(8,128)(2,1)S(1)}, u32[]{:S(2)}, u32[]{:S(2)}) collective-permute-start(bf16[128,1024]{1,0:T(8,128)(2,1)S(1)} %get-tuple-element.76), channel_id=1, source_target_pairs={{0,1},{1,0},{2,3},{3,2},{4,5},{5,4},{6,7},{7,6},{8,9},{9,8},{10,11... | collective-permute-start | bytes 786440 | tf_op jit(solution)/shard_map/ppermute | solution.py:523
  1.8 17.3 %collective-permute-start.1 = (bf16[128,1024]{1,0:T(8,128)(2,1)S(1)}, bf16[128,1024]{1,0:T(8,128)(2,1)S(1)}, u32[]{:S(2)}, u32[]{:S(2)}) collective-permute-start(bf16[128,1024]{1,0:T(8,128)(2,1)S(1)} %get-tuple-element.75), channel_id=1, source_target_pairs={{1,2},{2,1},{3,4},{4,3},{5,6},{6,5},{7,8},{8,7},{9,10},{10,9},{11,... | collective-permute-start | bytes 786440 | tf_op jit(solution)/shard_map/ppermute | solution.py:523
  19.1 12.0 %copy-start.7 = (f32[100]{0:T(128)S(1)}, f32[100]{0:T(128)}, u32[]{:S(2)}) copy-start(f32[100]{0:T(128)} %param.15) | copy-start | bytes 1204
  19.1 12.2 %copy-start.6 = (f32[100,1024]{1,0:T(8,128)S(1)}, f32[100,1024]{1,0:T(8,128)}, u32[]{:S(2)}) copy-start(f32[100,1024]{1,0:T(8,128)} %param.13) | copy-start | bytes 1228804
  19.1 23.1 %copy-start.3 = (f32[1024]{0:T(1024)S(1)}, f32[1024]{0:T(1024)}, u32[]{:S(2)}) copy-start(f32[1024]{0:T(1024)} %param.14) | copy-start | bytes 12292
  22.7 19.5 %all-to-all-start = ((bf16[8,112,128]{2,1,0:T(8,128)(2,1)}), bf16[8,112,128]{2,1,0:T(8,128)(2,1)S(1)}, u32[]{:S(2)}, u32[]{:S(2)}) async-start(bf16[8,112,128]{2,1,0:T(8,128)(2,1)} %get-tuple-element.47), calls=%async_computation | async-start | bytes 458752 | tf_op jit(solution)/shard_map/all_to_all | solution.py:557
  44.4 14.4 %all-to-all-start.1 = ((bf16[8,112,128]{2,1,0:T(8,128)(2,1)}), bf16[8,112,128]{2,1,0:T(8,128)(2,1)S(1)}, u32[]{:S(2)}, u32[]{:S(2)}) async-start(bf16[8,112,128]{2,1,0:T(8,128)(2,1)} %pairs.1), calls=%async_computation.1 | async-start | bytes 458752 | tf_op jit(solution)/shard_map/all_to_all | solution.py:559
  58.8 16.4 %copy-start.5 = (bf16[1024,1024]{1,0:T(8,128)(2,1)S(1)}, bf16[1024,1024]{1,0:T(8,128)(2,1)}, u32[]{:S(2)}) copy-start(bf16[1024,1024]{1,0:T(8,128)(2,1)} %mix_ref.1) | copy-start | bytes 6291460
  66.9 8.4 %copy-start = (bf16[1024,1024]{1,0:T(8,128)(2,1)S(1)}, bf16[1024,1024]{1,0:T(8,128)(2,1)}, u32[]{:S(2)}) copy-start(bf16[1024,1024]{1,0:T(8,128)(2,1)} %get-tuple-element.51.normed0_ref.normed1_ref.normed_ref) | copy-start | bytes 6291460
  66.9 8.4 %copy-start.1 = (f32[1024,1]{1,0:T(8,128)S(1)}, f32[1024,1]{1,0:T(8,128)}, u32[]{:S(2)}) copy-start(f32[1024,1]{1,0:T(8,128)} %get-tuple-element.57.inv_ref) | copy-start | bytes 12292
  67.0 8.3 %copy-start.2 = (s32[4,1024]{1,0:T(4,128)S(1)}, s32[4,1024]{1,0:T(4,128)}, u32[]{:S(2)}) copy-start(s32[4,1024]{1,0:T(4,128)} %nb1_ref.5) | copy-start | bytes 49156
  67.0 2.9 %collective-permute-start.2 = (bf16[4,4,32,1152]{3,2,1,0:T(8,128)(2,1)S(1)}, bf16[4,4,32,1152]{3,2,1,0:T(8,128)(2,1)S(1)}, u32[]{:S(2)}, u32[]{:S(2)}) collective-permute-start(bf16[4,4,32,1152]{3,2,1,0:T(8,128)(2,1)S(1)} %get-tuple-element.54), channel_id=1, source_target_pairs={{0,1},{1,0},{2,3},{3,2},{4,5},{5,4},{6,7},{7,6},{8,9},{9,8},{10,11... | collective-permute-start | bytes 3538952 | tf_op jit(solution)/shard_map/ppermute | solution.py:523
  70.1 14.6 %collective-permute-start.3 = (bf16[4,32,1152]{2,1,0:T(8,128)(2,1)S(1)}, bf16[4,32,1152]{2,1,0:T(8,128)(2,1)S(1)}, u32[]{:S(2)}, u32[]{:S(2)}) collective-permute-start(bf16[4,32,1152]{2,1,0:T(8,128)(2,1)S(1)} %get-tuple-element.74), channel_id=1, source_target_pairs={{0,8},{1,9},{2,10},{3,11},{4,12},{5,13},{6,14},{7,15},{8,16},{9,17... | collective-permute-start | bytes 884744 | tf_op jit(solution)/shard_map/ppermute | solution.py:523
  71.7 13.1 %collective-permute-start.4 = (bf16[4,32,1152]{2,1,0:T(8,128)(2,1)S(1)}, bf16[4,32,1152]{2,1,0:T(8,128)(2,1)S(1)}, u32[]{:S(2)}, u32[]{:S(2)}) collective-permute-start(bf16[4,32,1152]{2,1,0:T(8,128)(2,1)S(1)} %get-tuple-element.73), channel_id=1, source_target_pairs={{0,16},{1,17},{2,18},{3,19},{4,20},{5,21},{6,22},{7,23},{8,24},{9,... | collective-permute-start | bytes 884744 | tf_op jit(solution)/shard_map/ppermute | solution.py:523
  72.8 15.1 %collective-permute-start.5 = (bf16[4,32,1152]{2,1,0:T(8,128)(2,1)S(1)}, bf16[4,32,1152]{2,1,0:T(8,128)(2,1)S(1)}, u32[]{:S(2)}, u32[]{:S(2)}) collective-permute-start(bf16[4,32,1152]{2,1,0:T(8,128)(2,1)S(1)} %get-tuple-element.72), channel_id=1, source_target_pairs={{0,24},{1,25},{2,26},{3,27},{4,28},{5,29},{6,30},{7,31},{8,0},{9,1... | collective-permute-start | bytes 884744 | tf_op jit(solution)/shard_map/ppermute | solution.py:523
  88.1 9.7 %collective-permute-start.8 = (bf16[32,1152]{1,0:T(8,128)(2,1)S(1)}, bf16[32,1152]{1,0:T(8,128)(2,1)S(1)}, u32[]{:S(2)}, u32[]{:S(2)}) collective-permute-start(bf16[32,1152]{1,0:T(8,128)(2,1)S(1)} %get-tuple-element.78), channel_id=1, source_target_pairs={{0,6},{1,7},{2,0},{3,1},{4,2},{5,3},{6,4},{7,5},{8,14},{9,15},{10,... | collective-permute-start | bytes 221192 | tf_op jit(solution)/shard_map/ppermute | solution.py:523
  91.4 7.7 %collective-permute-start.7 = (bf16[32,1152]{1,0:T(8,128)(2,1)S(1)}, bf16[32,1152]{1,0:T(8,128)(2,1)S(1)}, u32[]{:S(2)}, u32[]{:S(2)}) collective-permute-start(bf16[32,1152]{1,0:T(8,128)(2,1)S(1)} %get-tuple-element.79), channel_id=1, source_target_pairs={{0,4},{1,5},{2,6},{3,7},{4,0},{5,1},{6,2},{7,3},{8,12},{9,13},{10,... | collective-permute-start | bytes 221192 | tf_op jit(solution)/shard_map/ppermute | solution.py:523
  92.0 7.1 %collective-permute-start.6 = (bf16[32,1152]{1,0:T(8,128)(2,1)S(1)}, bf16[32,1152]{1,0:T(8,128)(2,1)S(1)}, u32[]{:S(2)}, u32[]{:S(2)}) collective-permute-start(bf16[32,1152]{1,0:T(8,128)(2,1)S(1)} %get-tuple-element.77), channel_id=1, source_target_pairs={{0,2},{1,3},{2,4},{3,5},{4,6},{5,7},{6,0},{7,1},{8,10},{9,11},{10,... | collective-permute-start | bytes 221192 | tf_op jit(solution)/shard_map/ppermute | solution.py:523
  93.7 9.3 %collective-permute-start.12 = (bf16[128,1024]{1,0:T(8,128)(2,1)S(1)}, bf16[128,1024]{1,0:T(8,128)(2,1)S(1)}, u32[]{:S(2)}, u32[]{:S(2)}) collective-permute-start(bf16[128,1024]{1,0:T(8,128)(2,1)S(1)} %get-tuple-element.63), channel_id=1, source_target_pairs={{0,1},{1,0},{2,3},{3,2},{4,5},{5,4},{6,7},{7,6},{8,9},{9,8},{10,11... | collective-permute-start | bytes 786440 | tf_op jit(solution)/shard_map/ppermute | solution.py:523
  93.7 11.3 %collective-permute-start.13 = (bf16[128,1024]{1,0:T(8,128)(2,1)S(1)}, bf16[128,1024]{1,0:T(8,128)(2,1)S(1)}, u32[]{:S(2)}, u32[]{:S(2)}) collective-permute-start(bf16[128,1024]{1,0:T(8,128)(2,1)S(1)} %get-tuple-element.64), channel_id=1, source_target_pairs={{1,2},{2,1},{3,4},{4,3},{5,6},{6,5},{7,8},{8,7},{9,10},{10,9},{11,... | collective-permute-start | bytes 786440 | tf_op jit(solution)/shard_map/ppermute | solution.py:523
  99.1 6.7 %collective-permute-start.9 = (bf16[32,1152]{1,0:T(8,128)(2,1)S(1)}, bf16[32,1152]{1,0:T(8,128)(2,1)S(1)}, u32[]{:S(2)}, u32[]{:S(2)}) collective-permute-start(bf16[32,1152]{1,0:T(8,128)(2,1)S(1)} %fusion.9), channel_id=1, source_target_pairs={{0,64},{32,96},{64,128},{96,160},{128,192},{160,224},{192,0},{224,... | collective-permute-start | bytes 221192 | tf_op jit(solution)/shard_map/ppermute | solution.py:523
  99.4 6.4 %collective-permute-start.10 = (bf16[32,1152]{1,0:T(8,128)(2,1)S(1)}, bf16[32,1152]{1,0:T(8,128)(2,1)S(1)}, u32[]{:S(2)}, u32[]{:S(2)}) collective-permute-start(bf16[32,1152]{1,0:T(8,128)(2,1)S(1)} %fusion.9), channel_id=1, source_target_pairs={{0,128},{32,160},{64,192},{96,224},{128,0},{160,32},{192,64},{224,... | collective-permute-start | bytes 221192 | tf_op jit(solution)/shard_map/ppermute | solution.py:523
  101.5 4.9 %collective-permute-start.11 = (bf16[32,1152]{1,0:T(8,128)(2,1)S(1)}, bf16[32,1152]{1,0:T(8,128)(2,1)S(1)}, u32[]{:S(2)}, u32[]{:S(2)}) collective-permute-start(bf16[32,1152]{1,0:T(8,128)(2,1)S(1)} %fusion.9), channel_id=1, source_target_pairs={{0,192},{32,224},{64,0},{96,32},{128,64},{160,96},{192,128},{224,1... | collective-permute-start | bytes 221192 | tf_op jit(solution)/shard_map/ppermute | solution.py:523
  106.4 8.6 %collective-permute-start.14 = (bf16[32,1152]{1,0:T(8,128)(2,1)S(1)}, bf16[32,1152]{1,0:T(8,128)(2,1)S(1)}, u32[]{:S(2)}, u32[]{:S(2)}) collective-permute-start(bf16[32,1152]{1,0:T(8,128)(2,1)S(1)} %add_convert_fusion.4.one_ref), channel_id=1, source_target_pairs={{0,32},{32,0},{64,96},{96,64},{128,160},{160,128},{192,224},{224,1... | collective-permute-start | bytes 221192 | tf_op jit(solution)/shard_map/ppermute | solution.py:523
  (1 other events, 8.3 us)
